TPU v7x, 256 devices: a whole 4x4x8 slice. The times are simulated.
256 devices in a mesh: sector: 32 (over y, z), inner: 8 (over x, core).
Axes of the slice: x: 4, y: 4, z: 8, core: 2. Of those that a mesh axis runs over, the one named last changes fastest.
Arguments:
- corner: bfloat16 [32, 64, 64], P('sector'), may hold values from -6 to 6
- edge_tensor: bfloat16 [2, 32, 256, 4096], P(None, 'sector', 'inner'), may hold values from -0.75 to 0.75
- site_tensor: bfloat16 [32, 256, 256], P('sector', None, 'inner'), may hold values from -0.375 to 0.375
- projector: bfloat16 [2, 32, 64, 16384], P(None, 'sector', None, 'inner'), may hold values from -0.046875 to 0.046875
- lengths: int32 [32], P('sector'), may hold values from 1 to 64, 1536 in all
- joining: int32 [2, 2048], replicated, may hold values from 0 to 2047, as said below
Outputs:
- corner_one: bfloat16 [32, 64, 64], P('sector')
- corner_two: bfloat16 [32, 64, 64], P('sector')
Inputs may be any that keep to these rules, and one draw needn't show every extreme that they name: joining[m] is a permutation of 0 to 2047; of each aligned block of 64 rows exactly 2 rows go into each aligned block of 64 new rows.
All inputs are finite; a program needn't handle non-finite values. No bound on the sum of `lengths` on one device may be relied on, other than what follows from the above.
Results may differ from a plain program's by a relative error of at most 0.01.
Values may be sent and summed in bfloat16 or wider, within the bound.
No kernel may reach another device: no remote copies, remote signals or barrier semaphores. Data moves between devices by JAX's collectives and lax.ppermute only.
A program may use at most 64 MiB of HBM per device.

v0:
```python
import jax
import jax.numpy as jnp
from jax import lax
from jax.sharding import PartitionSpec as P

MOVES = 2


def routing(joining_row, row_count, peers):
    per_peer = row_count // peers
    targets = (joining_row // row_count).reshape(peers, row_count)
    matches = (targets[:, :, None] == jnp.arange(peers, dtype=jnp.int32)[None, None, :]).astype(
        jnp.int32
    )
    earlier = jnp.cumsum(matches, axis=1) - matches
    ranking = jnp.sum(earlier * matches, axis=2)
    send_slot = targets * per_peer + ranking
    recv_slot = jnp.arange(peers, dtype=jnp.int32)[:, None] * per_peer + ranking
    return (send_slot, recv_slot)


def send_partial(outgoing):
    return lax.all_to_all(outgoing, "sector", split_axis=0, concat_axis=0, tiled=True)


def regroup(payload, joining_row, sector_index, sender):
    row_count = payload.shape[0]
    peers = lax.axis_size("sector")
    send_slot, recv_slot = routing(joining_row, row_count, peers)
    own_slots = lax.dynamic_slice_in_dim(send_slot, sector_index, 1, 0)[0]
    picked = (
        jnp.zeros((row_count,), jnp.int32).at[own_slots].set(jnp.arange(row_count, dtype=jnp.int32))
    )
    outgoing = jnp.take(payload, picked, axis=0).reshape(
        peers, row_count // peers, payload.shape[1]
    )
    incoming = sender(outgoing).reshape(row_count, payload.shape[1])
    anchor = (
        jnp.zeros((peers * row_count,), jnp.int32)
        .at[joining_row]
        .set(jnp.arange(peers * row_count, dtype=jnp.int32))
    )
    wanted = lax.dynamic_slice_in_dim(anchor, sector_index * row_count, row_count, 0)
    positions = jnp.take(recv_slot.reshape(-1), wanted)
    return jnp.take(incoming, positions, axis=0)


def body(corner, edge_tensor, site_tensor, projector, lengths, joining):
    sector_index = lax.axis_index("sector")
    inner_index = lax.axis_index("inner")
    local_sectors = corner.shape[0]
    width = corner.shape[1]
    inner_part = edge_tensor.shape[2]
    virtual = site_tensor.shape[1]
    block_rows = local_sectors * width
    alive_rows = jnp.arange(width, dtype=jnp.int32)[None, :] < lengths[:, None]
    sector_mask = alive_rows[:, :, None] & alive_rows[:, None, :]
    full_site = lax.all_gather(site_tensor, "inner", axis=2, tiled=True)
    site_rows = lax.dynamic_slice_in_dim(full_site, inner_index * inner_part, inner_part, 1)
    corner_in = corner
    results = []
    for move in range(MOVES):
        edges = edge_tensor[move]
        shaped = edges.reshape(local_sectors, inner_part, width, width)
        expanded = jnp.einsum(
            "sab,skbc->sakc", corner_in, shaped, preferred_element_type=jnp.float32
        ).astype(jnp.bfloat16)
        partial_value = jnp.einsum(
            "skq,sakb->saqb", site_rows, expanded, preferred_element_type=jnp.float32
        ).reshape(block_rows, virtual * width)
        moved = regroup(partial_value, joining[move], sector_index, send_partial)
        regrouped = lax.psum_scatter(moved, "inner", scatter_dimension=1, tiled=True).astype(
            jnp.bfloat16
        )
        shaped_rows = regrouped.reshape(local_sectors, width, inner_part, width)
        proj_view = projector[move].reshape(local_sectors, width, inner_part, width)
        term = jnp.einsum(
            "sakb,sgkb->sag", shaped_rows, proj_view, preferred_element_type=jnp.float32
        )
        total = lax.psum(term, "inner")
        corner_out = jnp.where(sector_mask, total, 0.0).astype(jnp.bfloat16)
        results.append(corner_out)
        corner_in = corner_out
    return (results[0], results[1])


def solution(mesh):
    placed = (
        P("sector", None, None),
        P(None, "sector", "inner", None),
        P("sector", None, "inner"),
        P(None, "sector", None, "inner"),
        P("sector"),
        P(),
    )
    return jax.shard_map(
        body,
        mesh=mesh,
        in_specs=placed,
        out_specs=(P("sector", None, None), P("sector", None, None)),
        check_vma=False,
    )
```

profile of v0, /device:TPU:1, one launch (start us, length us, event | category | flops | bytes accessed | tf_op | source)
XLA Modules:
  0.0 481.3 jit_solution(11594816371361037695)
XLA Ops:
  8.2 1.7 select_reduce_fusion
  10.1 1.7 select_reduce_fusion.1
  14.7 16.0 %all_gather.3 = bf16[1,256,256]{1,2,0:T(8,128)(2,1)S(1)} all-gather(bf16[1,256,32]{1,2,0:T(8,128)(2,1)} %param.12), channel_id=1, replica_groups=mesh['sector'=32,'inner'=8] {'inner'}, dimensions={2}, use_global_device_ids=true | all-gather | bytes 147456 | tf_op jit(solution)/shard_map/all_gather | solution.py:58
  31.0 2.8 convolution_bitcast_fusion.1
  33.8 6.9 %copy.57 = f32[1,64,256,64]{3,2,1,0:T(8,128)} copy(f32[1,64,256,64]{2,3,1,0:T(8,128)} %convolution_bitcast_fusion.1) | data formatting | bytes 8388608 | tf_op jit(solution)/shard_map/skq,sakb->saqb/transpose | solution.py:68
  40.7 6.9 %reshape.329 = f32[64,16384]{1,0:T(8,128)} reshape(f32[1,64,256,64]{3,2,1,0:T(8,128)} %copy.57) | data formatting | bytes 8388608 | tf_op jit(solution)/shard_map/reshape | solution.py:70
  47.6 7.6 %gather_fusion = f32[64,16384]{1,0:T(8,128)} fusion(f32[64,16384]{1,0:T(8,128)} %reshape.329, s32[1024]{0:T(1024)S(1)} %pad_clamp_fusion.4), kind=kCustom, calls=%fused_computation.clone | custom fusion | bytes 8388864 | tf_op jit(solution)/shard_map/jit(_take)/gather | solution.py:34
  55.2 4.5 broadcast_select_fusion.3
  59.6 5.8 %reshape.330 = f32[32,2,16384]{2,1,0:T(2,128)} reshape(f32[64,16384]{1,0:T(8,128)} %broadcast_select_fusion.3) | data formatting | bytes 8388608 | tf_op jit(solution)/shard_map/reshape | solution.py:34
  65.5 10.1 %all-to-all-start = ((f32[32,2,16384]{2,1,0:T(2,128)}), f32[32,2,16384]{2,1,0:T(2,128)}, u32[]{:S(2)}, u32[]{:S(2)}) async-start(f32[32,2,16384]{2,1,0:T(2,128)} %reshape.330), calls=%async_computation | async-start | bytes 8388608 | tf_op jit(solution)/shard_map/all_to_all | solution.py:23
  76.1 8.0 %scatter_custom_fusion.1 = s32[2048]{0:T(1024)S(1)} fusion(s32[2048]{0:T(1024)S(1)} %bitcast.61, s32[2048]{0:T(1024)S(1)} %iota.36, s32[]{:T(128)} %constant.61.clone.1), kind=kCustom, calls=%fused_computation.82 | custom fusion | bytes 8196 | tf_op jit(solution)/shard_map/scatter | solution.py:41
  85.2 84.7 %all-to-all-done = f32[32,2,16384]{2,1,0:T(2,128)} async-done(((f32[32,2,16384]{2,1,0:T(2,128)}), f32[32,2,16384]{2,1,0:T(2,128)}, u32[]{:S(2)}, u32[]{:S(2)}) %all-to-all-start) | async-done | bytes 4194336 | tf_op jit(solution)/shard_map/all_to_all | solution.py:23
  169.9 6.0 %reshape.331 = f32[64,16384]{1,0:T(8,128)} reshape(f32[32,2,16384]{2,1,0:T(2,128)} %all-to-all-done) | data formatting | bytes 8388608 | tf_op jit(solution)/shard_map/reshape | solution.py:37
  175.9 7.6 %gather_fusion.2 = f32[64,16384]{1,0:T(8,128)} fusion(f32[64,16384]{1,0:T(8,128)} %reshape.331, s32[1024]{0:T(1024)S(1)} %pad_clamp_fusion.3), kind=kCustom, calls=%fused_computation.2.clone | custom fusion | bytes 8388864 | tf_op jit(solution)/shard_map/jit(_take)/gather | solution.py:45
  183.5 4.5 broadcast_select_fusion.2
  191.6 32.7 %reduce-scatter.3.cloned.1.call-done = f32[64,2048]{1,0:T(8,128)} async-done(((f32[64,16384]{1,0:T(8,128)}), f32[64,2048]{1,0:T(8,128)}) %reduce-scatter.3.cloned.1.call-update) | async-done | bytes 524304 | tf_op jit(solution)/shard_map/reduce_scatter | solution.py:72
  224.3 1.1 convert_element_type.28
  226.3 24.2 %psum.14 = bf16[1,64,64]{2,1,0:T(8,128)(2,1)S(1)} all-reduce(f32[1,64,64]{2,1,0:T(8,128)S(1)} %convolution_bitcast_fusion.3), channel_id=1, replica_groups=mesh['sector'=32,'inner'=8] {'inner'}, use_global_device_ids=true, to_apply=%region_5.8 | all-reduce | flops 4096 | bytes 24576 | tf_op jit(solution)/shard_map/psum | solution.py:80
  250.8 2.8 convolution_bitcast_fusion
  253.6 6.9 %copy.66 = f32[1,64,256,64]{3,2,1,0:T(8,128)} copy(f32[1,64,256,64]{2,3,1,0:T(8,128)} %convolution_bitcast_fusion) | data formatting | bytes 8388608 | tf_op jit(solution)/shard_map/skq,sakb->saqb/transpose | solution.py:68
  260.5 6.9 %reshape.336 = f32[64,16384]{1,0:T(8,128)} reshape(f32[1,64,256,64]{3,2,1,0:T(8,128)} %copy.66) | data formatting | bytes 8388608 | tf_op jit(solution)/shard_map/reshape | solution.py:70
  267.4 7.6 %gather_fusion.3 = f32[64,16384]{1,0:T(8,128)} fusion(f32[64,16384]{1,0:T(8,128)} %reshape.336, s32[1024]{0:T(1024)S(1)} %pad_clamp_fusion.1), kind=kCustom, calls=%fused_computation.3.clone | custom fusion | bytes 8388864 | tf_op jit(solution)/shard_map/jit(_take)/gather | solution.py:34
  275.0 4.5 broadcast_select_fusion.1
  279.5 5.8 %reshape.337 = f32[32,2,16384]{2,1,0:T(2,128)} reshape(f32[64,16384]{1,0:T(8,128)} %broadcast_select_fusion.1) | data formatting | bytes 8388608 | tf_op jit(solution)/shard_map/reshape | solution.py:34
  285.3 9.7 %all-to-all-start.1 = ((f32[32,2,16384]{2,1,0:T(2,128)}), f32[32,2,16384]{2,1,0:T(2,128)}, u32[]{:S(2)}, u32[]{:S(2)}) async-start(f32[32,2,16384]{2,1,0:T(2,128)} %reshape.337), calls=%async_computation.2 | async-start | bytes 8388608 | tf_op jit(solution)/shard_map/all_to_all | solution.py:23
  295.1 8.3 %scatter_custom_fusion.3 = s32[2048]{0:T(1024)S(1)} fusion(s32[2048]{0:T(1024)S(1)} %bitcast.60, s32[2048]{0:T(1024)S(1)} %iota.38, s32[]{:T(128)} %constant.61.clone.1), kind=kCustom, calls=%fused_computation.80 | custom fusion | bytes 8196 | tf_op jit(solution)/shard_map/scatter | solution.py:41
  304.4 81.7 %all-to-all-done.1 = f32[32,2,16384]{2,1,0:T(2,128)} async-done(((f32[32,2,16384]{2,1,0:T(2,128)}), f32[32,2,16384]{2,1,0:T(2,128)}, u32[]{:S(2)}, u32[]{:S(2)}) %all-to-all-start.1) | async-done | bytes 4194336 | tf_op jit(solution)/shard_map/all_to_all | solution.py:23
  386.1 6.0 %reshape.338 = f32[64,16384]{1,0:T(8,128)} reshape(f32[32,2,16384]{2,1,0:T(2,128)} %all-to-all-done.1) | data formatting | bytes 8388608 | tf_op jit(solution)/shard_map/reshape | solution.py:37
  392.1 7.6 %gather_fusion.5 = f32[64,16384]{1,0:T(8,128)} fusion(f32[64,16384]{1,0:T(8,128)} %reshape.338, s32[1024]{0:T(1024)S(1)} %pad_clamp_fusion), kind=kCustom, calls=%fused_computation.4.clone | custom fusion | bytes 8388864 | tf_op jit(solution)/shard_map/jit(_take)/gather | solution.py:45
  399.7 4.5 broadcast_select_fusion
  404.8 42.9 %reduce-scatter.5.cloned.1.call-done = f32[64,2048]{1,0:T(8,128)} async-done(((f32[64,16384]{1,0:T(8,128)}), f32[64,2048]{1,0:T(8,128)}) %reduce-scatter.5.cloned.1.call-update) | async-done | bytes 524304 | tf_op jit(solution)/shard_map/reduce_scatter | solution.py:72
  449.6 24.1 %psum.15 = bf16[1,64,64]{2,1,0:T(8,128)(2,1)S(1)} all-reduce(f32[1,64,64]{2,1,0:T(8,128)S(1)} %convolution_bitcast_fusion.2), channel_id=1, replica_groups=mesh['sector'=32,'inner'=8] {'inner'}, use_global_device_ids=true, to_apply=%region_11.14 | all-reduce | flops 4096 | bytes 24576 | tf_op jit(solution)/shard_map/psum | solution.py:80
  (69 shorter events, 14.2 us)
Async XLA Ops:
  7.2 23.5 %copy-start = (bf16[1,64,64]{2,1,0:T(8,128)(2,1)S(1)}, bf16[1,64,64]{2,1,0:T(8,128)(2,1)}, u32[]{:S(2)}) copy-start(bf16[1,64,64]{2,1,0:T(8,128)(2,1)} %param.10) | copy-start | bytes 24580
  65.5 10.6 %copy-start.4 = (s32[2,2048]{1,0:T(2,128)S(1)}, s32[2,2048]{1,0:T(2,128)}, u32[]{:S(2)}) copy-start(s32[2,2048]{1,0:T(2,128)} %param.15) | copy-start | bytes 49156
  65.5 104.4 %all-to-all-start = ((f32[32,2,16384]{2,1,0:T(2,128)}), f32[32,2,16384]{2,1,0:T(2,128)}, u32[]{:S(2)}, u32[]{:S(2)}) async-start(f32[32,2,16384]{2,1,0:T(2,128)} %reshape.330), calls=%async_computation | async-start | bytes 8388608 | tf_op jit(solution)/shard_map/all_to_all | solution.py:23
  75.6 148.7 %reduce-scatter.3.cloned.1.call-start = ((), (), s32[]{:S(2)}) async-start(), calls=%async_computation.4 | async-start | bytes 4718592 | tf_op jit(solution)/shard_map/reduce_scatter | solution.py:72
  188.0 1.0 copy-start.2
  250.5 10.0 %copy-start.3 = (bf16[1,64,64]{2,1,0:T(8,128)(2,1)}, bf16[1,64,64]{2,1,0:T(8,128)(2,1)S(1)}, u32[]{:S(2)}) copy-start(bf16[1,64,64]{2,1,0:T(8,128)(2,1)S(1)} %fusion.20) | copy-start | bytes 24580
  285.3 100.8 %all-to-all-start.1 = ((f32[32,2,16384]{2,1,0:T(2,128)}), f32[32,2,16384]{2,1,0:T(2,128)}, u32[]{:S(2)}, u32[]{:S(2)}) async-start(f32[32,2,16384]{2,1,0:T(2,128)} %reshape.337), calls=%async_computation.2 | async-start | bytes 8388608 | tf_op jit(solution)/shard_map/all_to_all | solution.py:23
  295.0 152.6 %reduce-scatter.5.cloned.1.call-start = ((), (), s32[]{:S(2)}) async-start(), calls=%async_computation.5 | async-start | bytes 4718592 | tf_op jit(solution)/shard_map/reduce_scatter | solution.py:72
  399.7 74.7 %copy-start.1 = (bf16[1,64,64]{2,1,0:T(8,128)(2,1)S(1)}, bf16[1,64,64]{2,1,0:T(8,128)(2,1)}, u32[]{:S(2)}) copy-start(bf16[1,64,64]{2,1,0:T(8,128)(2,1)} %param.10) | copy-start | bytes 24580
Sparse Core Ops, SparseCore 0:
  188.1 36.1 reduce-scatter.2
  404.4 43.2 reduce-scatter.4
where the time goes:
time: 485 us; the launch traced here: 481 us
  waiting for transfers between devices  242 us (50%)
  local copies, waits for them, and re-layouts  108 us (22%)
  blocking collectives  64.4 us (13%)
  other arithmetic  25.1 us (5%)
  starting transfers between devices  20 us (4%)
  between operations  15 us (3%)
  matrix products  6.97 us (1%)
    all_to_all x2, waiting for transfers between devices, send_partial(): lax.all_to_all(outgoing, 'sector', split_axis=0, concat_axis=0, tiled=True)  166 us
    reduce_scatter x2, waiting for transfers between devices, body(): lax.psum_scatter(moved, 'inner', scatter_dimension=1, tiled=True)  75.5 us
    psum x2, blocking collectives, body(): total = lax.psum(term, 'inner')  48.3 us
    all_to_all x2, starting transfers between devices, send_partial(): lax.all_to_all(outgoing, 'sector', split_axis=0, concat_axis=0, tiled=True)  19.8 us
    scatter x2, local copies, waits for them, and re-layouts, regroup(): anchor = jnp.zeros((peers * row_count,), jnp.int32).at[joining_row].set(j...  16.4 us
    all_gather x1, blocking collectives, body(): full_site = lax.all_gather(site_tensor, 'inner', axis=2, tiled=True)  16 us
    gather x2, local copies, waits for them, and re-layouts, regroup(): jnp.take(payload, picked, axis=0)  15.2 us
    gather x2, local copies, waits for them, and re-layouts, regroup(): return jnp.take(incoming, positions, axis=0)  15.2 us
  transfers between devices with their start and end apart: 4, of which 4 were waited for; matrix products, arithmetic and copies ran while one was open for 4% of the time, Pallas kernels for 0%

commit v1 on v0

v1 whole, which is shorter than its diff:
```python
import functools

import jax
import jax.numpy as jnp
from jax import lax
from jax.experimental import pallas as pl
from jax.experimental.pallas import tpu as pltpu
from jax.sharding import PartitionSpec as P

BF = jnp.bfloat16
F32 = jnp.float32
INNER = 8
SECTORS = 32
W = 64
KQ = 256


def iota(shape, dim):
    return lax.broadcasted_iota(jnp.int32, shape, dim)


def dot(a, b):
    return lax.dot_general(a, b, (((1,), (0,)), ((), ())), preferred_element_type=F32)


def dot_nt(a, b):
    return lax.dot_general(a, b, (((1,), (1,)), ((), ())), preferred_element_type=F32)


def one_hot(cond):
    return jnp.where(cond, 1.0, 0.0).astype(BF)


def shuffle_matrix():
    row = iota((1024, 1), 0)
    want = (row % 16) * 64 + (row // 128) * 8 + (row // 16) % 8
    return one_hot(iota((1024, 1024), 1) == want)


def edge_blocks(edge, shuffle):
    stacked = jnp.concatenate([edge[:, n * 1024 : (n + 1) * 1024] for n in range(4)], axis=0)
    return dot_nt(stacked, shuffle).astype(BF)


def proj_blocks(proj, shuffle):
    stacked = jnp.concatenate([proj[:, n * 1024 : (n + 1) * 1024] for n in range(2)], axis=0)
    return dot_nt(shuffle, stacked).astype(BF)


def prep_first(edge_ref, site_ref, out_ref):
    shuffle = shuffle_matrix()
    blocks = edge_blocks(edge_ref[0, 0], shuffle)
    site_t = site_ref[0]
    for j in range(INNER):
        out_ref[j, 0:128, :] = blocks[:, j * 128 : (j + 1) * 128]
        out_ref[j, 128:160, :] = site_t[:, 0:128]
        out_ref[j, 160:192, :] = site_t[:, 128:256]


def prep_rest(edge_ref, proj_ref, out_ref):
    shuffle = shuffle_matrix()
    blocks = edge_blocks(edge_ref[0, 0], shuffle)
    for j in range(INNER):
        out_ref[j, 0:128, :] = blocks[:, j * 128 : (j + 1) * 128]
    for m in range(2):
        rows = proj_blocks(proj_ref[m, 0], shuffle)
        for j in range(INNER):
            out_ref[j, (m + 1) * 128 : (m + 2) * 128, :] = rows[j * 128 : (j + 1) * 128, :]


def own_row(joining_ref, move, sector):
    pair = joining_ref[move : move + 1, pl.ds(pl.multiple_of((sector // 2) * 128, 128), 128)]
    return jnp.where(sector % 2 == 0, pair[:, :W], pair[:, W:])


def send_slots(own):
    column = jnp.sum(
        jnp.where(iota((W, W), 0) == iota((W, W), 1), own, 0), axis=1, keepdims=True
    )
    before = ((column // W) == (own // W)) & (column < own)
    rank = jnp.sum(before.astype(jnp.int32), axis=0, keepdims=True)
    return (own // W) * 2 + rank


def expand(corner, slots, edges, site_t):
    pick = one_hot(slots == iota((512, W), 0) // 8)
    picked = dot(pick, corner).astype(BF)
    lane = iota((W, 512), 1)
    spread = one_hot((lane // 128) * 16 + lane % 16 == iota((W, 512), 0))
    wide_lane = iota((512, 512), 1)
    same = (wide_lane // 16) % 8 == iota((512, 512), 0) % 8
    kron = jnp.where(same, dot(picked, spread), 0.0).astype(BF)
    expanded = dot_nt(kron, edges).astype(BF)
    return dot_nt(expanded, site_t).astype(BF)


def gather_edges(ref, base):
    parts = []
    for n in range(4):
        parts.append(
            jnp.concatenate(
                [ref[i, base + n * 32 : base + (n + 1) * 32, :] for i in range(INNER)], axis=0
            )
        )
    return jnp.concatenate(parts, axis=1)


def gather_site(ref):
    halves = []
    for n in range(2):
        pieces = []
        for h in range(2):
            for i in range(INNER):
                start = 128 + n * 32 + h * 16
                pieces.append(ref[i, start : start + 16, :])
        halves.append(jnp.concatenate(pieces, axis=0))
    return jnp.concatenate(halves, axis=1)


def first_rows(corner_ref, first_ref, joining_ref, out_ref):
    sector = lax.axis_index("sector")
    slots = send_slots(own_row(joining_ref, 0, sector))
    rows = expand(corner_ref[0], slots, gather_edges(first_ref, 0), gather_site(first_ref))
    for t in range(SECTORS):
        out_ref[t] = rows[t * 16 : (t + 1) * 16, :]


def arrival_rows(joining_ref, move, sector):
    chunks = jnp.concatenate(
        [joining_ref[move : move + 1, n * 128 : (n + 1) * 128] for n in range(16)], axis=0
    )
    mine = (chunks // W) == sector
    place = chunks % W
    low = jnp.where(mine, place, W)
    high = jnp.where(mine, place, -1)
    even = iota((16, 128), 1) < W
    columns = [
        jnp.min(jnp.where(even, low, W), axis=1, keepdims=True),
        jnp.max(jnp.where(even, high, -1), axis=1, keepdims=True),
        jnp.min(jnp.where(even, W, low), axis=1, keepdims=True),
        jnp.max(jnp.where(even, -1, high), axis=1, keepdims=True),
    ]
    lane = iota((16, 512), 1)
    kind = (lane // 8) % 4
    value = jnp.where(
        kind == 0,
        columns[0],
        jnp.where(kind == 1, columns[1], jnp.where(kind == 2, columns[2], columns[3])),
    )
    return jnp.sum(jnp.where(lane // 32 == iota((16, 512), 0), value, 0), axis=0, keepdims=True)


def project(move, incoming_ref, rest_ref, joining_ref, out_ref):
    sector = lax.axis_index("sector")
    arrivals = arrival_rows(joining_ref, move, sector)
    row = iota((512, 512), 0)
    place = one_hot((row // W == iota((512, 512), 1) % 8) & (row % W == arrivals))
    incoming = jnp.concatenate([incoming_ref[s] for s in range(SECTORS)], axis=0)
    placed = dot(place, incoming).astype(BF)
    left = jnp.concatenate(
        [
            jnp.concatenate(
                [placed[b * W : (b + 1) * W, h * 128 : (h + 1) * 128] for b in range(8)], axis=1
            )
            for h in range(2)
        ],
        axis=0,
    )
    base = (move + 1) * 128
    right = jnp.concatenate(
        [
            rest_ref[i, base + b * 16 : base + (b + 1) * 16, :]
            for b in range(8)
            for i in range(INNER)
        ],
        axis=0,
    )
    both = dot(left, right)
    term = both[:W, :W] + both[W:, W:]
    packed = jnp.concatenate([term[:32], term[32:]], axis=1)
    for j in range(INNER):
        out_ref[j] = packed


def finished(terms_ref, lengths_ref):
    total = terms_ref[0]
    for j in range(1, INNER):
        total = total + terms_ref[j]
    total = jnp.concatenate([total[:, :W], total[:, W:]], axis=0)
    alive = lengths_ref[0]
    keep = (iota((W, W), 0) < alive) & (iota((W, W), 1) < alive)
    return jnp.where(keep, total, 0.0).astype(BF)


def second_rows(terms_ref, lengths_ref, first_ref, rest_ref, joining_ref, corner_ref, out_ref):
    sector = lax.axis_index("sector")
    corner = finished(terms_ref, lengths_ref)
    corner_ref[0] = corner
    slots = send_slots(own_row(joining_ref, 1, sector))
    rows = expand(corner, slots, gather_edges(rest_ref, 0), gather_site(first_ref))
    for t in range(SECTORS):
        out_ref[t] = rows[t * 16 : (t + 1) * 16, :]


def last(terms_ref, lengths_ref, corner_ref):
    corner_ref[0] = finished(terms_ref, lengths_ref)


def vmem():
    return pl.BlockSpec(memory_space=pltpu.VMEM)


def smem():
    return pl.BlockSpec(memory_space=pltpu.SMEM)


def call(kernel, outs, *args, specs=None, name=None, flops=0):
    return pl.pallas_call(
        kernel,
        out_shape=outs,
        in_specs=specs or [vmem()] * len(args),
        out_specs=jax.tree.map(lambda _: vmem(), outs),
        compiler_params=pltpu.CompilerParams(vmem_limit_bytes=48 * 2**20),
        name=name,
    )(*args)


def shape(dims, dtype):
    return jax.ShapeDtypeStruct(dims, dtype)


def swap(x, axis):
    return lax.all_to_all(x, axis, split_axis=0, concat_axis=0, tiled=True)


def one_move(index, array):
    dims = (1,) + array.shape[1:]
    return pl.BlockSpec(dims, lambda g: (index,) + (0,) * (len(dims) - 1))


def body(corner, edge_tensor, site_tensor, projector, lengths, joining):
    site_tensor = jnp.swapaxes(site_tensor, 1, 2)
    whole = lambda a: pl.BlockSpec(a.shape, lambda g: (0,) * a.ndim)
    params = pltpu.CompilerParams(vmem_limit_bytes=48 * 2**20)
    first = pl.pallas_call(
        prep_first,
        grid=(1,),
        out_shape=shape((INNER, 192, 128), BF),
        in_specs=[one_move(0, edge_tensor), whole(site_tensor)],
        out_specs=pl.BlockSpec((INNER, 192, 128), lambda g: (0, 0, 0)),
        compiler_params=params,
        name="prep_first",
    )(edge_tensor, site_tensor)
    first = swap(first, "inner")
    rest = pl.pallas_call(
        prep_rest,
        grid=(1,),
        out_shape=shape((INNER, 384, 128), BF),
        in_specs=[one_move(1, edge_tensor), whole(projector)],
        out_specs=pl.BlockSpec((INNER, 384, 128), lambda g: (0, 0, 0)),
        compiler_params=params,
        name="prep_rest",
    )(edge_tensor, projector)
    rest = swap(rest, "inner")
    rows_shape = shape((SECTORS, 16, KQ), BF)
    terms_shape = shape((INNER, 32, 128), F32)
    corner_shape = shape((1, W, W), BF)
    rows = call(first_rows, rows_shape, corner, first, joining, name="first_rows")
    rows = swap(rows, "sector")
    terms = call(
        functools.partial(project, 0), terms_shape, rows, rest, joining, name="project_first"
    )
    terms = swap(terms, "inner")
    one, rows = call(
        second_rows,
        (corner_shape, rows_shape),
        terms,
        lengths,
        first,
        rest,
        joining,
        specs=[vmem(), smem(), vmem(), vmem(), vmem()],
        name="second_rows",
    )
    rows = swap(rows, "sector")
    terms = call(
        functools.partial(project, 1), terms_shape, rows, rest, joining, name="project_second"
    )
    terms = swap(terms, "inner")
    two = call(last, corner_shape, terms, lengths, specs=[vmem(), smem()], name="last")
    return (one, two)


def solution(mesh):
    placed = (
        P("sector", None, None),
        P(None, "sector", "inner", None),
        P("sector", None, "inner"),
        P(None, "sector", None, "inner"),
        P("sector"),
        P(),
    )
    return jax.shard_map(
        body,
        mesh=mesh,
        in_specs=placed,
        out_specs=(P("sector", None, None), P("sector", None, None)),
        check_vma=False,
    )
```

time: 485 us -> 97 us (0.20)
  waiting for transfers between devices: 242 us -> 21.1 us
  local copies, waits for them, and re-layouts: 108 us -> 1.77 us
  other arithmetic: 25.1 us -> 0 us
  blocking collectives: 64.4 us -> 44.8 us
  between operations: 15 us -> 1.33 us
  Pallas kernels: 0 us -> 9.45 us
  matrix products: 6.97 us -> 0 us
    all_to_all x2 -> x3, waiting for transfers between devices: 166 us -> 21.1 us  [swap(): return lax.all_to_all(x, axis, split_axis=0, concat_axis=0, tiled=True)]
    reduce_scatter x2 -> x0, waiting for transfers between devices: 75.5 us -> none  [body(): lax.psum_scatter(moved, 'inner', scatter_dimension=1, tiled=True)]
    psum x2 -> x0, blocking collectives: 48.3 us -> none  [body(): total = lax.psum(term, 'inner')]
    all_to_all x0 -> x3, blocking collectives: none -> 44.8 us  [swap(): return lax.all_to_all(x, axis, split_axis=0, concat_axis=0, tiled=True)]
    reshape x6 -> x0, local copies, waits for them, and re-layouts: 37.5 us -> none  [the longest x2 13.8 us: body(): partial_value = jnp.einsum('skq,sakb->saqb', site_rows, expanded, preferr...]
    gather x6 -> x0, local copies, waits for them, and re-layouts: 31.9 us -> none  [the longest x2 15.2 us: regroup(): jnp.take(payload, picked, axis=0)]
    select_n x12 -> x0, other arithmetic: 18.1 us -> none  [the longest x2 8.92 us: regroup(): return jnp.take(incoming, positions, axis=0)]
    scatter x4 -> x0, local copies, waits for them, and re-layouts: 17.9 us -> none  [the longest x2 16.4 us: regroup(): anchor = jnp.zeros((peers * row_count,), jnp.int32).at[joining_row].set(j...]
  transfers between devices with their start and end apart: 4 -> 3, of which waited for: 4 -> 3; matrix products, arithmetic and copies ran while one was open for 4% -> 0% of each run, Pallas kernels for 0% -> 4%
where the time goes in v1:
time: 97 us; the launch traced here: 96.5 us
  blocking collectives  44.8 us (46%)
  waiting for transfers between devices  21.1 us (22%)
  starting transfers between devices  17.9 us (18%)
  Pallas kernels  9.45 us (10%)
  local copies, waits for them, and re-layouts  1.77 us (2%)
  between operations  1.33 us (1%)
    all_to_all x3, blocking collectives, swap(): return lax.all_to_all(x, axis, split_axis=0, concat_axis=0, tiled=True)  44.8 us
    all_to_all x3, waiting for transfers between devices, swap(): return lax.all_to_all(x, axis, split_axis=0, concat_axis=0, tiled=True)  21.1 us
    all_to_all x3, starting transfers between devices, swap(): return lax.all_to_all(x, axis, split_axis=0, concat_axis=0, tiled=True)  17.9 us
    pallas_call x5, Pallas kernels, call(): pl.pallas_call(kernel, out_shape=outs, in_specs=specs or [vmem()] * len(a...  4.91 us
    pallas_call x1, Pallas kernels, body(): pl.pallas_call(prep_rest, grid=(1,), out_shape=shape((INNER, 384, 128), B...  2.9 us
  transfers between devices with their start and end apart: 3, of which 3 were waited for; matrix products, arithmetic and copies ran while one was open for 0% of the time, Pallas kernels for 4%

profile of v1, /device:TPU:1, one launch (start us, length us, event | category | flops | bytes accessed | tf_op | source)
XLA Modules:
  0.0 96.5 jit_solution(7992992930637401636)
XLA Ops:
  0.6 0.0 copy-start
  0.6 1.0 %copy-done = bf16[2,1,32,4096]{3,2,1,0:T(8,128)(2,1)S(1)} copy-done((bf16[2,1,32,4096]{3,2,1,0:T(8,128)(2,1)S(1)}, bf16[2,1,32,4096]{3,2,1,0:T(8,128)(2,1)}, u32[]{:S(2)}) %copy-start) | copy-done | bytes 524312
  1.7 0.0 copy-start.4
  1.7 0.7 copy-done.4
  2.4 0.0 copy-start.2
  2.4 1.6 %prep_first.1 = bf16[8,192,128]{2,1,0:T(8,128)(2,1)} custom-call(bf16[2,1,32,4096]{3,2,1,0:T(8,128)(2,1)S(1)} %copy-done, bf16[1,32,256]{2,1,0:T(8,128)(2,1)S(1)} %bitcast.1), custom_call_target="tpu_custom_call" | custom-call | tf_op jit(solution)/shard_map/prep_first/pallas_call | solution.py:245
  4.0 0.0 copy-start.1
  4.0 6.7 %all-to-all-start = ((bf16[8,192,128]{2,1,0:T(8,128)(2,1)}), bf16[8,192,128]{2,1,0:T(8,128)(2,1)S(1)}, u32[]{:S(2)}, u32[]{:S(2)}) async-start(bf16[8,192,128]{2,1,0:T(8,128)(2,1)} %prep_first.1), calls=%async_computation | async-start | bytes 786432 | tf_op jit(solution)/shard_map/all_to_all | solution.py:233
  10.8 0.0 copy-done.2
  10.8 0.0 copy-done.1
  10.8 2.9 %prep_rest.1 = bf16[8,384,128]{2,1,0:T(8,128)(2,1)} custom-call(bf16[2,1,32,4096]{3,2,1,0:T(8,128)(2,1)S(1)} %copy-done.1, bf16[2,1,64,2048]{3,2,1,0:T(8,128)(2,1)S(1)} %copy-done.2), custom_call_target="tpu_custom_call" | custom-call | tf_op jit(solution)/shard_map/prep_rest/pallas_call | solution.py:255
  13.7 0.0 copy-start.3
  13.7 0.0 copy-start.5
  13.7 5.2 %all-to-all-done.first_ref = bf16[8,192,128]{2,1,0:T(8,128)(2,1)S(1)} async-done(((bf16[8,192,128]{2,1,0:T(8,128)(2,1)}), bf16[8,192,128]{2,1,0:T(8,128)(2,1)S(1)}, u32[]{:S(2)}, u32[]{:S(2)}) %all-to-all-start) | async-done | bytes 393248 | tf_op jit(solution)/shard_map/all_to_all | solution.py:233
  18.9 4.3 %all-to-all-start.2 = ((bf16[8,384,128]{2,1,0:T(8,128)(2,1)}), bf16[8,384,128]{2,1,0:T(8,128)(2,1)S(1)}, u32[]{:S(2)}, u32[]{:S(2)}) async-start(bf16[8,384,128]{2,1,0:T(8,128)(2,1)} %prep_rest.1), calls=%async_computation.2 | async-start | bytes 1572864 | tf_op jit(solution)/shard_map/all_to_all | solution.py:233
  23.2 0.0 copy-done.3
  23.2 0.0 copy-done.5
  23.2 1.0 %first_rows.1 = bf16[32,16,256]{2,1,0:T(8,128)(2,1)S(1)} custom-call(bf16[1,64,64]{2,1,0:T(8,128)(2,1)S(1)} %copy-done.5, bf16[8,192,128]{2,1,0:T(8,128)(2,1)S(1)} %all-to-all-done.first_ref, s32[2,2048]{1,0:T(2,128)S(1)} %copy-done.3), custom_call_target="tpu_custom_call" | custom-call | tf_op jit(solution)/shard_map/first_rows/pallas_call | solution.py:218
  24.2 11.3 %all-to-all-done.2.rest_ref = bf16[8,384,128]{2,1,0:T(8,128)(2,1)S(1)} async-done(((bf16[8,384,128]{2,1,0:T(8,128)(2,1)}), bf16[8,384,128]{2,1,0:T(8,128)(2,1)S(1)}, u32[]{:S(2)}, u32[]{:S(2)}) %all-to-all-start.2) | async-done | bytes 786464 | tf_op jit(solution)/shard_map/all_to_all | solution.py:233
  35.5 19.9 %all_to_all.30.incoming_ref = bf16[32,16,256]{2,1,0:T(8,128)(2,1)S(1)} all-to-all(bf16[32,16,256]{2,1,0:T(8,128)(2,1)S(1)} %first_rows.1), channel_id=1, replica_groups=mesh['sector'=32,'inner'=8] {'sector'}, dimensions={0} | all-to-all | bytes 524288 | tf_op jit(solution)/shard_map/all_to_all | solution.py:233
  55.4 1.5 %project_first.1 = f32[8,32,128]{2,1,0:T(8,128)} custom-call(bf16[32,16,256]{2,1,0:T(8,128)(2,1)S(1)} %all_to_all.30.incoming_ref, bf16[8,384,128]{2,1,0:T(8,128)(2,1)S(1)} %all-to-all-done.2.rest_ref, s32[2,2048]{1,0:T(2,128)S(1)} %copy-done.3), custom_call_target="tpu_custom_call" | custom-call | tf_op jit(solution)/shard_map/project_first/pallas_call | solution.py:218
  56.8 6.9 %all-to-all-start.3 = ((f32[8,32,128]{2,1,0:T(8,128)}), f32[8,32,128]{2,1,0:T(8,128)S(1)}, u32[]{:S(2)}, u32[]{:S(2)}) async-start(f32[8,32,128]{2,1,0:T(8,128)} %project_first.1), calls=%async_computation.3 | async-start | bytes 262144 | tf_op jit(solution)/shard_map/all_to_all | solution.py:233
  64.4 4.6 %all-to-all-done.3.terms_ref = f32[8,32,128]{2,1,0:T(8,128)S(1)} async-done(((f32[8,32,128]{2,1,0:T(8,128)}), f32[8,32,128]{2,1,0:T(8,128)S(1)}, u32[]{:S(2)}, u32[]{:S(2)}) %all-to-all-start.3) | async-done | bytes 131104 | tf_op jit(solution)/shard_map/all_to_all | solution.py:233
  69.0 1.0 second_rows.1
  70.0 13.7 %all_to_all.31.incoming_ref = bf16[32,16,256]{2,1,0:T(8,128)(2,1)S(1)} all-to-all(bf16[32,16,256]{2,1,0:T(8,128)(2,1)S(1)} %get-tuple-element.5), channel_id=1, replica_groups=mesh['sector'=32,'inner'=8] {'sector'}, dimensions={0} | all-to-all | bytes 524288 | tf_op jit(solution)/shard_map/all_to_all | solution.py:233
  83.7 0.8 project_second.1
  84.5 11.3 %all_to_all.32.terms_ref = f32[8,32,128]{2,1,0:T(8,128)S(1)} all-to-all(f32[8,32,128]{2,1,0:T(8,128)S(1)} %project_second.1), channel_id=1, replica_groups=mesh['sector'=32,'inner'=8] {'inner'}, dimensions={0} | all-to-all | bytes 262144 | tf_op jit(solution)/shard_map/all_to_all | solution.py:233
  95.8 0.7 last.1
Async XLA Ops:
  0.6 1.0 %copy-start = (bf16[2,1,32,4096]{3,2,1,0:T(8,128)(2,1)S(1)}, bf16[2,1,32,4096]{3,2,1,0:T(8,128)(2,1)}, u32[]{:S(2)}) copy-start(bf16[2,1,32,4096]{3,2,1,0:T(8,128)(2,1)} %edge_ref.3) | copy-start | bytes 1572868
  1.7 0.7 copy-start.4
  2.4 8.4 %copy-start.2 = (bf16[2,1,64,2048]{3,2,1,0:T(8,128)(2,1)S(1)}, bf16[2,1,64,2048]{3,2,1,0:T(8,128)(2,1)}, u32[]{:S(2)}) copy-start(bf16[2,1,64,2048]{3,2,1,0:T(8,128)(2,1)} %proj_ref.1) | copy-start | bytes 1572868
  4.0 6.7 %copy-start.1 = (bf16[2,1,32,4096]{3,2,1,0:T(8,128)(2,1)S(1)}, bf16[2,1,32,4096]{3,2,1,0:T(8,128)(2,1)}, u32[]{:S(2)}) copy-start(bf16[2,1,32,4096]{3,2,1,0:T(8,128)(2,1)} %edge_ref.3) | copy-start | bytes 1572868
  4.0 14.8 %all-to-all-start = ((bf16[8,192,128]{2,1,0:T(8,128)(2,1)}), bf16[8,192,128]{2,1,0:T(8,128)(2,1)S(1)}, u32[]{:S(2)}, u32[]{:S(2)}) async-start(bf16[8,192,128]{2,1,0:T(8,128)(2,1)} %prep_first.1), calls=%async_computation | async-start | bytes 786432 | tf_op jit(solution)/shard_map/all_to_all | solution.py:233
  13.7 9.5 %copy-start.3 = (s32[2,2048]{1,0:T(2,128)S(1)}, s32[2,2048]{1,0:T(2,128)}, u32[]{:S(2)}) copy-start(s32[2,2048]{1,0:T(2,128)} %joining_ref.7) | copy-start | bytes 49156
  13.7 9.5 %copy-start.5 = (bf16[1,64,64]{2,1,0:T(8,128)(2,1)S(1)}, bf16[1,64,64]{2,1,0:T(8,128)(2,1)}, u32[]{:S(2)}) copy-start(bf16[1,64,64]{2,1,0:T(8,128)(2,1)} %corner_ref.1) | copy-start | bytes 24580
  18.9 16.6 %all-to-all-start.2 = ((bf16[8,384,128]{2,1,0:T(8,128)(2,1)}), bf16[8,384,128]{2,1,0:T(8,128)(2,1)S(1)}, u32[]{:S(2)}, u32[]{:S(2)}) async-start(bf16[8,384,128]{2,1,0:T(8,128)(2,1)} %prep_rest.1), calls=%async_computation.2 | async-start | bytes 1572864 | tf_op jit(solution)/shard_map/all_to_all | solution.py:233
  56.8 12.2 %all-to-all-start.3 = ((f32[8,32,128]{2,1,0:T(8,128)}), f32[8,32,128]{2,1,0:T(8,128)S(1)}, u32[]{:S(2)}, u32[]{:S(2)}) async-start(f32[8,32,128]{2,1,0:T(8,128)} %project_first.1), calls=%async_computation.3 | async-start | bytes 262144 | tf_op jit(solution)/shard_map/all_to_all | solution.py:233

commit v2 on v1

--- a/solution.py
+++ b/solution.py
@@ -47,25 +47,49 @@
     return dot_nt(shuffle, stacked).astype(BF)
 
 
-def prep_first(edge_ref, site_ref, out_ref):
+def prep_first(edge_hbm, site_hbm, proj_hbm, out_ref, edge_ref, site_ref, proj_ref, sems):
+    copies = [
+        pltpu.make_async_copy(edge_hbm.at[0, 0], edge_ref, sems.at[0]),
+        pltpu.make_async_copy(site_hbm.at[0], site_ref, sems.at[1]),
+        pltpu.make_async_copy(proj_hbm.at[0, 0], proj_ref, sems.at[2]),
+    ]
+    for copy in copies:
+        copy.start()
     shuffle = shuffle_matrix()
-    blocks = edge_blocks(edge_ref[0, 0], shuffle)
-    site_t = site_ref[0]
+    for copy in copies:
+        copy.wait()
+    blocks = edge_blocks(edge_ref[...], shuffle)
+    rows = proj_blocks(proj_ref[...], shuffle)
+    site_t = site_ref[...]
     for j in range(INNER):
         out_ref[j, 0:128, :] = blocks[:, j * 128 : (j + 1) * 128]
         out_ref[j, 128:160, :] = site_t[:, 0:128]
         out_ref[j, 160:192, :] = site_t[:, 128:256]
-
-
-def prep_rest(edge_ref, proj_ref, out_ref):
-    shuffle = shuffle_matrix()
-    blocks = edge_blocks(edge_ref[0, 0], shuffle)
-    for j in range(INNER):
-        out_ref[j, 0:128, :] = blocks[:, j * 128 : (j + 1) * 128]
-    for m in range(2):
-        rows = proj_blocks(proj_ref[m, 0], shuffle)
-        for j in range(INNER):
-            out_ref[j, (m + 1) * 128 : (m + 2) * 128, :] = rows[j * 128 : (j + 1) * 128, :]
+        out_ref[j, 192:320, :] = rows[j * 128 : (j + 1) * 128, :]
+
+
+def own_shuffle():
+    row = iota((128, 1), 0)
+    want = (row % 16) * 64 + lax.axis_index("inner") * 8 + row // 16
+    return one_hot(iota((128, 1024), 1) == want)
+
+
+def pick_edge(edge_ref, out_ref):
+    shuffle = own_shuffle()
+    for n in range(4):
+        out_ref[:, n * 128 : (n + 1) * 128] = dot_nt(
+            edge_ref[:, n * 1024 : (n + 1) * 1024], shuffle
+        ).astype(BF)
+
+
+def pick_proj(proj_ref, out_ref):
+    shuffle = own_shuffle()
+    for i in range(INNER):
+        rows = proj_ref[i * W : (i + 1) * W, :]
+        stacked = jnp.concatenate([rows[:, :1024], rows[:, 1024:]], axis=0)
+        picked = dot_nt(shuffle, stacked).astype(BF)
+        for b in range(8):
+            out_ref[b * 128 + i * 16 : b * 128 + (i + 1) * 16, :] = picked[b * 16 : (b + 1) * 16, :]
 
 
 def own_row(joining_ref, move, sector):
@@ -117,12 +141,16 @@
     return jnp.concatenate(halves, axis=1)
 
 
-def first_rows(corner_ref, first_ref, joining_ref, out_ref):
+def first_rows(corner_ref, first_ref, joining_ref, lengths_hbm, out_ref, alive_ref, length, sem):
+    copy = pltpu.make_async_copy(lengths_hbm, length, sem)
+    copy.start()
     sector = lax.axis_index("sector")
     slots = send_slots(own_row(joining_ref, 0, sector))
     rows = expand(corner_ref[0], slots, gather_edges(first_ref, 0), gather_site(first_ref))
     for t in range(SECTORS):
         out_ref[t] = rows[t * 16 : (t + 1) * 16, :]
+    copy.wait()
+    alive_ref[...] = jnp.full((8, 128), length[0], jnp.int32)
 
 
 def arrival_rows(joining_ref, move, sector):
@@ -150,7 +178,13 @@
     return jnp.sum(jnp.where(lane // 32 == iota((16, 512), 0), value, 0), axis=0, keepdims=True)
 
 
-def project(move, incoming_ref, rest_ref, joining_ref, out_ref):
+def first_proj(ref):
+    return jnp.concatenate(
+        [ref[i, 192 + b * 16 : 192 + (b + 1) * 16, :] for b in range(8) for i in range(INNER)], axis=0
+    )
+
+
+def project(move, incoming_ref, proj_ref, joining_ref, out_ref):
     sector = lax.axis_index("sector")
     arrivals = arrival_rows(joining_ref, move, sector)
     row = iota((512, 512), 0)
@@ -166,61 +200,54 @@
         ],
         axis=0,
     )
-    base = (move + 1) * 128
-    right = jnp.concatenate(
-        [
-            rest_ref[i, base + b * 16 : base + (b + 1) * 16, :]
-            for b in range(8)
-            for i in range(INNER)
-        ],
-        axis=0,
-    )
+    right = first_proj(proj_ref) if move == 0 else proj_ref[...]
     both = dot(left, right)
     term = both[:W, :W] + both[W:, W:]
-    packed = jnp.concatenate([term[:32], term[32:]], axis=1)
+    packed = jnp.concatenate([term[:32], term[32:]], axis=1).astype(BF)
     for j in range(INNER):
         out_ref[j] = packed
 
 
-def finished(terms_ref, lengths_ref):
-    total = terms_ref[0]
+def finished(terms_ref, alive_ref):
+    total = terms_ref[0].astype(F32)
     for j in range(1, INNER):
-        total = total + terms_ref[j]
+        total = total + terms_ref[j].astype(F32)
     total = jnp.concatenate([total[:, :W], total[:, W:]], axis=0)
-    alive = lengths_ref[0]
+    alive = alive_ref[0:1, 0:W]
     keep = (iota((W, W), 0) < alive) & (iota((W, W), 1) < alive)
     return jnp.where(keep, total, 0.0).astype(BF)
 
 
-def second_rows(terms_ref, lengths_ref, first_ref, rest_ref, joining_ref, corner_ref, out_ref):
+def second_rows(terms_ref, alive_ref, first_ref, edge_ref, joining_ref, corner_ref, out_ref):
     sector = lax.axis_index("sector")
-    corner = finished(terms_ref, lengths_ref)
+    corner = finished(terms_ref, alive_ref)
     corner_ref[0] = corner
     slots = send_slots(own_row(joining_ref, 1, sector))
-    rows = expand(corner, slots, gather_edges(rest_ref, 0), gather_site(first_ref))
+    rows = expand(corner, slots, edge_ref[...], gather_site(first_ref))
     for t in range(SECTORS):
         out_ref[t] = rows[t * 16 : (t + 1) * 16, :]
 
 
-def last(terms_ref, lengths_ref, corner_ref):
-    corner_ref[0] = finished(terms_ref, lengths_ref)
+def last(terms_ref, alive_ref, corner_ref):
+    corner_ref[0] = finished(terms_ref, alive_ref)
 
 
 def vmem():
     return pl.BlockSpec(memory_space=pltpu.VMEM)
 
 
-def smem():
-    return pl.BlockSpec(memory_space=pltpu.SMEM)
-
-
-def call(kernel, outs, *args, specs=None, name=None, flops=0):
+def hbm():
+    return pl.BlockSpec(memory_space=pltpu.HBM)
+
+
+def call(kernel, outs, *args, specs=None, scratch=(), room=32, name=None):
     return pl.pallas_call(
         kernel,
         out_shape=outs,
         in_specs=specs or [vmem()] * len(args),
         out_specs=jax.tree.map(lambda _: vmem(), outs),
-        compiler_params=pltpu.CompilerParams(vmem_limit_bytes=48 * 2**20),
+        scratch_shapes=scratch,
+        compiler_params=pltpu.CompilerParams(vmem_limit_bytes=room * 2**20),
         name=name,
     )(*args)
 
@@ -233,61 +260,63 @@
     return lax.all_to_all(x, axis, split_axis=0, concat_axis=0, tiled=True)
 
 
-def one_move(index, array):
-    dims = (1,) + array.shape[1:]
-    return pl.BlockSpec(dims, lambda g: (index,) + (0,) * (len(dims) - 1))
-
-
 def body(corner, edge_tensor, site_tensor, projector, lengths, joining):
-    site_tensor = jnp.swapaxes(site_tensor, 1, 2)
-    whole = lambda a: pl.BlockSpec(a.shape, lambda g: (0,) * a.ndim)
-    params = pltpu.CompilerParams(vmem_limit_bytes=48 * 2**20)
-    first = pl.pallas_call(
+    edge_all = lax.all_gather(edge_tensor[1, 0], "inner", axis=0, tiled=True)
+    proj_all = lax.all_gather(projector[1, 0], "inner", axis=0, tiled=True)
+    first = call(
         prep_first,
-        grid=(1,),
-        out_shape=shape((INNER, 192, 128), BF),
-        in_specs=[one_move(0, edge_tensor), whole(site_tensor)],
-        out_specs=pl.BlockSpec((INNER, 192, 128), lambda g: (0, 0, 0)),
-        compiler_params=params,
+        shape((INNER, 320, 128), BF),
+        edge_tensor,
+        jnp.swapaxes(site_tensor, 1, 2),
+        projector,
+        specs=[hbm(), hbm(), hbm()],
+        scratch=[
+            pltpu.VMEM((32, 4096), BF),
+            pltpu.VMEM((32, KQ), BF),
+            pltpu.VMEM((W, 2048), BF),
+            pltpu.SemaphoreType.DMA((3,)),
+        ],
+        room=60,
         name="prep_first",
-    )(edge_tensor, site_tensor)
+    )
     first = swap(first, "inner")
-    rest = pl.pallas_call(
-        prep_rest,
-        grid=(1,),
-        out_shape=shape((INNER, 384, 128), BF),
-        in_specs=[one_move(1, edge_tensor), whole(projector)],
-        out_specs=pl.BlockSpec((INNER, 384, 128), lambda g: (0, 0, 0)),
-        compiler_params=params,
-        name="prep_rest",
-    )(edge_tensor, projector)
-    rest = swap(rest, "inner")
     rows_shape = shape((SECTORS, 16, KQ), BF)
-    terms_shape = shape((INNER, 32, 128), F32)
+    terms_shape = shape((INNER, 32, 128), BF)
     corner_shape = shape((1, W, W), BF)
-    rows = call(first_rows, rows_shape, corner, first, joining, name="first_rows")
+    rows, alive = call(
+        first_rows,
+        (rows_shape, shape((8, 128), jnp.int32)),
+        corner,
+        first,
+        joining,
+        lengths,
+        specs=[vmem(), vmem(), vmem(), hbm()],
+        scratch=[pltpu.SMEM((1,), jnp.int32), pltpu.SemaphoreType.DMA],
+        name="first_rows",
+    )
     rows = swap(rows, "sector")
     terms = call(
-        functools.partial(project, 0), terms_shape, rows, rest, joining, name="project_first"
+        functools.partial(project, 0), terms_shape, rows, first, joining, name="project_first"
     )
     terms = swap(terms, "inner")
+    edges = call(pick_edge, shape((KQ, 512), BF), edge_all, name="pick_edge")
+    projs = call(pick_proj, shape((1024, 128), BF), proj_all, name="pick_proj")
     one, rows = call(
         second_rows,
         (corner_shape, rows_shape),
         terms,
-        lengths,
+        alive,
         first,
-        rest,
+        edges,
         joining,
-        specs=[vmem(), smem(), vmem(), vmem(), vmem()],
         name="second_rows",
     )
     rows = swap(rows, "sector")
     terms = call(
-        functools.partial(project, 1), terms_shape, rows, rest, joining, name="project_second"
+        functools.partial(project, 1), terms_shape, rows, projs, joining, name="project_second"
     )
     terms = swap(terms, "inner")
-    two = call(last, corner_shape, terms, lengths, specs=[vmem(), smem()], name="last")
+    two = call(last, corner_shape, terms, alive, name="last")
     return (one, two)
 
 

time: 97 us -> 104 us (1.072)
  blocking collectives: 44.8 us -> 31.3 us
  between operations: 1.33 us -> 14.7 us
  local copies, waits for them, and re-layouts: 1.77 us -> 6.55 us
  Pallas kernels: 9.45 us -> 10.7 us
    all_to_all x3 -> x2, blocking collectives: 44.8 us -> 31.3 us  [swap(): return lax.all_to_all(x, axis, split_axis=0, concat_axis=0, tiled=True)]
    pallas_call x5 -> x8, Pallas kernels: 4.91 us -> 10.7 us  [call(): pl.pallas_call(kernel, out_shape=outs, in_specs=specs or [vmem()] * len(a...]
    pallas_call x2 -> x0, Pallas kernels: 4.54 us -> none  [the longest x1 2.9 us: body(): pl.pallas_call(prep_rest, grid=(1,), out_shape=shape((INNER, 384, 128), B...]
    slice x0 -> x2, local copies, waits for them, and re-layouts: none -> 3.35 us  [the longest x1 1.69 us: body(): edge_all = lax.all_gather(edge_tensor[1, 0], 'inner', axis=0, tiled=True)]
    unnamed x12 -> x8, local copies, waits for them, and re-layouts: 1.77 us -> 3.2 us
  transfers between devices with their start and end apart: 3 -> 5, of which waited for: 3 -> 3; matrix products, arithmetic and copies ran while one was open for 0% -> 2% of each run, Pallas kernels for 4% -> 9%
where the time goes in v2:
time: 104 us; the launch traced here: 103 us
  blocking collectives  31.3 us (30%)
  waiting for transfers between devices  21.7 us (21%)
  starting transfers between devices  18.2 us (18%)
  between operations  14.7 us (14%)
  Pallas kernels  10.7 us (10%)
  local copies, waits for them, and re-layouts  6.55 us (6%)
    all_to_all x2, blocking collectives, swap(): return lax.all_to_all(x, axis, split_axis=0, concat_axis=0, tiled=True)  31.3 us
    all_to_all x3, waiting for transfers between devices, swap(): return lax.all_to_all(x, axis, split_axis=0, concat_axis=0, tiled=True)  21.7 us
    all_to_all x3, starting transfers between devices, swap(): return lax.all_to_all(x, axis, split_axis=0, concat_axis=0, tiled=True)  18.1 us
    pallas_call x8, Pallas kernels, call(): pl.pallas_call(kernel, out_shape=outs, in_specs=specs or [vmem()] * len(a...  10.7 us
    unnamed x8, local copies, waits for them, and re-layouts  3.2 us
  transfers between devices with their start and end apart: 5, of which 3 were waited for; matrix products, arithmetic and copies ran while one was open for 2% of the time, Pallas kernels for 9%

profile of v2, /device:TPU:1, one launch (start us, length us, event | category | flops | bytes accessed | tf_op | source)
XLA Modules:
  0.0 103.3 jit_solution(16712033074422905612)
XLA Ops:
  7.2 0.0 all-gather.5.cloned.1.call-start
  7.2 1.7 %slice.6 = bf16[1,1,32,4096]{3,2,1,0:T(8,128)(2,1)} slice(bf16[2,1,32,4096]{3,2,1,0:T(8,128)(2,1)} %edge_hbm.1), slice={[1:2], [0:1], [0:32], [0:4096]} | slice | bytes 524288 | tf_op jit(solution)/shard_map/slice | solution.py:264
  8.9 0.0 copy-start.2
  8.9 0.0 copy-start.3
  8.9 0.0 all-gather.5.cloned.1.call-update
  8.9 0.0 all-gather.7.cloned.1.call-start
  9.0 1.7 %slice.7 = bf16[1,1,64,2048]{3,2,1,0:T(8,128)(2,1)} slice(bf16[2,1,64,2048]{3,2,1,0:T(8,128)(2,1)} %proj_hbm.1), slice={[1:2], [0:1], [0:64], [0:2048]} | slice | bytes 524288 | tf_op jit(solution)/shard_map/slice | solution.py:265
  10.6 0.0 all-gather.7.cloned.1.call-update
  10.7 3.3 %prep_first.1 = bf16[8,320,128]{2,1,0:T(8,128)(2,1)} custom-call(bf16[2,1,32,4096]{3,2,1,0:T(8,128)(2,1)} %edge_hbm.1, bf16[1,32,256]{2,1,0:T(8,128)(2,1)} %bitcast.5, bf16[2,1,64,2048]{3,2,1,0:T(8,128)(2,1)} %proj_hbm.1), custom_call_target="tpu_custom_call" | custom-call | tf_op jit(solution)/shard_map/prep_first/pallas_call | solution.py:244
  13.9 6.7 %all-to-all-start = ((bf16[8,320,128]{2,1,0:T(8,128)(2,1)}), bf16[8,320,128]{2,1,0:T(8,128)(2,1)S(1)}, u32[]{:S(2)}, u32[]{:S(2)}) async-start(bf16[8,320,128]{2,1,0:T(8,128)(2,1)} %prep_first.1), calls=%async_computation | async-start | bytes 1310720 | tf_op jit(solution)/shard_map/all_to_all | solution.py:260
  21.3 11.5 %all-to-all-done.first_ref.proj_ref = bf16[8,320,128]{2,1,0:T(8,128)(2,1)S(1)} async-done(((bf16[8,320,128]{2,1,0:T(8,128)(2,1)}), bf16[8,320,128]{2,1,0:T(8,128)(2,1)S(1)}, u32[]{:S(2)}, u32[]{:S(2)}) %all-to-all-start) | async-done | bytes 655392 | tf_op jit(solution)/shard_map/all_to_all | solution.py:260
  32.7 0.0 copy-done.2
  32.7 0.0 copy-done.3
  32.7 1.4 %first_rows.1 = (bf16[32,16,256]{2,1,0:T(8,128)(2,1)S(1)}, s32[8,128]{1,0:T(8,128)S(1)}) custom-call(bf16[1,64,64]{2,1,0:T(8,128)(2,1)S(1)} %copy-done.3, bf16[8,320,128]{2,1,0:T(8,128)(2,1)S(1)} %all-to-all-done.first_ref.proj_ref, s32[2,2048]{1,0:T(2,128)S(1)} %copy-done.2, s32[1]{0:T(128)S(6)} %copy.8.lengths_hbm), custom_call_target="tpu_custom_call" | custom-call | tf_op jit(solution)/shard_map/first_rows/pallas_call | solution.py:244
  34.2 20.5 %all_to_all.25.incoming_ref = bf16[32,16,256]{2,1,0:T(8,128)(2,1)S(1)} all-to-all(bf16[32,16,256]{2,1,0:T(8,128)(2,1)S(1)} %get-tuple-element.6), channel_id=1, replica_groups=mesh['sector'=32,'inner'=8] {'sector'}, dimensions={0} | all-to-all | bytes 524288 | tf_op jit(solution)/shard_map/all_to_all | solution.py:260
  54.7 1.4 %project_first.1 = bf16[8,32,128]{2,1,0:T(8,128)(2,1)} custom-call(bf16[32,16,256]{2,1,0:T(8,128)(2,1)S(1)} %all_to_all.25.incoming_ref, bf16[8,320,128]{2,1,0:T(8,128)(2,1)S(1)} %all-to-all-done.first_ref.proj_ref, s32[2,2048]{1,0:T(2,128)S(1)} %copy-done.2), custom_call_target="tpu_custom_call" | custom-call | tf_op jit(solution)/shard_map/project_first/pallas_call | solution.py:244
  56.1 6.9 %all-to-all-start.2 = ((bf16[8,32,128]{2,1,0:T(8,128)(2,1)}), bf16[8,32,128]{2,1,0:T(8,128)(2,1)S(1)}, u32[]{:S(2)}, u32[]{:S(2)}) async-start(bf16[8,32,128]{2,1,0:T(8,128)(2,1)} %project_first.1), calls=%async_computation.2 | async-start | bytes 131072 | tf_op jit(solution)/shard_map/all_to_all | solution.py:260
  63.1 0.0 all-gather.5.cloned.1.call-done
  63.1 0.0 copy-start.1
  63.1 1.6 %copy-done.1 = bf16[1,1,256,4096]{3,2,1,0:T(8,128)(2,1)S(1)} copy-done((bf16[1,1,256,4096]{3,2,1,0:T(8,128)(2,1)S(1)}, bf16[1,1,256,4096]{3,2,1,0:T(8,128)(2,1)}, u32[]{:S(2)}) %copy-start.1) | copy-done | bytes 2097176
  64.7 0.7 pick_edge.1.edge_ref
  65.4 2.9 %all-to-all-done.2.terms_ref = bf16[8,32,128]{2,1,0:T(8,128)(2,1)S(1)} async-done(((bf16[8,32,128]{2,1,0:T(8,128)(2,1)}), bf16[8,32,128]{2,1,0:T(8,128)(2,1)S(1)}, u32[]{:S(2)}, u32[]{:S(2)}) %all-to-all-start.2) | async-done | bytes 65568 | tf_op jit(solution)/shard_map/all_to_all | solution.py:260
  68.3 1.7 %second_rows.1 = (bf16[1,64,64]{2,1,0:T(8,128)(2,1)}, bf16[32,16,256]{2,1,0:T(8,128)(2,1)}) custom-call(bf16[8,32,128]{2,1,0:T(8,128)(2,1)S(1)} %all-to-all-done.2.terms_ref, s32[8,128]{1,0:T(8,128)S(1)} %get-tuple-element.7.alive_ref, bf16[8,320,128]{2,1,0:T(8,128)(2,1)S(1)} %all-to-all-done.first_ref.proj_ref, bf16[256,512]{1,0:T(8,128)(2,1)S(1)} %pick_edge.1.edge_ref, ...), custom_call_target="tpu_custom_call" | custom-call | tf_op jit(solution)/shard_map/second_rows/pallas_call | solution.py:244
  70.0 4.5 %all-to-all-start.3 = ((bf16[32,16,256]{2,1,0:T(8,128)(2,1)}), bf16[32,16,256]{2,1,0:T(8,128)(2,1)S(1)}, u32[]{:S(2)}, u32[]{:S(2)}) async-start(bf16[32,16,256]{2,1,0:T(8,128)(2,1)} %get-tuple-element.9), calls=%async_computation.3 | async-start | bytes 524288 | tf_op jit(solution)/shard_map/all_to_all | solution.py:260
  74.4 0.0 all-gather.7.cloned.1.call-done
  74.5 0.0 copy-start
  74.5 1.6 %copy-done = bf16[1,1,512,2048]{3,2,1,0:T(8,128)(2,1)S(1)} copy-done((bf16[1,1,512,2048]{3,2,1,0:T(8,128)(2,1)S(1)}, bf16[1,1,512,2048]{3,2,1,0:T(8,128)(2,1)}, u32[]{:S(2)}) %copy-start) | copy-done | bytes 2097176
  76.0 0.7 pick_proj.1.proj_ref
  76.8 7.3 %all-to-all-done.3.incoming_ref = bf16[32,16,256]{2,1,0:T(8,128)(2,1)S(1)} async-done(((bf16[32,16,256]{2,1,0:T(8,128)(2,1)}), bf16[32,16,256]{2,1,0:T(8,128)(2,1)S(1)}, u32[]{:S(2)}, u32[]{:S(2)}) %all-to-all-start.3) | async-done | bytes 262176 | tf_op jit(solution)/shard_map/all_to_all | solution.py:260
  84.1 0.8 project_second.1
  84.9 10.8 %all_to_all.26.terms_ref = bf16[8,32,128]{2,1,0:T(8,128)(2,1)S(1)} all-to-all(bf16[8,32,128]{2,1,0:T(8,128)(2,1)S(1)} %project_second.1), channel_id=1, replica_groups=mesh['sector'=32,'inner'=8] {'inner'}, dimensions={0} | all-to-all | bytes 131072 | tf_op jit(solution)/shard_map/all_to_all | solution.py:260
  95.7 0.7 last.1
Async XLA Ops:
  7.2 55.9 %all-gather.5.cloned.1.call-start = ((), (), s32[]{:S(2)}) async-start(), calls=%async_computation.5 | async-start | bytes 2359296 | tf_op jit(solution)/shard_map/all_gather | solution.py:264
  8.9 23.8 %copy-start.2 = (s32[2,2048]{1,0:T(2,128)S(1)}, s32[2,2048]{1,0:T(2,128)}, u32[]{:S(2)}) copy-start(s32[2,2048]{1,0:T(2,128)} %joining_ref.7) | copy-start | bytes 49156
  8.9 23.8 %copy-start.3 = (bf16[1,64,64]{2,1,0:T(8,128)(2,1)S(1)}, bf16[1,64,64]{2,1,0:T(8,128)(2,1)}, u32[]{:S(2)}) copy-start(bf16[1,64,64]{2,1,0:T(8,128)(2,1)} %corner_ref.1) | copy-start | bytes 24580
  8.9 65.5 %all-gather.7.cloned.1.call-start = ((), (), s32[]{:S(2)}) async-start(), calls=%async_computation.6 | async-start | bytes 2359296 | tf_op jit(solution)/shard_map/all_gather | solution.py:265
  13.9 18.8 %all-to-all-start = ((bf16[8,320,128]{2,1,0:T(8,128)(2,1)}), bf16[8,320,128]{2,1,0:T(8,128)(2,1)S(1)}, u32[]{:S(2)}, u32[]{:S(2)}) async-start(bf16[8,320,128]{2,1,0:T(8,128)(2,1)} %prep_first.1), calls=%async_computation | async-start | bytes 1310720 | tf_op jit(solution)/shard_map/all_to_all | solution.py:260
  56.1 12.1 %all-to-all-start.2 = ((bf16[8,32,128]{2,1,0:T(8,128)(2,1)}), bf16[8,32,128]{2,1,0:T(8,128)(2,1)S(1)}, u32[]{:S(2)}, u32[]{:S(2)}) async-start(bf16[8,32,128]{2,1,0:T(8,128)(2,1)} %project_first.1), calls=%async_computation.2 | async-start | bytes 131072 | tf_op jit(solution)/shard_map/all_to_all | solution.py:260
  63.1 1.6 %copy-start.1 = (bf16[1,1,256,4096]{3,2,1,0:T(8,128)(2,1)S(1)}, bf16[1,1,256,4096]{3,2,1,0:T(8,128)(2,1)}, u32[]{:S(2)}) copy-start(bf16[1,1,256,4096]{3,2,1,0:T(8,128)(2,1)} %all-gather.5.cloned.1.call-done) | copy-start | bytes 6291460
  70.0 14.1 %all-to-all-start.3 = ((bf16[32,16,256]{2,1,0:T(8,128)(2,1)}), bf16[32,16,256]{2,1,0:T(8,128)(2,1)S(1)}, u32[]{:S(2)}, u32[]{:S(2)}) async-start(bf16[32,16,256]{2,1,0:T(8,128)(2,1)} %get-tuple-element.9), calls=%async_computation.3 | async-start | bytes 524288 | tf_op jit(solution)/shard_map/all_to_all | solution.py:260
  74.5 1.6 %copy-start = (bf16[1,1,512,2048]{3,2,1,0:T(8,128)(2,1)S(1)}, bf16[1,1,512,2048]{3,2,1,0:T(8,128)(2,1)}, u32[]{:S(2)}) copy-start(bf16[1,1,512,2048]{3,2,1,0:T(8,128)(2,1)} %all-gather.7.cloned.1.call-done) | copy-start | bytes 6291460
Sparse Core Ops, SparseCore 0:
  9.9 33.9 all-gather.4
  45.7 28.4 all-gather.6

commit v3 on v2

--- a/solution.py
+++ b/solution.py
@@ -68,28 +68,13 @@
         out_ref[j, 192:320, :] = rows[j * 128 : (j + 1) * 128, :]
 
 
-def own_shuffle():
-    row = iota((128, 1), 0)
-    want = (row % 16) * 64 + lax.axis_index("inner") * 8 + row // 16
-    return one_hot(iota((128, 1024), 1) == want)
-
-
-def pick_edge(edge_ref, out_ref):
-    shuffle = own_shuffle()
-    for n in range(4):
-        out_ref[:, n * 128 : (n + 1) * 128] = dot_nt(
-            edge_ref[:, n * 1024 : (n + 1) * 1024], shuffle
-        ).astype(BF)
-
-
-def pick_proj(proj_ref, out_ref):
-    shuffle = own_shuffle()
-    for i in range(INNER):
-        rows = proj_ref[i * W : (i + 1) * W, :]
-        stacked = jnp.concatenate([rows[:, :1024], rows[:, 1024:]], axis=0)
-        picked = dot_nt(shuffle, stacked).astype(BF)
-        for b in range(8):
-            out_ref[b * 128 + i * 16 : b * 128 + (i + 1) * 16, :] = picked[b * 16 : (b + 1) * 16, :]
+def prep_rest(edge_ref, proj_ref, out_ref):
+    shuffle = shuffle_matrix()
+    blocks = edge_blocks(edge_ref[0, 0], shuffle)
+    rows = proj_blocks(proj_ref[0, 0], shuffle)
+    for j in range(INNER):
+        out_ref[j, 0:128, :] = blocks[:, j * 128 : (j + 1) * 128]
+        out_ref[j, 128:256, :] = rows[j * 128 : (j + 1) * 128, :]
 
 
 def own_row(joining_ref, move, sector):
@@ -141,16 +126,13 @@
     return jnp.concatenate(halves, axis=1)
 
 
-def first_rows(corner_ref, first_ref, joining_ref, lengths_hbm, out_ref, alive_ref, length, sem):
-    copy = pltpu.make_async_copy(lengths_hbm, length, sem)
-    copy.start()
+def first_rows(corner_ref, first_ref, joining_ref, lengths_ref, out_ref, alive_ref):
     sector = lax.axis_index("sector")
     slots = send_slots(own_row(joining_ref, 0, sector))
     rows = expand(corner_ref[0], slots, gather_edges(first_ref, 0), gather_site(first_ref))
     for t in range(SECTORS):
         out_ref[t] = rows[t * 16 : (t + 1) * 16, :]
-    copy.wait()
-    alive_ref[...] = jnp.full((8, 128), length[0], jnp.int32)
+    alive_ref[...] = jnp.full((8, 128), lengths_ref[0], jnp.int32)
 
 
 def arrival_rows(joining_ref, move, sector):
@@ -178,13 +160,13 @@
     return jnp.sum(jnp.where(lane // 32 == iota((16, 512), 0), value, 0), axis=0, keepdims=True)
 
 
-def first_proj(ref):
+def gather_proj(ref):
     return jnp.concatenate(
         [ref[i, 192 + b * 16 : 192 + (b + 1) * 16, :] for b in range(8) for i in range(INNER)], axis=0
     )
 
 
-def project(move, incoming_ref, proj_ref, joining_ref, out_ref):
+def project(move, incoming_ref, proj_ref, joining_ref, *refs):
     sector = lax.axis_index("sector")
     arrivals = arrival_rows(joining_ref, move, sector)
     row = iota((512, 512), 0)
@@ -200,40 +182,61 @@
         ],
         axis=0,
     )
-    right = first_proj(proj_ref) if move == 0 else proj_ref[...]
-    both = dot(left, right)
+    both = dot(left, gather_proj(proj_ref))
     term = both[:W, :W] + both[W:, W:]
-    packed = jnp.concatenate([term[:32], term[32:]], axis=1).astype(BF)
-    for j in range(INNER):
-        out_ref[j] = packed
-
-
-def finished(terms_ref, alive_ref):
-    total = terms_ref[0].astype(F32)
-    for j in range(1, INNER):
-        total = total + terms_ref[j].astype(F32)
+    packed = jnp.concatenate([term[:32], term[32:]], axis=1)
+    out_ref = refs[-1]
+    if move == 0:
+        rest_ref = refs[0]
+        high = packed.astype(BF)
+        low = (packed - high.astype(F32)).astype(BF)
+        for j in range(INNER):
+            out_ref[j, 0:32, :] = high
+            out_ref[j, 32:64, :] = low
+            out_ref[j, 64:320, :] = rest_ref[j]
+    else:
+        for j in range(INNER):
+            out_ref[j] = packed
+
+
+def finished(terms, alive_ref):
+    total = terms[0]
+    for term in terms[1:]:
+        total = total + term
     total = jnp.concatenate([total[:, :W], total[:, W:]], axis=0)
     alive = alive_ref[0:1, 0:W]
     keep = (iota((W, W), 0) < alive) & (iota((W, W), 1) < alive)
     return jnp.where(keep, total, 0.0).astype(BF)
 
 
-def second_rows(terms_ref, alive_ref, first_ref, edge_ref, joining_ref, corner_ref, out_ref):
+def second_rows(second_ref, alive_ref, first_ref, joining_ref, corner_ref, out_ref):
     sector = lax.axis_index("sector")
-    corner = finished(terms_ref, alive_ref)
+    terms = [
+        second_ref[j, 0:32, :].astype(F32) + second_ref[j, 32:64, :].astype(F32)
+        for j in range(INNER)
+    ]
+    corner = finished(terms, alive_ref)
     corner_ref[0] = corner
     slots = send_slots(own_row(joining_ref, 1, sector))
-    rows = expand(corner, slots, edge_ref[...], gather_site(first_ref))
+    rows = expand(corner, slots, gather_edges(second_ref, 64), gather_site(first_ref))
     for t in range(SECTORS):
         out_ref[t] = rows[t * 16 : (t + 1) * 16, :]
 
 
 def last(terms_ref, alive_ref, corner_ref):
-    corner_ref[0] = finished(terms_ref, alive_ref)
+    corner_ref[0] = finished([terms_ref[j] for j in range(INNER)], alive_ref)
 
 
 def vmem():
     return pl.BlockSpec(memory_space=pltpu.VMEM)
+
+
+def smem():
+    return pl.BlockSpec(memory_space=pltpu.SMEM)
+
+
+def second_move(array):
+    return pl.BlockSpec((1,) + array.shape[1:], lambda g: (1, 0, 0, 0))
 
 
 def hbm():
@@ -261,8 +264,6 @@
 
 
 def body(corner, edge_tensor, site_tensor, projector, lengths, joining):
-    edge_all = lax.all_gather(edge_tensor[1, 0], "inner", axis=0, tiled=True)
-    proj_all = lax.all_gather(projector[1, 0], "inner", axis=0, tiled=True)
     first = call(
         prep_first,
         shape((INNER, 320, 128), BF),
@@ -280,8 +281,17 @@
         name="prep_first",
     )
     first = swap(first, "inner")
+    rest_shape = (INNER, 256, 128)
+    rest = pl.pallas_call(
+        prep_rest,
+        grid=(1,),
+        out_shape=shape(rest_shape, BF),
+        in_specs=[second_move(edge_tensor), second_move(projector)],
+        out_specs=pl.BlockSpec(rest_shape, lambda g: (0, 0, 0)),
+        compiler_params=pltpu.CompilerParams(vmem_limit_bytes=32 * 2**20),
+        name="prep_rest",
+    )(edge_tensor, projector)
     rows_shape = shape((SECTORS, 16, KQ), BF)
-    terms_shape = shape((INNER, 32, 128), BF)
     corner_shape = shape((1, W, W), BF)
     rows, alive = call(
         first_rows,
@@ -290,30 +300,31 @@
         first,
         joining,
         lengths,
-        specs=[vmem(), vmem(), vmem(), hbm()],
-        scratch=[pltpu.SMEM((1,), jnp.int32), pltpu.SemaphoreType.DMA],
+        specs=[vmem(), vmem(), vmem(), smem()],
         name="first_rows",
+    )
+    rows = swap(rows, "sector")
+    second = call(
+        functools.partial(project, 0),
+        shape((INNER, 320, 128), BF),
+        rows,
+        first,
+        joining,
+        rest,
+        name="project_first",
+    )
+    second = swap(second, "inner")
+    one, rows = call(
+        second_rows, (corner_shape, rows_shape), second, alive, first, joining, name="second_rows"
     )
     rows = swap(rows, "sector")
     terms = call(
-        functools.partial(project, 0), terms_shape, rows, first, joining, name="project_first"
-    )
-    terms = swap(terms, "inner")
-    edges = call(pick_edge, shape((KQ, 512), BF), edge_all, name="pick_edge")
-    projs = call(pick_proj, shape((1024, 128), BF), proj_all, name="pick_proj")
-    one, rows = call(
-        second_rows,
-        (corner_shape, rows_shape),
-        terms,
-        alive,
-        first,
-        edges,
+        functools.partial(project, 1),
+        shape((INNER, 32, 128), F32),
+        rows,
+        second,
         joining,
-        name="second_rows",
-    )
-    rows = swap(rows, "sector")
-    terms = call(
-        functools.partial(project, 1), terms_shape, rows, projs, joining, name="project_second"
+        name="project_second",
     )
     terms = swap(terms, "inner")
     two = call(last, corner_shape, terms, alive, name="last")

time: 104 us -> 88.8 us (0.85)
  between operations: 14.7 us -> 1.37 us
  blocking collectives: 31.3 us -> 41.9 us
  local copies, waits for them, and re-layouts: 6.55 us -> 0.03 us
  waiting for transfers between devices: 21.7 us -> 18.4 us
  starting transfers between devices: 18.2 us -> 17 us
    all_to_all x2 -> x3, blocking collectives: 31.3 us -> 41.9 us  [swap(): return lax.all_to_all(x, axis, split_axis=0, concat_axis=0, tiled=True)]
    slice x2 -> x0, local copies, waits for them, and re-layouts: 3.35 us -> none  [the longest x1 1.69 us: body(): edge_all = lax.all_gather(edge_tensor[1, 0], 'inner', axis=0, tiled=True)]
    all_to_all x3 -> x2, waiting for transfers between devices: 21.7 us -> 18.4 us  [swap(): return lax.all_to_all(x, axis, split_axis=0, concat_axis=0, tiled=True)]
    unnamed x8, local copies, waits for them, and re-layouts: 3.2 us -> 0.03 us
    pallas_call x8 -> x6, Pallas kernels: 10.7 us -> 8.19 us  [call(): pl.pallas_call(kernel, out_shape=outs, in_specs=specs or [vmem()] * len(a...]
    pallas_call x0 -> x1, Pallas kernels: none -> 1.53 us  [body(): pl.pallas_call(prep_rest, grid=(1,), out_shape=shape(rest_shape, BF), in_...]
    all_to_all x3 -> x2, starting transfers between devices: 18.1 us -> 17 us  [swap(): return lax.all_to_all(x, axis, split_axis=0, concat_axis=0, tiled=True)]
  transfers between devices with their start and end apart: 5 -> 2, of which waited for: 3 -> 2; matrix products, arithmetic and copies ran while one was open for 2% -> 0% of each run, Pallas kernels for 9% -> 2%
where the time goes in v3:
time: 88.8 us; the launch traced here: 88.4 us
  blocking collectives  41.9 us (47%)
  waiting for transfers between devices  18.4 us (21%)
  starting transfers between devices  17 us (19%)
  Pallas kernels  9.72 us (11%)
  between operations  1.37 us (2%)
    all_to_all x3, blocking collectives, swap(): return lax.all_to_all(x, axis, split_axis=0, concat_axis=0, tiled=True)  41.9 us
    all_to_all x2, waiting for transfers between devices, swap(): return lax.all_to_all(x, axis, split_axis=0, concat_axis=0, tiled=True)  18.4 us
    all_to_all x2, starting transfers between devices, swap(): return lax.all_to_all(x, axis, split_axis=0, concat_axis=0, tiled=True)  17 us
    pallas_call x6, Pallas kernels, call(): pl.pallas_call(kernel, out_shape=outs, in_specs=specs or [vmem()] * len(a...  8.19 us
  transfers between devices with their start and end apart: 2, of which 2 were waited for; matrix products, arithmetic and copies ran while one was open for 0% of the time, Pallas kernels for 2%

profile of v3, /device:TPU:1, one launch (start us, length us, event | category | flops | bytes accessed | tf_op | source)
XLA Modules:
  0.0 88.4 jit_solution(17697247493164134087)
XLA Ops:
  0.6 3.2 %prep_first.1 = bf16[8,320,128]{2,1,0:T(8,128)(2,1)} custom-call(bf16[2,1,32,4096]{3,2,1,0:T(8,128)(2,1)} %edge_ref.1, bf16[1,32,256]{2,1,0:T(8,128)(2,1)} %bitcast.1, bf16[2,1,64,2048]{3,2,1,0:T(8,128)(2,1)} %proj_ref.1), custom_call_target="tpu_custom_call" | custom-call | tf_op jit(solution)/shard_map/prep_first/pallas_call | solution.py:247
  3.9 0.0 copy-start.2
  3.9 0.0 copy-start.3
  3.9 6.7 %all-to-all-start = ((bf16[8,320,128]{2,1,0:T(8,128)(2,1)}), bf16[8,320,128]{2,1,0:T(8,128)(2,1)S(1)}, u32[]{:S(2)}, u32[]{:S(2)}) async-start(bf16[8,320,128]{2,1,0:T(8,128)(2,1)} %prep_first.1), calls=%async_computation | async-start | bytes 1310720 | tf_op jit(solution)/shard_map/all_to_all | solution.py:263
  11.3 0.0 copy-start
  11.3 0.0 copy-start.1
  11.3 10.2 %all-to-all-done.first_ref.proj_ref = bf16[8,320,128]{2,1,0:T(8,128)(2,1)S(1)} async-done(((bf16[8,320,128]{2,1,0:T(8,128)(2,1)}), bf16[8,320,128]{2,1,0:T(8,128)(2,1)S(1)}, u32[]{:S(2)}, u32[]{:S(2)}) %all-to-all-start) | async-done | bytes 655392 | tf_op jit(solution)/shard_map/all_to_all | solution.py:263
  21.5 0.0 copy-done.2
  21.5 0.0 copy-done.3
  21.5 1.7 %first_rows.1 = (bf16[32,16,256]{2,1,0:T(8,128)(2,1)}, s32[8,128]{1,0:T(8,128)S(1)}) custom-call(bf16[1,64,64]{2,1,0:T(8,128)(2,1)S(1)} %copy-done.3, bf16[8,320,128]{2,1,0:T(8,128)(2,1)S(1)} %all-to-all-done.first_ref.proj_ref, s32[2,2048]{1,0:T(2,128)S(1)} %copy-done.2, s32[1]{0:T(128)S(6)} %copy.8.lengths_ref), custom_call_target="tpu_custom_call" | custom-call | tf_op jit(solution)/shard_map/first_rows/pallas_call | solution.py:247
  23.2 10.3 %all-to-all-start.1 = ((bf16[32,16,256]{2,1,0:T(8,128)(2,1)}), bf16[32,16,256]{2,1,0:T(8,128)(2,1)S(1)}, u32[]{:S(2)}, u32[]{:S(2)}) async-start(bf16[32,16,256]{2,1,0:T(8,128)(2,1)} %get-tuple-element.6), calls=%async_computation.1 | async-start | bytes 524288 | tf_op jit(solution)/shard_map/all_to_all | solution.py:263
  33.5 0.0 copy-done
  33.5 0.0 copy-done.1
  33.5 1.5 %prep_rest.1.refs_0_ = bf16[8,256,128]{2,1,0:T(8,128)(2,1)S(1)} custom-call(bf16[2,1,32,4096]{3,2,1,0:T(8,128)(2,1)S(1)} %copy-done, bf16[2,1,64,2048]{3,2,1,0:T(8,128)(2,1)S(1)} %copy-done.1), custom_call_target="tpu_custom_call" | custom-call | tf_op jit(solution)/shard_map/prep_rest/pallas_call | solution.py:285
  35.0 8.1 %all-to-all-done.1.incoming_ref = bf16[32,16,256]{2,1,0:T(8,128)(2,1)S(1)} async-done(((bf16[32,16,256]{2,1,0:T(8,128)(2,1)}), bf16[32,16,256]{2,1,0:T(8,128)(2,1)S(1)}, u32[]{:S(2)}, u32[]{:S(2)}) %all-to-all-start.1) | async-done | bytes 262176 | tf_op jit(solution)/shard_map/all_to_all | solution.py:263
  43.2 0.8 project_first.1
  44.0 16.9 %all_to_all.25.second_ref.proj_ref = bf16[8,320,128]{2,1,0:T(8,128)(2,1)S(1)} all-to-all(bf16[8,320,128]{2,1,0:T(8,128)(2,1)S(1)} %project_first.1), channel_id=1, replica_groups=mesh['sector'=32,'inner'=8] {'inner'}, dimensions={0} | all-to-all | bytes 1310720 | tf_op jit(solution)/shard_map/all_to_all | solution.py:263
  61.0 1.0 %second_rows.1 = (bf16[1,64,64]{2,1,0:T(8,128)(2,1)}, bf16[32,16,256]{2,1,0:T(8,128)(2,1)S(1)}) custom-call(bf16[8,320,128]{2,1,0:T(8,128)(2,1)S(1)} %all_to_all.25.second_ref.proj_ref, s32[8,128]{1,0:T(8,128)S(1)} %get-tuple-element.7.alive_ref, bf16[8,320,128]{2,1,0:T(8,128)(2,1)S(1)} %all-to-all-done.first_ref.proj_ref, s32[2,2048]{1,0:T(2,128)S(1)} %copy-done.2), custom_call_target="tpu_custom_call" | custom-call | tf_op jit(solution)/shard_map/second_rows/pallas_call | solution.py:247
  61.9 13.7 %all_to_all.26.incoming_ref = bf16[32,16,256]{2,1,0:T(8,128)(2,1)S(1)} all-to-all(bf16[32,16,256]{2,1,0:T(8,128)(2,1)S(1)} %get-tuple-element.9), channel_id=1, replica_groups=mesh['sector'=32,'inner'=8] {'sector'}, dimensions={0} | all-to-all | bytes 524288 | tf_op jit(solution)/shard_map/all_to_all | solution.py:263
  75.6 0.8 project_second.1
  76.5 11.3 %all_to_all.27.terms_ref = f32[8,32,128]{2,1,0:T(8,128)S(1)} all-to-all(f32[8,32,128]{2,1,0:T(8,128)S(1)} %project_second.1), channel_id=1, replica_groups=mesh['sector'=32,'inner'=8] {'inner'}, dimensions={0} | all-to-all | bytes 262144 | tf_op jit(solution)/shard_map/all_to_all | solution.py:263
  87.7 0.7 last.1
Async XLA Ops:
  3.9 17.6 %copy-start.2 = (s32[2,2048]{1,0:T(2,128)S(1)}, s32[2,2048]{1,0:T(2,128)}, u32[]{:S(2)}) copy-start(s32[2,2048]{1,0:T(2,128)} %joining_ref.7) | copy-start | bytes 49156
  3.9 17.6 %copy-start.3 = (bf16[1,64,64]{2,1,0:T(8,128)(2,1)S(1)}, bf16[1,64,64]{2,1,0:T(8,128)(2,1)}, u32[]{:S(2)}) copy-start(bf16[1,64,64]{2,1,0:T(8,128)(2,1)} %corner_ref.1) | copy-start | bytes 24580
  3.9 17.6 %all-to-all-start = ((bf16[8,320,128]{2,1,0:T(8,128)(2,1)}), bf16[8,320,128]{2,1,0:T(8,128)(2,1)S(1)}, u32[]{:S(2)}, u32[]{:S(2)}) async-start(bf16[8,320,128]{2,1,0:T(8,128)(2,1)} %prep_first.1), calls=%async_computation | async-start | bytes 1310720 | tf_op jit(solution)/shard_map/all_to_all | solution.py:263
  11.3 22.2 %copy-start = (bf16[2,1,32,4096]{3,2,1,0:T(8,128)(2,1)S(1)}, bf16[2,1,32,4096]{3,2,1,0:T(8,128)(2,1)}, u32[]{:S(2)}) copy-start(bf16[2,1,32,4096]{3,2,1,0:T(8,128)(2,1)} %edge_ref.1) | copy-start | bytes 1572868
  11.3 22.2 %copy-start.1 = (bf16[2,1,64,2048]{3,2,1,0:T(8,128)(2,1)S(1)}, bf16[2,1,64,2048]{3,2,1,0:T(8,128)(2,1)}, u32[]{:S(2)}) copy-start(bf16[2,1,64,2048]{3,2,1,0:T(8,128)(2,1)} %proj_ref.1) | copy-start | bytes 1572868
  23.2 20.0 %all-to-all-start.1 = ((bf16[32,16,256]{2,1,0:T(8,128)(2,1)}), bf16[32,16,256]{2,1,0:T(8,128)(2,1)S(1)}, u32[]{:S(2)}, u32[]{:S(2)}) async-start(bf16[32,16,256]{2,1,0:T(8,128)(2,1)} %get-tuple-element.6), calls=%async_computation.1 | async-start | bytes 524288 | tf_op jit(solution)/shard_map/all_to_all | solution.py:263

commit v4 on v2

v4 whole, which is shorter than its diff:
```python
import functools

import jax
import jax.numpy as jnp
from jax import lax
from jax.experimental import pallas as pl
from jax.experimental.pallas import tpu as pltpu
from jax.sharding import PartitionSpec as P

BF = jnp.bfloat16
F32 = jnp.float32
INNER = 8
SECTORS = 32
W = 64
KQ = 256


def iota(shape, dim):
    return lax.broadcasted_iota(jnp.int32, shape, dim)


def dot(a, b):
    return lax.dot_general(a, b, (((1,), (0,)), ((), ())), preferred_element_type=F32)


def dot_nt(a, b):
    return lax.dot_general(a, b, (((1,), (1,)), ((), ())), preferred_element_type=F32)


def one_hot(cond):
    return jnp.where(cond, 1.0, 0.0).astype(BF)


def shuffle_matrix():
    row = iota((1024, 1), 0)
    want = (row % 16) * 64 + (row // 128) * 8 + (row // 16) % 8
    return one_hot(iota((1024, 1024), 1) == want)


def prep(
    edge_hbm,
    site_hbm,
    proj_hbm,
    first_hbm,
    keep_hbm,
    give_hbm,
    edge_ref,
    site_ref,
    proj_ref,
    first_ref,
    rest_ref,
    sems,
):
    copies = [
        pltpu.make_async_copy(edge_hbm, edge_ref, sems.at[0]),
        pltpu.make_async_copy(proj_hbm, proj_ref, sems.at[1]),
        pltpu.make_async_copy(site_hbm, site_ref, sems.at[2]),
    ]
    for copy in copies:
        copy.start()
    shuffle = shuffle_matrix()
    copies[0].wait()
    copies[2].wait()
    stacked = jnp.concatenate(
        [edge_ref[m, 0, :, n * 1024 : (n + 1) * 1024] for m in range(2) for n in range(4)], axis=0
    )
    blocks = dot_nt(stacked, shuffle).astype(BF)
    site_t = site_ref[0]
    for j in range(INNER):
        first_ref[j, 0:128, :] = blocks[0:128, j * 128 : (j + 1) * 128]
        rest_ref[j // 2, j % 2, 128:256, :] = blocks[128:256, j * 128 : (j + 1) * 128]
        first_ref[j, 128:160, :] = site_t[:, 0:128]
        first_ref[j, 160:192, :] = site_t[:, 128:256]
    outs = [
        pltpu.make_async_copy(first_ref, first_hbm, sems.at[3]),
    ]
    core = lax.axis_index("inner") % 2
    outs.append(pltpu.make_async_copy(rest_ref.at[:, core], keep_hbm, sems.at[4]))
    outs.append(pltpu.make_async_copy(rest_ref.at[:, 1 - core], give_hbm, sems.at[5]))
    outs[0].start()
    copies[1].wait()
    stacked = jnp.concatenate(
        [proj_ref[m, 0, :, n * 1024 : (n + 1) * 1024] for m in range(2) for n in range(2)], axis=0
    )
    rows = dot_nt(shuffle, stacked).astype(BF)
    for j in range(INNER):
        rest_ref[j // 2, j % 2, 0:128, :] = rows[j * 128 : (j + 1) * 128, 0:128]
        rest_ref[j // 2, j % 2, 256:384, :] = rows[j * 128 : (j + 1) * 128, 128:256]
    for copy in outs[1:]:
        copy.start()
    for copy in outs:
        copy.wait()


def own_row(joining_ref, move, sector):
    pair = joining_ref[move : move + 1, pl.ds(pl.multiple_of((sector // 2) * 128, 128), 128)]
    return jnp.where(sector % 2 == 0, pair[:, :W], pair[:, W:])


def send_slots(own):
    column = jnp.sum(
        jnp.where(iota((W, W), 0) == iota((W, W), 1), own, 0), axis=1, keepdims=True
    )
    before = ((column // W) == (own // W)) & (column < own)
    rank = jnp.sum(before.astype(jnp.int32), axis=0, keepdims=True)
    return (own // W) * 2 + rank


def expand(corner, slots, edges, site_t):
    pick = one_hot(slots == iota((512, W), 0) // 8)
    picked = dot(pick, corner).astype(BF)
    lane = iota((W, 512), 1)
    spread = one_hot((lane // 128) * 16 + lane % 16 == iota((W, 512), 0))
    wide_lane = iota((512, 512), 1)
    same = (wide_lane // 16) % 8 == iota((512, 512), 0) % 8
    kron = jnp.where(same, dot(picked, spread), 0.0).astype(BF)
    expanded = dot_nt(kron, edges).astype(BF)
    return dot_nt(expanded, site_t).astype(BF)


def gather_edges(read):
    parts = []
    for n in range(4):
        parts.append(
            jnp.concatenate(
                [read(i, n * 32, 32) for i in range(INNER)], axis=0
            )
        )
    return jnp.concatenate(parts, axis=1)


def gather_site(ref):
    halves = []
    for n in range(2):
        pieces = []
        for h in range(2):
            for i in range(INNER):
                start = 128 + n * 32 + h * 16
                pieces.append(ref[i, start : start + 16, :])
        halves.append(jnp.concatenate(pieces, axis=0))
    return jnp.concatenate(halves, axis=1)


def first_rows(
    corner_ref,
    first_ref,
    joining_ref,
    lengths_ref,
    keep_ref,
    took_ref,
    out_ref,
    alive_ref,
    *step_refs,
):
    chip = lax.axis_index("inner") // 2
    for step in range(4):
        to = (chip + step) % 4
        for plane, ref in enumerate((keep_ref, took_ref)):
            step_refs[step][plane] = ref[to, 0:128, :]
            step_refs[4 + step][plane] = ref[to, 128:384, :]
    alive_ref[...] = jnp.full((8, 128), lengths_ref[0], jnp.int32)
    sector = lax.axis_index("sector")
    slots = send_slots(own_row(joining_ref, 0, sector))
    rows = expand(corner_ref[0], slots, gather_edges(lambda i, a, n: first_ref[i, a : a + n, :]), gather_site(first_ref))
    for t in range(SECTORS):
        out_ref[t] = rows[t * 16 : (t + 1) * 16, :]


def arrival_rows(joining_ref, move, sector):
    chunks = jnp.concatenate(
        [joining_ref[move : move + 1, n * 128 : (n + 1) * 128] for n in range(16)], axis=0
    )
    mine = (chunks // W) == sector
    place = chunks % W
    low = jnp.where(mine, place, W)
    high = jnp.where(mine, place, -1)
    even = iota((16, 128), 1) < W
    columns = [
        jnp.min(jnp.where(even, low, W), axis=1, keepdims=True),
        jnp.max(jnp.where(even, high, -1), axis=1, keepdims=True),
        jnp.min(jnp.where(even, W, low), axis=1, keepdims=True),
        jnp.max(jnp.where(even, -1, high), axis=1, keepdims=True),
    ]
    lane = iota((16, 512), 1)
    kind = (lane // 8) % 4
    value = jnp.where(
        kind == 0,
        columns[0],
        jnp.where(kind == 1, columns[1], jnp.where(kind == 2, columns[2], columns[3])),
    )
    return jnp.sum(jnp.where(lane // 32 == iota((16, 512), 0), value, 0), axis=0, keepdims=True)


def by_source(step_refs, start, blocks_ref):
    chip, core = lax.axis_index("inner") // 2, lax.axis_index("inner") % 2
    for step, ref in enumerate(step_refs):
        source = (chip + 4 - step) % 4 * 2
        blocks_ref[source + core] = ref[0, start : start + 128, :]
        blocks_ref[source + 1 - core] = ref[1, start : start + 128, :]


def project(move, incoming_ref, joining_ref, *refs):
    *step_refs, out_ref, blocks_ref = refs
    by_source(step_refs, 0 if move == 0 else 128, blocks_ref)
    pieces = [blocks_ref[i, b * 16 : (b + 1) * 16, :] for b in range(8) for i in range(INNER)]
    proj = jnp.concatenate(pieces, axis=0)
    sector = lax.axis_index("sector")
    arrivals = arrival_rows(joining_ref, move, sector)
    row = iota((512, 512), 0)
    place = one_hot((row // W == iota((512, 512), 1) % 8) & (row % W == arrivals))
    incoming = jnp.concatenate([incoming_ref[s] for s in range(SECTORS)], axis=0)
    placed = dot(place, incoming).astype(BF)
    left = jnp.concatenate(
        [
            jnp.concatenate(
                [placed[b * W : (b + 1) * W, h * 128 : (h + 1) * 128] for b in range(8)], axis=1
            )
            for h in range(2)
        ],
        axis=0,
    )
    both = dot(left, proj)
    term = both[:W, :W] + both[W:, W:]
    packed = jnp.concatenate([term[:32], term[32:]], axis=1)
    for j in range(INNER):
        out_ref[j] = packed


def finished(terms, alive_ref):
    total = terms[0]
    for term in terms[1:]:
        total = total + term
    total = jnp.concatenate([total[:, :W], total[:, W:]], axis=0)
    alive = alive_ref[0:1, 0:W]
    keep = (iota((W, W), 0) < alive) & (iota((W, W), 1) < alive)
    return jnp.where(keep, total, 0.0).astype(BF)


def second_rows(terms_ref, alive_ref, first_ref, joining_ref, *refs):
    *step_refs, corner_ref, out_ref, blocks_ref = refs
    by_source(step_refs, 0, blocks_ref)
    sector = lax.axis_index("sector")
    terms = [terms_ref[j] for j in range(INNER)]
    corner = finished(terms, alive_ref)
    corner_ref[0] = corner
    slots = send_slots(own_row(joining_ref, 1, sector))
    rows = expand(corner, slots, gather_edges(lambda i, a, n: blocks_ref[i, a : a + n, :]), gather_site(first_ref))
    for t in range(SECTORS):
        out_ref[t] = rows[t * 16 : (t + 1) * 16, :]


def last(terms_ref, alive_ref, corner_ref):
    corner_ref[0] = finished([terms_ref[j] for j in range(INNER)], alive_ref)


def vmem():
    return pl.BlockSpec(memory_space=pltpu.VMEM)


def smem():
    return pl.BlockSpec(memory_space=pltpu.SMEM)


def hbm():
    return pl.BlockSpec(memory_space=pltpu.HBM)


def call(kernel, outs, *args, specs=None, out_specs=None, scratch=(), room=32, name=None):
    return pl.pallas_call(
        kernel,
        out_shape=outs,
        in_specs=specs or [vmem()] * len(args),
        out_specs=out_specs or jax.tree.map(lambda _: vmem(), outs),
        scratch_shapes=scratch,
        compiler_params=pltpu.CompilerParams(vmem_limit_bytes=room * 2**20),
        name=name,
    )(*args)


def shape(dims, dtype):
    return jax.ShapeDtypeStruct(dims, dtype)


def swap(x, axis):
    return lax.all_to_all(x, axis, split_axis=0, concat_axis=0, tiled=True)


def body(corner, edge_tensor, site_tensor, projector, lengths, joining):
    first, keep, give = call(
        prep,
        (shape((INNER, 192, 128), BF),) + (shape((4, 384, 128), BF),) * 2,
        edge_tensor,
        jnp.swapaxes(site_tensor, 1, 2),
        projector,
        specs=[hbm(), hbm(), hbm()],
        out_specs=(hbm(),) * 3,
        scratch=[
            pltpu.VMEM((2, 1, 32, 4096), BF),
            pltpu.VMEM((1, 32, KQ), BF),
            pltpu.VMEM((2, 1, W, 2048), BF),
            pltpu.VMEM((INNER, 192, 128), BF),
            pltpu.VMEM((4, 2, 384, 128), BF),
            pltpu.SemaphoreType.DMA((6,)),
        ],
        room=60,
        name="prep",
    )
    first = swap(first, "inner")
    took = lax.ppermute(give, "inner", [(i, i ^ 1) for i in range(INNER)])
    rows_shape = shape((SECTORS, 16, KQ), BF)
    corner_shape = shape((1, W, W), BF)
    rows, alive, *steps = call(
        first_rows,
        (rows_shape, shape((8, 128), jnp.int32)) + (shape((2, 128, 128), BF),) * 4
        + (shape((2, 256, 128), BF),) * 4,
        corner,
        first,
        joining,
        lengths,
        keep,
        took,
        specs=[vmem(), vmem(), vmem(), smem(), vmem(), vmem()],
        name="first_rows",
    )
    rows = swap(rows, "sector")
    for step in (1, 2, 3, 5, 6, 7):
        pairs = [(i, (i + 2 * step) % INNER) for i in range(INNER)]
        steps[step] = lax.ppermute(steps[step], "inner", pairs)
    terms_shape = shape((INNER, 32, 128), F32)
    blocks = [pltpu.VMEM((INNER, 128, 128), BF)]
    terms = call(
        functools.partial(project, 0),
        terms_shape,
        rows,
        joining,
        *steps[:4],
        scratch=blocks,
        name="project_first",
    )
    terms = swap(terms, "inner")
    one, rows = call(
        second_rows,
        (corner_shape, rows_shape),
        terms,
        alive,
        first,
        joining,
        *steps[4:],
        scratch=blocks,
        name="second_rows",
    )
    rows = swap(rows, "sector")
    terms = call(
        functools.partial(project, 1),
        terms_shape,
        rows,
        joining,
        *steps[4:],
        scratch=blocks,
        name="project_second",
    )
    terms = swap(terms, "inner")
    two = call(last, corner_shape, terms, alive, name="last")
    return (one, two)


def solution(mesh):
    placed = (
        P("sector", None, None),
        P(None, "sector", "inner", None),
        P("sector", None, "inner"),
        P(None, "sector", None, "inner"),
        P("sector"),
        P(),
    )
    return jax.shard_map(
        body,
        mesh=mesh,
        in_specs=placed,
        out_specs=(P("sector", None, None), P("sector", None, None)),
        check_vma=False,
    )
```

time: 104 us -> 84.7 us (0.81)
  between operations: 14.7 us -> 1.35 us
  starting transfers between devices: 18.2 us -> 31.4 us
  local copies, waits for them, and re-layouts: 6.55 us -> 0.01 us
  waiting for transfers between devices: 21.7 us -> 15.2 us
  blocking collectives: 31.3 us -> 27 us
  Pallas kernels: 10.7 us -> 9.13 us
    ppermute x0 -> x7, starting transfers between devices: none -> 10.5 us  [the longest x6 7.19 us: body(): steps[step] = lax.ppermute(steps[step], 'inner', pairs)]
    all_to_all x3, waiting for transfers between devices: 21.7 us -> 15.2 us  [swap(): return lax.all_to_all(x, axis, split_axis=0, concat_axis=0, tiled=True)]
    all_to_all x2, blocking collectives: 31.3 us -> 27 us  [swap(): return lax.all_to_all(x, axis, split_axis=0, concat_axis=0, tiled=True)]
    slice x2 -> x0, local copies, waits for them, and re-layouts: 3.35 us -> none  [the longest x1 1.69 us: body(): edge_all = lax.all_gather(edge_tensor[1, 0], 'inner', axis=0, tiled=True)]
    unnamed x8 -> x6, local copies, waits for them, and re-layouts: 3.2 us -> 0.01 us
    all_to_all x3, starting transfers between devices: 18.1 us -> 20.9 us  [swap(): return lax.all_to_all(x, axis, split_axis=0, concat_axis=0, tiled=True)]
    pallas_call x8 -> x6, Pallas kernels: 10.7 us -> 9.13 us  [call(): pl.pallas_call(kernel, out_shape=outs, in_specs=specs or [vmem()] * len(a...]
  transfers between devices with their start and end apart: 5 -> 10, of which waited for: 3 -> 3; matrix products, arithmetic and copies ran while one was open for 2% -> 0% of each run, Pallas kernels for 9% -> 2%
where the time goes in v4:
time: 84.7 us; the launch traced here: 84.1 us
  starting transfers between devices  31.4 us (37%)
  blocking collectives  27 us (32%)
  waiting for transfers between devices  15.2 us (18%)
  Pallas kernels  9.13 us (11%)
  between operations  1.35 us (2%)
    all_to_all x2, blocking collectives, swap(): return lax.all_to_all(x, axis, split_axis=0, concat_axis=0, tiled=True)  27 us
    all_to_all x3, starting transfers between devices, swap(): return lax.all_to_all(x, axis, split_axis=0, concat_axis=0, tiled=True)  20.9 us
    all_to_all x3, waiting for transfers between devices, swap(): return lax.all_to_all(x, axis, split_axis=0, concat_axis=0, tiled=True)  15.2 us
    pallas_call x6, Pallas kernels, call(): pl.pallas_call(kernel, out_shape=outs, in_specs=specs or [vmem()] * len(a...  9.13 us
    ppermute x6, starting transfers between devices, body(): steps[step] = lax.ppermute(steps[step], 'inner', pairs)  7.19 us
    ppermute x1, starting transfers between devices, body(): took = lax.ppermute(give, 'inner', [(i, i ^ 1) for i in range(INNER)])  3.33 us
  transfers between devices with their start and end apart: 10, of which 3 were waited for; matrix products, arithmetic and copies ran while one was open for 0% of the time, Pallas kernels for 2%

profile of v4, /device:TPU:1, one launch (start us, length us, event | category | flops | bytes accessed | tf_op | source)
XLA Modules:
  0.0 84.1 jit_solution(17315928246884594445)
XLA Ops:
  0.6 3.5 %prep.1 = (bf16[8,192,128]{2,1,0:T(8,128)(2,1)}, bf16[4,384,128]{2,1,0:T(8,128)(2,1)}, bf16[4,384,128]{2,1,0:T(8,128)(2,1)}) custom-call(bf16[2,1,32,4096]{3,2,1,0:T(8,128)(2,1)} %edge_hbm.1, bf16[1,32,256]{2,1,0:T(8,128)(2,1)} %bitcast.1, bf16[2,1,64,2048]{3,2,1,0:T(8,128)(2,1)} %proj_hbm.1), custom_call_target="tpu_custom_call" | custom-call | tf_op jit(solution)/shard_map/prep/pallas_call | solution.py:269
  4.1 3.3 %collective-permute-start = (bf16[4,384,128]{2,1,0:T(8,128)(2,1)}, bf16[4,384,128]{2,1,0:T(8,128)(2,1)S(1)}, u32[]{:S(2)}, u32[]{:S(2)}) collective-permute-start(bf16[4,384,128]{2,1,0:T(8,128)(2,1)} %get-tuple-element.19), channel_id=1, source_target_pairs={{0,1},{1,0},{2,3},{3,2},{4,5},{5,4},{6,7},{7,6},{8,9},{9,8},{10,11... | collective-permute-start | bytes 1179656 | tf_op jit(solution)/shard_map/ppermute | solution.py:309
  7.5 0.0 copy-start
  7.5 3.5 %all-to-all-start = ((bf16[8,192,128]{2,1,0:T(8,128)(2,1)}), bf16[8,192,128]{2,1,0:T(8,128)(2,1)S(1)}, u32[]{:S(2)}, u32[]{:S(2)}) async-start(bf16[8,192,128]{2,1,0:T(8,128)(2,1)} %get-tuple-element.17), calls=%async_computation | async-start | bytes 786432 | tf_op jit(solution)/shard_map/all_to_all | solution.py:285
  11.7 7.4 %all-to-all-done.first_ref = bf16[8,192,128]{2,1,0:T(8,128)(2,1)S(1)} async-done(((bf16[8,192,128]{2,1,0:T(8,128)(2,1)}), bf16[8,192,128]{2,1,0:T(8,128)(2,1)S(1)}, u32[]{:S(2)}, u32[]{:S(2)}) %all-to-all-start) | async-done | bytes 393248 | tf_op jit(solution)/shard_map/all_to_all | solution.py:285
  19.1 0.0 collective-permute-done.took_ref
  19.1 0.0 copy-done
  19.1 0.0 copy-done.1
  19.1 0.0 copy-done.2
  19.1 1.7 %first_rows.1 = (bf16[32,16,256]{2,1,0:T(8,128)(2,1)}, s32[8,128]{1,0:T(8,128)S(1)}, bf16[2,128,128]{2,1,0:T(8,128)(2,1)S(1)}, bf16[2,128,128]{2,1,0:T(8,128)(2,...) custom-call(bf16[1,64,64]{2,1,0:T(8,128)(2,1)S(1)} %copy-done.2, ...), custom_call_target="tpu_custom_call" | custom-call | tf_op jit(solution)/shard_map/first_rows/pallas_call | solution.py:269
  20.8 10.5 %all-to-all-start.1 = ((bf16[32,16,256]{2,1,0:T(8,128)(2,1)}), bf16[32,16,256]{2,1,0:T(8,128)(2,1)S(1)}, u32[]{:S(2)}, u32[]{:S(2)}) async-start(bf16[32,16,256]{2,1,0:T(8,128)(2,1)} %get-tuple-element.20), calls=%async_computation.1 | async-start | bytes 524288 | tf_op jit(solution)/shard_map/all_to_all | solution.py:285
  31.3 0.4 collective-permute-start.1
  31.7 1.8 %collective-permute-start.2 = (bf16[2,128,128]{2,1,0:T(8,128)(2,1)S(1)}, bf16[2,128,128]{2,1,0:T(8,128)(2,1)S(1)}, u32[]{:S(2)}, u32[]{:S(2)}) collective-permute-start(bf16[2,128,128]{2,1,0:T(8,128)(2,1)S(1)} %get-tuple-element.23), channel_id=1, source_target_pairs={{0,4},{1,5},{2,6},{3,7},{4,0},{5,1},{6,2},{7,3},{8,12},{9,13},{10,... | collective-permute-start | bytes 196616 | tf_op jit(solution)/shard_map/ppermute | solution.py:328
  33.4 0.7 collective-permute-start.3
  34.1 0.8 collective-permute-start.4
  34.9 1.5 %collective-permute-start.5 = (bf16[2,256,128]{2,1,0:T(8,128)(2,1)S(1)}, bf16[2,256,128]{2,1,0:T(8,128)(2,1)S(1)}, u32[]{:S(2)}, u32[]{:S(2)}) collective-permute-start(bf16[2,256,128]{2,1,0:T(8,128)(2,1)S(1)} %get-tuple-element.28), channel_id=1, source_target_pairs={{0,4},{1,5},{2,6},{3,7},{4,0},{5,1},{6,2},{7,3},{8,12},{9,13},{10,... | collective-permute-start | bytes 393224 | tf_op jit(solution)/shard_map/ppermute | solution.py:328
  36.4 0.0 collective-permute-done.1.refs_1_
  36.4 2.1 %collective-permute-start.6 = (bf16[2,256,128]{2,1,0:T(8,128)(2,1)S(1)}, bf16[2,256,128]{2,1,0:T(8,128)(2,1)S(1)}, u32[]{:S(2)}, u32[]{:S(2)}) collective-permute-start(bf16[2,256,128]{2,1,0:T(8,128)(2,1)S(1)} %get-tuple-element.29), channel_id=1, source_target_pairs={{0,6},{1,7},{2,0},{3,1},{4,2},{5,3},{6,4},{7,5},{8,14},{9,15},{10,... | collective-permute-start | bytes 393224 | tf_op jit(solution)/shard_map/ppermute | solution.py:328
  38.5 0.0 collective-permute-done.2.refs_2_
  38.5 0.0 collective-permute-done.3.refs_3_
  38.5 2.5 %all-to-all-done.1.incoming_ref = bf16[32,16,256]{2,1,0:T(8,128)(2,1)S(1)} async-done(((bf16[32,16,256]{2,1,0:T(8,128)(2,1)}), bf16[32,16,256]{2,1,0:T(8,128)(2,1)S(1)}, u32[]{:S(2)}, u32[]{:S(2)}) %all-to-all-start.1) | async-done | bytes 262176 | tf_op jit(solution)/shard_map/all_to_all | solution.py:285
  41.0 1.5 %project_first.1 = f32[8,32,128]{2,1,0:T(8,128)} custom-call(bf16[32,16,256]{2,1,0:T(8,128)(2,1)S(1)} %all-to-all-done.1.incoming_ref, s32[2,2048]{1,0:T(2,128)S(1)} %copy-done.1, bf16[2,128,128]{2,1,0:T(8,128)(2,1)S(1)} %get-tuple-element.21.refs_0_, bf16[2,128,128]{2,1,0:T(8,128)(2,1)S(1)} %collective-permute-done.1.refs_1_, ...), custom_call_target="tpu_custom_call" | custom-call | tf_op jit(solution)/shard_map/project_first/pallas_call | solution.py:269
  42.5 6.9 %all-to-all-start.2 = ((f32[8,32,128]{2,1,0:T(8,128)}), f32[8,32,128]{2,1,0:T(8,128)S(1)}, u32[]{:S(2)}, u32[]{:S(2)}) async-start(f32[8,32,128]{2,1,0:T(8,128)} %project_first.1), calls=%async_computation.2 | async-start | bytes 262144 | tf_op jit(solution)/shard_map/all_to_all | solution.py:285
  49.4 0.0 collective-permute-done.4.refs_1_
  49.4 0.0 collective-permute-done.5.refs_2_
  49.4 0.0 collective-permute-done.6.refs_3_
  49.4 5.3 %all-to-all-done.2.terms_ref = f32[8,32,128]{2,1,0:T(8,128)S(1)} async-done(((f32[8,32,128]{2,1,0:T(8,128)}), f32[8,32,128]{2,1,0:T(8,128)S(1)}, u32[]{:S(2)}, u32[]{:S(2)}) %all-to-all-start.2) | async-done | bytes 131104 | tf_op jit(solution)/shard_map/all_to_all | solution.py:285
  54.7 1.0 %second_rows.1 = (bf16[1,64,64]{2,1,0:T(8,128)(2,1)}, bf16[32,16,256]{2,1,0:T(8,128)(2,1)S(1)}) custom-call(f32[8,32,128]{2,1,0:T(8,128)S(1)} %all-to-all-done.2.terms_ref, s32[8,128]{1,0:T(8,128)S(1)} %get-tuple-element.25.alive_ref, bf16[8,192,128]{2,1,0:T(8,128)(2,1)S(1)} %all-to-all-done.first_ref, s32[2,2048]{1,0:T(2,128)S(1)} %copy-done.1, ...), custom_call_target="tpu_custom_call" | custom-call | tf_op jit(solution)/shard_map/second_rows/pallas_call | solution.py:269
  55.6 15.7 %all_to_all.25.incoming_ref = bf16[32,16,256]{2,1,0:T(8,128)(2,1)S(1)} all-to-all(bf16[32,16,256]{2,1,0:T(8,128)(2,1)S(1)} %get-tuple-element.31), channel_id=1, replica_groups=mesh['sector'=32,'inner'=8] {'sector'}, dimensions={0} | all-to-all | bytes 524288 | tf_op jit(solution)/shard_map/all_to_all | solution.py:285
  71.4 0.8 project_second.1
  72.2 11.3 %all_to_all.26.terms_ref = f32[8,32,128]{2,1,0:T(8,128)S(1)} all-to-all(f32[8,32,128]{2,1,0:T(8,128)S(1)} %project_second.1), channel_id=1, replica_groups=mesh['sector'=32,'inner'=8] {'inner'}, dimensions={0} | all-to-all | bytes 262144 | tf_op jit(solution)/shard_map/all_to_all | solution.py:285
  83.5 0.7 last.1
  (2 shorter events, 0.0 us)
Async XLA Ops:
  4.1 15.0 %collective-permute-start = (bf16[4,384,128]{2,1,0:T(8,128)(2,1)}, bf16[4,384,128]{2,1,0:T(8,128)(2,1)S(1)}, u32[]{:S(2)}, u32[]{:S(2)}) collective-permute-start(bf16[4,384,128]{2,1,0:T(8,128)(2,1)} %get-tuple-element.19), channel_id=1, source_target_pairs={{0,1},{1,0},{2,3},{3,2},{4,5},{5,4},{6,7},{7,6},{8,9},{9,8},{10,11... | collective-permute-start | bytes 1179656 | tf_op jit(solution)/shard_map/ppermute | solution.py:309
  7.5 11.6 %copy-start = (bf16[4,384,128]{2,1,0:T(8,128)(2,1)S(1)}, bf16[4,384,128]{2,1,0:T(8,128)(2,1)}, u32[]{:S(2)}) copy-start(bf16[4,384,128]{2,1,0:T(8,128)(2,1)} %get-tuple-element.18.keep_ref) | copy-start | bytes 1179652
  7.5 11.6 %copy-start.1 = (s32[2,2048]{1,0:T(2,128)S(1)}, s32[2,2048]{1,0:T(2,128)}, u32[]{:S(2)}) copy-start(s32[2,2048]{1,0:T(2,128)} %joining_ref.7) | copy-start | bytes 49156
  7.5 11.6 %copy-start.2 = (bf16[1,64,64]{2,1,0:T(8,128)(2,1)S(1)}, bf16[1,64,64]{2,1,0:T(8,128)(2,1)}, u32[]{:S(2)}) copy-start(bf16[1,64,64]{2,1,0:T(8,128)(2,1)} %corner_ref.1) | copy-start | bytes 24580
  7.5 11.6 %all-to-all-start = ((bf16[8,192,128]{2,1,0:T(8,128)(2,1)}), bf16[8,192,128]{2,1,0:T(8,128)(2,1)S(1)}, u32[]{:S(2)}, u32[]{:S(2)}) async-start(bf16[8,192,128]{2,1,0:T(8,128)(2,1)} %get-tuple-element.17), calls=%async_computation | async-start | bytes 786432 | tf_op jit(solution)/shard_map/all_to_all | solution.py:285
  20.8 20.2 %all-to-all-start.1 = ((bf16[32,16,256]{2,1,0:T(8,128)(2,1)}), bf16[32,16,256]{2,1,0:T(8,128)(2,1)S(1)}, u32[]{:S(2)}, u32[]{:S(2)}) async-start(bf16[32,16,256]{2,1,0:T(8,128)(2,1)} %get-tuple-element.20), calls=%async_computation.1 | async-start | bytes 524288 | tf_op jit(solution)/shard_map/all_to_all | solution.py:285
  31.3 5.1 %collective-permute-start.1 = (bf16[2,128,128]{2,1,0:T(8,128)(2,1)S(1)}, bf16[2,128,128]{2,1,0:T(8,128)(2,1)S(1)}, u32[]{:S(2)}, u32[]{:S(2)}) collective-permute-start(bf16[2,128,128]{2,1,0:T(8,128)(2,1)S(1)} %get-tuple-element.22), channel_id=1, source_target_pairs={{0,2},{1,3},{2,4},{3,5},{4,6},{5,7},{6,0},{7,1},{8,10},{9,11},{10,... | collective-permute-start | bytes 196616 | tf_op jit(solution)/shard_map/ppermute | solution.py:328
  31.7 6.8 %collective-permute-start.2 = (bf16[2,128,128]{2,1,0:T(8,128)(2,1)S(1)}, bf16[2,128,128]{2,1,0:T(8,128)(2,1)S(1)}, u32[]{:S(2)}, u32[]{:S(2)}) collective-permute-start(bf16[2,128,128]{2,1,0:T(8,128)(2,1)S(1)} %get-tuple-element.23), channel_id=1, source_target_pairs={{0,4},{1,5},{2,6},{3,7},{4,0},{5,1},{6,2},{7,3},{8,12},{9,13},{10,... | collective-permute-start | bytes 196616 | tf_op jit(solution)/shard_map/ppermute | solution.py:328
  33.4 5.1 %collective-permute-start.3 = (bf16[2,128,128]{2,1,0:T(8,128)(2,1)S(1)}, bf16[2,128,128]{2,1,0:T(8,128)(2,1)S(1)}, u32[]{:S(2)}, u32[]{:S(2)}) collective-permute-start(bf16[2,128,128]{2,1,0:T(8,128)(2,1)S(1)} %get-tuple-element.24), channel_id=1, source_target_pairs={{0,6},{1,7},{2,0},{3,1},{4,2},{5,3},{6,4},{7,5},{8,14},{9,15},{10,... | collective-permute-start | bytes 196616 | tf_op jit(solution)/shard_map/ppermute | solution.py:328
  34.1 15.2 %collective-permute-start.4 = (bf16[2,256,128]{2,1,0:T(8,128)(2,1)S(1)}, bf16[2,256,128]{2,1,0:T(8,128)(2,1)S(1)}, u32[]{:S(2)}, u32[]{:S(2)}) collective-permute-start(bf16[2,256,128]{2,1,0:T(8,128)(2,1)S(1)} %get-tuple-element.27), channel_id=1, source_target_pairs={{0,2},{1,3},{2,4},{3,5},{4,6},{5,7},{6,0},{7,1},{8,10},{9,11},{10,... | collective-permute-start | bytes 393224 | tf_op jit(solution)/shard_map/ppermute | solution.py:328
  34.9 14.5 %collective-permute-start.5 = (bf16[2,256,128]{2,1,0:T(8,128)(2,1)S(1)}, bf16[2,256,128]{2,1,0:T(8,128)(2,1)S(1)}, u32[]{:S(2)}, u32[]{:S(2)}) collective-permute-start(bf16[2,256,128]{2,1,0:T(8,128)(2,1)S(1)} %get-tuple-element.28), channel_id=1, source_target_pairs={{0,4},{1,5},{2,6},{3,7},{4,0},{5,1},{6,2},{7,3},{8,12},{9,13},{10,... | collective-permute-start | bytes 393224 | tf_op jit(solution)/shard_map/ppermute | solution.py:328
  36.4 13.0 %collective-permute-start.6 = (bf16[2,256,128]{2,1,0:T(8,128)(2,1)S(1)}, bf16[2,256,128]{2,1,0:T(8,128)(2,1)S(1)}, u32[]{:S(2)}, u32[]{:S(2)}) collective-permute-start(bf16[2,256,128]{2,1,0:T(8,128)(2,1)S(1)} %get-tuple-element.29), channel_id=1, source_target_pairs={{0,6},{1,7},{2,0},{3,1},{4,2},{5,3},{6,4},{7,5},{8,14},{9,15},{10,... | collective-permute-start | bytes 393224 | tf_op jit(solution)/shard_map/ppermute | solution.py:328
  42.5 12.2 %all-to-all-start.2 = ((f32[8,32,128]{2,1,0:T(8,128)}), f32[8,32,128]{2,1,0:T(8,128)S(1)}, u32[]{:S(2)}, u32[]{:S(2)}) async-start(f32[8,32,128]{2,1,0:T(8,128)} %project_first.1), calls=%async_computation.2 | async-start | bytes 262144 | tf_op jit(solution)/shard_map/all_to_all | solution.py:285

commit v5 on v4

--- a/solution.py
+++ b/solution.py
@@ -92,6 +92,16 @@
         copy.wait()
 
 
+def tables(corner_ref, joining_ref, lengths_ref, kron_ref, info_ref):
+    sector = lax.axis_index("sector")
+    pick = pick_matrix(send_slots(own_row(joining_ref, 0, sector)))
+    kron_ref[...] = kron_matrix(pick, corner_ref[0])
+    for move in range(2):
+        info_ref[move : move + 1, :] = arrival_rows(joining_ref, move, sector)
+    info_ref[2:3, 0:W] = send_slots(own_row(joining_ref, 1, sector))
+    info_ref[3:4, :] = jnp.full((1, 512), lengths_ref[0], jnp.int32)
+
+
 def own_row(joining_ref, move, sector):
     pair = joining_ref[move : move + 1, pl.ds(pl.multiple_of((sector // 2) * 128, 128), 128)]
     return jnp.where(sector % 2 == 0, pair[:, :W], pair[:, W:])
@@ -106,14 +116,20 @@
     return (own // W) * 2 + rank
 
 
-def expand(corner, slots, edges, site_t):
-    pick = one_hot(slots == iota((512, W), 0) // 8)
+def pick_matrix(slots):
+    return one_hot(slots == iota((512, W), 0) // 8)
+
+
+def kron_matrix(pick, corner):
     picked = dot(pick, corner).astype(BF)
     lane = iota((W, 512), 1)
     spread = one_hot((lane // 128) * 16 + lane % 16 == iota((W, 512), 0))
     wide_lane = iota((512, 512), 1)
     same = (wide_lane // 16) % 8 == iota((512, 512), 0) % 8
-    kron = jnp.where(same, dot(picked, spread), 0.0).astype(BF)
+    return jnp.where(same, dot(picked, spread), 0.0).astype(BF)
+
+
+def expand(kron, edges, site_t):
     expanded = dot_nt(kron, edges).astype(BF)
     return dot_nt(expanded, site_t).astype(BF)
 
@@ -141,29 +157,17 @@
     return jnp.concatenate(halves, axis=1)
 
 
-def first_rows(
-    corner_ref,
-    first_ref,
-    joining_ref,
-    lengths_ref,
-    keep_ref,
-    took_ref,
-    out_ref,
-    alive_ref,
-    *step_refs,
-):
+def first_rows(kron_ref, first_ref, keep_ref, took_ref, out_ref, *step_refs):
+    edges = gather_edges(lambda i, a, n: first_ref[i, a : a + n, :])
+    rows = expand(kron_ref[...], edges, gather_site(first_ref))
+    for t in range(SECTORS):
+        out_ref[t] = rows[t * 16 : (t + 1) * 16, :]
     chip = lax.axis_index("inner") // 2
     for step in range(4):
         to = (chip + step) % 4
         for plane, ref in enumerate((keep_ref, took_ref)):
             step_refs[step][plane] = ref[to, 0:128, :]
             step_refs[4 + step][plane] = ref[to, 128:384, :]
-    alive_ref[...] = jnp.full((8, 128), lengths_ref[0], jnp.int32)
-    sector = lax.axis_index("sector")
-    slots = send_slots(own_row(joining_ref, 0, sector))
-    rows = expand(corner_ref[0], slots, gather_edges(lambda i, a, n: first_ref[i, a : a + n, :]), gather_site(first_ref))
-    for t in range(SECTORS):
-        out_ref[t] = rows[t * 16 : (t + 1) * 16, :]
 
 
 def arrival_rows(joining_ref, move, sector):
@@ -199,17 +203,15 @@
         blocks_ref[source + 1 - core] = ref[1, start : start + 128, :]
 
 
-def project(move, incoming_ref, joining_ref, *refs):
+def project(move, incoming_ref, info_ref, *refs):
     *step_refs, out_ref, blocks_ref = refs
     by_source(step_refs, 0 if move == 0 else 128, blocks_ref)
     pieces = [blocks_ref[i, b * 16 : (b + 1) * 16, :] for b in range(8) for i in range(INNER)]
     proj = jnp.concatenate(pieces, axis=0)
-    sector = lax.axis_index("sector")
-    arrivals = arrival_rows(joining_ref, move, sector)
+    incoming = jnp.concatenate([incoming_ref[s] for s in range(SECTORS)], axis=0)
     row = iota((512, 512), 0)
-    place = one_hot((row // W == iota((512, 512), 1) % 8) & (row % W == arrivals))
-    incoming = jnp.concatenate([incoming_ref[s] for s in range(SECTORS)], axis=0)
-    placed = dot(place, incoming).astype(BF)
+    here = (row // W == iota((512, 512), 1) % 8) & (row % W == info_ref[move : move + 1, :])
+    placed = dot(one_hot(here), incoming).astype(BF)
     left = jnp.concatenate(
         [
             jnp.concatenate(
@@ -226,31 +228,29 @@
         out_ref[j] = packed
 
 
-def finished(terms, alive_ref):
+def finished(terms, info_ref):
     total = terms[0]
     for term in terms[1:]:
         total = total + term
     total = jnp.concatenate([total[:, :W], total[:, W:]], axis=0)
-    alive = alive_ref[0:1, 0:W]
+    alive = info_ref[3:4, 0:W]
     keep = (iota((W, W), 0) < alive) & (iota((W, W), 1) < alive)
     return jnp.where(keep, total, 0.0).astype(BF)
 
 
-def second_rows(terms_ref, alive_ref, first_ref, joining_ref, *refs):
+def second_rows(terms_ref, info_ref, first_ref, *refs):
     *step_refs, corner_ref, out_ref, blocks_ref = refs
     by_source(step_refs, 0, blocks_ref)
-    sector = lax.axis_index("sector")
-    terms = [terms_ref[j] for j in range(INNER)]
-    corner = finished(terms, alive_ref)
+    corner = finished([terms_ref[j] for j in range(INNER)], info_ref)
     corner_ref[0] = corner
-    slots = send_slots(own_row(joining_ref, 1, sector))
-    rows = expand(corner, slots, gather_edges(lambda i, a, n: blocks_ref[i, a : a + n, :]), gather_site(first_ref))
+    edges = gather_edges(lambda i, a, n: blocks_ref[i, a : a + n, :])
+    rows = expand(kron_matrix(pick_matrix(info_ref[2:3, 0:W]), corner), edges, gather_site(first_ref))
     for t in range(SECTORS):
         out_ref[t] = rows[t * 16 : (t + 1) * 16, :]
 
 
-def last(terms_ref, alive_ref, corner_ref):
-    corner_ref[0] = finished([terms_ref[j] for j in range(INNER)], alive_ref)
+def last(terms_ref, info_ref, corner_ref):
+    corner_ref[0] = finished([terms_ref[j] for j in range(INNER)], info_ref)
 
 
 def vmem():
@@ -306,20 +306,25 @@
         name="prep",
     )
     first = swap(first, "inner")
+    kron, info = call(
+        tables,
+        (shape((512, 512), BF), shape((8, 512), jnp.int32)),
+        corner,
+        joining,
+        lengths,
+        specs=[vmem(), vmem(), smem()],
+        name="tables",
+    )
     took = lax.ppermute(give, "inner", [(i, i ^ 1) for i in range(INNER)])
     rows_shape = shape((SECTORS, 16, KQ), BF)
     corner_shape = shape((1, W, W), BF)
-    rows, alive, *steps = call(
+    rows, *steps = call(
         first_rows,
-        (rows_shape, shape((8, 128), jnp.int32)) + (shape((2, 128, 128), BF),) * 4
-        + (shape((2, 256, 128), BF),) * 4,
-        corner,
+        (rows_shape,) + (shape((2, 128, 128), BF),) * 4 + (shape((2, 256, 128), BF),) * 4,
+        kron,
         first,
-        joining,
-        lengths,
         keep,
         took,
-        specs=[vmem(), vmem(), vmem(), smem(), vmem(), vmem()],
         name="first_rows",
     )
     rows = swap(rows, "sector")
@@ -332,7 +337,7 @@
         functools.partial(project, 0),
         terms_shape,
         rows,
-        joining,
+        info,
         *steps[:4],
         scratch=blocks,
         name="project_first",
@@ -342,9 +347,8 @@
         second_rows,
         (corner_shape, rows_shape),
         terms,
-        alive,
+        info,
         first,
-        joining,
         *steps[4:],
         scratch=blocks,
         name="second_rows",
@@ -354,13 +358,13 @@
         functools.partial(project, 1),
         terms_shape,
         rows,
-        joining,
+        info,
         *steps[4:],
         scratch=blocks,
         name="project_second",
     )
     terms = swap(terms, "inner")
-    two = call(last, corner_shape, terms, alive, name="last")
+    two = call(last, corner_shape, terms, info, name="last")
     return (one, two)
 
 

time: 84.7 us -> 83.7 us (0.988)
    pallas_call x6 -> x7, Pallas kernels: 9.13 us -> 8.79 us  [call(): pl.pallas_call(kernel, out_shape=outs, in_specs=specs or [vmem()] * len(a...]
where the time goes in v5:
time: 83.7 us; the launch traced here: 83.1 us
  starting transfers between devices  31.4 us (38%)
  blocking collectives  27 us (32%)
  waiting for transfers between devices  14.6 us (17%)
  Pallas kernels  8.79 us (11%)
  between operations  1.36 us (2%)
    all_to_all x2, blocking collectives, swap(): return lax.all_to_all(x, axis, split_axis=0, concat_axis=0, tiled=True)  27 us
    all_to_all x3, starting transfers between devices, swap(): return lax.all_to_all(x, axis, split_axis=0, concat_axis=0, tiled=True)  20.9 us
    all_to_all x3, waiting for transfers between devices, swap(): return lax.all_to_all(x, axis, split_axis=0, concat_axis=0, tiled=True)  14.5 us
    pallas_call x7, Pallas kernels, call(): pl.pallas_call(kernel, out_shape=outs, in_specs=specs or [vmem()] * len(a...  8.79 us
    ppermute x6, starting transfers between devices, body(): steps[step] = lax.ppermute(steps[step], 'inner', pairs)  7.19 us
    ppermute x1, starting transfers between devices, body(): took = lax.ppermute(give, 'inner', [(i, i ^ 1) for i in range(INNER)])  3.33 us
  transfers between devices with their start and end apart: 10, of which 3 were waited for; matrix products, arithmetic and copies ran while one was open for 0% of the time, Pallas kernels for 2%

profile of v5, /device:TPU:1, one launch (start us, length us, event | category | flops | bytes accessed | tf_op | source)
XLA Modules:
  0.0 83.1 jit_solution(14639306993887426740)
XLA Ops:
  0.6 3.5 %prep.1 = (bf16[8,192,128]{2,1,0:T(8,128)(2,1)}, bf16[4,384,128]{2,1,0:T(8,128)(2,1)}, bf16[4,384,128]{2,1,0:T(8,128)(2,1)}) custom-call(bf16[2,1,32,4096]{3,2,1,0:T(8,128)(2,1)} %edge_hbm.1, bf16[1,32,256]{2,1,0:T(8,128)(2,1)} %bitcast.1, bf16[2,1,64,2048]{3,2,1,0:T(8,128)(2,1)} %proj_hbm.1), custom_call_target="tpu_custom_call" | custom-call | tf_op jit(solution)/shard_map/prep/pallas_call | solution.py:269
  4.1 3.3 %collective-permute-start = (bf16[4,384,128]{2,1,0:T(8,128)(2,1)}, bf16[4,384,128]{2,1,0:T(8,128)(2,1)S(1)}, u32[]{:S(2)}, u32[]{:S(2)}) collective-permute-start(bf16[4,384,128]{2,1,0:T(8,128)(2,1)} %get-tuple-element.21), channel_id=1, source_target_pairs={{0,1},{1,0},{2,3},{3,2},{4,5},{5,4},{6,7},{7,6},{8,9},{9,8},{10,11... | collective-permute-start | bytes 1179656 | tf_op jit(solution)/shard_map/ppermute | solution.py:318
  7.5 3.5 %all-to-all-start = ((bf16[8,192,128]{2,1,0:T(8,128)(2,1)}), bf16[8,192,128]{2,1,0:T(8,128)(2,1)S(1)}, u32[]{:S(2)}, u32[]{:S(2)}) async-start(bf16[8,192,128]{2,1,0:T(8,128)(2,1)} %get-tuple-element.19), calls=%async_computation | async-start | bytes 786432 | tf_op jit(solution)/shard_map/all_to_all | solution.py:285
  11.6 0.0 copy-done.1
  11.7 0.0 copy-done.2
  11.7 0.6 tables.1
  12.3 6.8 %all-to-all-done.first_ref = bf16[8,192,128]{2,1,0:T(8,128)(2,1)S(1)} async-done(((bf16[8,192,128]{2,1,0:T(8,128)(2,1)}), bf16[8,192,128]{2,1,0:T(8,128)(2,1)S(1)}, u32[]{:S(2)}, u32[]{:S(2)}) %all-to-all-start) | async-done | bytes 393248 | tf_op jit(solution)/shard_map/all_to_all | solution.py:285
  19.1 0.0 collective-permute-done.took_ref
  19.1 0.0 copy-done
  19.1 1.2 %first_rows.1 = (bf16[32,16,256]{2,1,0:T(8,128)(2,1)}, bf16[2,128,128]{2,1,0:T(8,128)(2,1)S(1)}, bf16[2,128,128]{2,1,0:T(8,128)(2,1)S(1)}, bf16[2,128,128]{2,1,0...) custom-call(bf16[512,512]{1,0:T(8,128)(2,1)S(1)} %get-tuple-element., ...), custom_call_target="tpu_custom_call" | custom-call | tf_op jit(solution)/shard_map/first_rows/pallas_call | solution.py:269
  20.3 10.5 %all-to-all-start.1 = ((bf16[32,16,256]{2,1,0:T(8,128)(2,1)}), bf16[32,16,256]{2,1,0:T(8,128)(2,1)S(1)}, u32[]{:S(2)}, u32[]{:S(2)}) async-start(bf16[32,16,256]{2,1,0:T(8,128)(2,1)} %get-tuple-element.22), calls=%async_computation.1 | async-start | bytes 524288 | tf_op jit(solution)/shard_map/all_to_all | solution.py:285
  30.8 0.4 collective-permute-start.1
  31.1 1.8 %collective-permute-start.2 = (bf16[2,128,128]{2,1,0:T(8,128)(2,1)S(1)}, bf16[2,128,128]{2,1,0:T(8,128)(2,1)S(1)}, u32[]{:S(2)}, u32[]{:S(2)}) collective-permute-start(bf16[2,128,128]{2,1,0:T(8,128)(2,1)S(1)} %get-tuple-element.26), channel_id=1, source_target_pairs={{0,4},{1,5},{2,6},{3,7},{4,0},{5,1},{6,2},{7,3},{8,12},{9,13},{10,... | collective-permute-start | bytes 196616 | tf_op jit(solution)/shard_map/ppermute | solution.py:333
  32.9 0.7 collective-permute-start.3
  33.6 0.8 collective-permute-start.4
  34.4 1.5 %collective-permute-start.5 = (bf16[2,256,128]{2,1,0:T(8,128)(2,1)S(1)}, bf16[2,256,128]{2,1,0:T(8,128)(2,1)S(1)}, u32[]{:S(2)}, u32[]{:S(2)}) collective-permute-start(bf16[2,256,128]{2,1,0:T(8,128)(2,1)S(1)} %get-tuple-element.30), channel_id=1, source_target_pairs={{0,4},{1,5},{2,6},{3,7},{4,0},{5,1},{6,2},{7,3},{8,12},{9,13},{10,... | collective-permute-start | bytes 393224 | tf_op jit(solution)/shard_map/ppermute | solution.py:333
  35.9 0.0 collective-permute-done.1.refs_1_
  35.9 2.1 %collective-permute-start.6 = (bf16[2,256,128]{2,1,0:T(8,128)(2,1)S(1)}, bf16[2,256,128]{2,1,0:T(8,128)(2,1)S(1)}, u32[]{:S(2)}, u32[]{:S(2)}) collective-permute-start(bf16[2,256,128]{2,1,0:T(8,128)(2,1)S(1)} %get-tuple-element.31), channel_id=1, source_target_pairs={{0,6},{1,7},{2,0},{3,1},{4,2},{5,3},{6,4},{7,5},{8,14},{9,15},{10,... | collective-permute-start | bytes 393224 | tf_op jit(solution)/shard_map/ppermute | solution.py:333
  38.0 0.0 collective-permute-done.2.refs_2_
  38.0 0.0 collective-permute-done.3.refs_3_
  38.0 2.5 %all-to-all-done.1.incoming_ref = bf16[32,16,256]{2,1,0:T(8,128)(2,1)S(1)} async-done(((bf16[32,16,256]{2,1,0:T(8,128)(2,1)}), bf16[32,16,256]{2,1,0:T(8,128)(2,1)S(1)}, u32[]{:S(2)}, u32[]{:S(2)}) %all-to-all-start.1) | async-done | bytes 262176 | tf_op jit(solution)/shard_map/all_to_all | solution.py:285
  40.5 1.3 %project_first.1 = f32[8,32,128]{2,1,0:T(8,128)} custom-call(bf16[32,16,256]{2,1,0:T(8,128)(2,1)S(1)} %all-to-all-done.1.incoming_ref, s32[8,512]{1,0:T(8,128)S(1)} %get-tuple-element.23.info_ref, bf16[2,128,128]{2,1,0:T(8,128)(2,1)S(1)} %get-tuple-element.24.refs_0_, bf16[2,128,128]{2,1,0:T(8,128)(2,1)S(1)} %collective-permute-done.1.refs_1_, ...), custom_call_target="tpu_custom_call" | custom-call | tf_op jit(solution)/shard_map/project_first/pallas_call | solution.py:269
  41.8 6.9 %all-to-all-start.2 = ((f32[8,32,128]{2,1,0:T(8,128)}), f32[8,32,128]{2,1,0:T(8,128)S(1)}, u32[]{:S(2)}, u32[]{:S(2)}) async-start(f32[8,32,128]{2,1,0:T(8,128)} %project_first.1), calls=%async_computation.2 | async-start | bytes 262144 | tf_op jit(solution)/shard_map/all_to_all | solution.py:285
  48.7 0.0 collective-permute-done.4.refs_1_
  48.7 0.0 collective-permute-done.5.refs_2_
  48.7 0.0 collective-permute-done.6.refs_3_
  48.7 5.3 %all-to-all-done.2.terms_ref = f32[8,32,128]{2,1,0:T(8,128)S(1)} async-done(((f32[8,32,128]{2,1,0:T(8,128)}), f32[8,32,128]{2,1,0:T(8,128)S(1)}, u32[]{:S(2)}, u32[]{:S(2)}) %all-to-all-start.2) | async-done | bytes 131104 | tf_op jit(solution)/shard_map/all_to_all | solution.py:285
  54.0 0.8 %second_rows.1 = (bf16[1,64,64]{2,1,0:T(8,128)(2,1)}, bf16[32,16,256]{2,1,0:T(8,128)(2,1)S(1)}) custom-call(f32[8,32,128]{2,1,0:T(8,128)S(1)} %all-to-all-done.2.terms_ref, s32[8,512]{1,0:T(8,128)S(1)} %get-tuple-element.23.info_ref, bf16[8,192,128]{2,1,0:T(8,128)(2,1)S(1)} %all-to-all-done.first_ref, bf16[2,256,128]{2,1,0:T(8,128)(2,1)S(1)} %get-tuple-element.28.refs_0_, ...), custom_call_target="tpu_custom_call" | custom-call | tf_op jit(solution)/shard_map/second_rows/pallas_call | solution.py:269
  54.8 15.7 %all_to_all.25.incoming_ref = bf16[32,16,256]{2,1,0:T(8,128)(2,1)S(1)} all-to-all(bf16[32,16,256]{2,1,0:T(8,128)(2,1)S(1)} %get-tuple-element.33), channel_id=1, replica_groups=mesh['sector'=32,'inner'=8] {'sector'}, dimensions={0} | all-to-all | bytes 524288 | tf_op jit(solution)/shard_map/all_to_all | solution.py:285
  70.5 0.6 project_second.1
  71.2 11.3 %all_to_all.26.terms_ref = f32[8,32,128]{2,1,0:T(8,128)S(1)} all-to-all(f32[8,32,128]{2,1,0:T(8,128)S(1)} %project_second.1), channel_id=1, replica_groups=mesh['sector'=32,'inner'=8] {'inner'}, dimensions={0} | all-to-all | bytes 262144 | tf_op jit(solution)/shard_map/all_to_all | solution.py:285
  82.5 0.7 last.1
  (3 shorter events, 0.0 us)
Async XLA Ops:
  4.1 15.0 %collective-permute-start = (bf16[4,384,128]{2,1,0:T(8,128)(2,1)}, bf16[4,384,128]{2,1,0:T(8,128)(2,1)S(1)}, u32[]{:S(2)}, u32[]{:S(2)}) collective-permute-start(bf16[4,384,128]{2,1,0:T(8,128)(2,1)} %get-tuple-element.21), channel_id=1, source_target_pairs={{0,1},{1,0},{2,3},{3,2},{4,5},{5,4},{6,7},{7,6},{8,9},{9,8},{10,11... | collective-permute-start | bytes 1179656 | tf_op jit(solution)/shard_map/ppermute | solution.py:318
  7.4 4.2 %copy-start.1 = (bf16[1,64,64]{2,1,0:T(8,128)(2,1)S(1)}, bf16[1,64,64]{2,1,0:T(8,128)(2,1)}, u32[]{:S(2)}) copy-start(bf16[1,64,64]{2,1,0:T(8,128)(2,1)} %corner_ref.1) | copy-start | bytes 24580
  7.5 4.2 %copy-start.2 = (s32[2,2048]{1,0:T(2,128)S(1)}, s32[2,2048]{1,0:T(2,128)}, u32[]{:S(2)}) copy-start(s32[2,2048]{1,0:T(2,128)} %joining_ref.1) | copy-start | bytes 49156
  7.5 11.6 %copy-start = (bf16[4,384,128]{2,1,0:T(8,128)(2,1)S(1)}, bf16[4,384,128]{2,1,0:T(8,128)(2,1)}, u32[]{:S(2)}) copy-start(bf16[4,384,128]{2,1,0:T(8,128)(2,1)} %get-tuple-element.20.keep_ref) | copy-start | bytes 1179652
  7.5 11.6 %all-to-all-start = ((bf16[8,192,128]{2,1,0:T(8,128)(2,1)}), bf16[8,192,128]{2,1,0:T(8,128)(2,1)S(1)}, u32[]{:S(2)}, u32[]{:S(2)}) async-start(bf16[8,192,128]{2,1,0:T(8,128)(2,1)} %get-tuple-element.19), calls=%async_computation | async-start | bytes 786432 | tf_op jit(solution)/shard_map/all_to_all | solution.py:285
  20.3 20.2 %all-to-all-start.1 = ((bf16[32,16,256]{2,1,0:T(8,128)(2,1)}), bf16[32,16,256]{2,1,0:T(8,128)(2,1)S(1)}, u32[]{:S(2)}, u32[]{:S(2)}) async-start(bf16[32,16,256]{2,1,0:T(8,128)(2,1)} %get-tuple-element.22), calls=%async_computation.1 | async-start | bytes 524288 | tf_op jit(solution)/shard_map/all_to_all | solution.py:285
  30.8 5.1 %collective-permute-start.1 = (bf16[2,128,128]{2,1,0:T(8,128)(2,1)S(1)}, bf16[2,128,128]{2,1,0:T(8,128)(2,1)S(1)}, u32[]{:S(2)}, u32[]{:S(2)}) collective-permute-start(bf16[2,128,128]{2,1,0:T(8,128)(2,1)S(1)} %get-tuple-element.25), channel_id=1, source_target_pairs={{0,2},{1,3},{2,4},{3,5},{4,6},{5,7},{6,0},{7,1},{8,10},{9,11},{10,... | collective-permute-start | bytes 196616 | tf_op jit(solution)/shard_map/ppermute | solution.py:333
  31.1 6.8 %collective-permute-start.2 = (bf16[2,128,128]{2,1,0:T(8,128)(2,1)S(1)}, bf16[2,128,128]{2,1,0:T(8,128)(2,1)S(1)}, u32[]{:S(2)}, u32[]{:S(2)}) collective-permute-start(bf16[2,128,128]{2,1,0:T(8,128)(2,1)S(1)} %get-tuple-element.26), channel_id=1, source_target_pairs={{0,4},{1,5},{2,6},{3,7},{4,0},{5,1},{6,2},{7,3},{8,12},{9,13},{10,... | collective-permute-start | bytes 196616 | tf_op jit(solution)/shard_map/ppermute | solution.py:333
  32.9 5.1 %collective-permute-start.3 = (bf16[2,128,128]{2,1,0:T(8,128)(2,1)S(1)}, bf16[2,128,128]{2,1,0:T(8,128)(2,1)S(1)}, u32[]{:S(2)}, u32[]{:S(2)}) collective-permute-start(bf16[2,128,128]{2,1,0:T(8,128)(2,1)S(1)} %get-tuple-element.27), channel_id=1, source_target_pairs={{0,6},{1,7},{2,0},{3,1},{4,2},{5,3},{6,4},{7,5},{8,14},{9,15},{10,... | collective-permute-start | bytes 196616 | tf_op jit(solution)/shard_map/ppermute | solution.py:333
  33.6 15.0 %collective-permute-start.4 = (bf16[2,256,128]{2,1,0:T(8,128)(2,1)S(1)}, bf16[2,256,128]{2,1,0:T(8,128)(2,1)S(1)}, u32[]{:S(2)}, u32[]{:S(2)}) collective-permute-start(bf16[2,256,128]{2,1,0:T(8,128)(2,1)S(1)} %get-tuple-element.29), channel_id=1, source_target_pairs={{0,2},{1,3},{2,4},{3,5},{4,6},{5,7},{6,0},{7,1},{8,10},{9,11},{10,... | collective-permute-start | bytes 393224 | tf_op jit(solution)/shard_map/ppermute | solution.py:333
  34.4 14.3 %collective-permute-start.5 = (bf16[2,256,128]{2,1,0:T(8,128)(2,1)S(1)}, bf16[2,256,128]{2,1,0:T(8,128)(2,1)S(1)}, u32[]{:S(2)}, u32[]{:S(2)}) collective-permute-start(bf16[2,256,128]{2,1,0:T(8,128)(2,1)S(1)} %get-tuple-element.30), channel_id=1, source_target_pairs={{0,4},{1,5},{2,6},{3,7},{4,0},{5,1},{6,2},{7,3},{8,12},{9,13},{10,... | collective-permute-start | bytes 393224 | tf_op jit(solution)/shard_map/ppermute | solution.py:333
  35.9 12.8 %collective-permute-start.6 = (bf16[2,256,128]{2,1,0:T(8,128)(2,1)S(1)}, bf16[2,256,128]{2,1,0:T(8,128)(2,1)S(1)}, u32[]{:S(2)}, u32[]{:S(2)}) collective-permute-start(bf16[2,256,128]{2,1,0:T(8,128)(2,1)S(1)} %get-tuple-element.31), channel_id=1, source_target_pairs={{0,6},{1,7},{2,0},{3,1},{4,2},{5,3},{6,4},{7,5},{8,14},{9,15},{10,... | collective-permute-start | bytes 393224 | tf_op jit(solution)/shard_map/ppermute | solution.py:333
  41.8 12.2 %all-to-all-start.2 = ((f32[8,32,128]{2,1,0:T(8,128)}), f32[8,32,128]{2,1,0:T(8,128)S(1)}, u32[]{:S(2)}, u32[]{:S(2)}) async-start(f32[8,32,128]{2,1,0:T(8,128)} %project_first.1), calls=%async_computation.2 | async-start | bytes 262144 | tf_op jit(solution)/shard_map/all_to_all | solution.py:285

commit v6 on v5

--- a/solution.py
+++ b/solution.py
@@ -32,9 +32,9 @@
 
 
 def shuffle_matrix():
-    row = iota((1024, 1), 0)
-    want = (row % 16) * 64 + (row // 128) * 8 + (row // 16) % 8
-    return one_hot(iota((1024, 1024), 1) == want)
+    row = iota((512, 1), 0)
+    want = (row % 8) * 64 + (row // 64) * 8 + (row // 8) % 8
+    return one_hot(iota((512, 512), 1) == want)
 
 
 def prep(
@@ -62,13 +62,19 @@
     copies[0].wait()
     copies[2].wait()
     stacked = jnp.concatenate(
-        [edge_ref[m, 0, :, n * 1024 : (n + 1) * 1024] for m in range(2) for n in range(4)], axis=0
-    )
-    blocks = dot_nt(stacked, shuffle).astype(BF)
+        [edge_ref[m, 0, :, n * 512 : (n + 1) * 512] for m in range(2) for n in range(8)], axis=0
+    )
+    blocks = dot_nt(stacked, shuffle)
     site_t = site_ref[0]
     for j in range(INNER):
-        first_ref[j, 0:128, :] = blocks[0:128, j * 128 : (j + 1) * 128]
-        rest_ref[j // 2, j % 2, 128:256, :] = blocks[128:256, j * 128 : (j + 1) * 128]
+        lanes = slice(j * W, (j + 1) * W)
+        tiles = []
+        for n in range(8):
+            low = blocks[n * 64 : n * 64 + 32, lanes]
+            high = blocks[n * 64 + 32 : n * 64 + 64, lanes]
+            tiles.append(jnp.concatenate([low, high], axis=1))
+        first_ref[j, 0:128, :] = jnp.concatenate(tiles[:4], axis=0).astype(BF)
+        rest_ref[j // 2, j % 2, 128:256, :] = jnp.concatenate(tiles[4:], axis=0).astype(BF)
         first_ref[j, 128:160, :] = site_t[:, 0:128]
         first_ref[j, 160:192, :] = site_t[:, 128:256]
     outs = [
@@ -82,7 +88,10 @@
     stacked = jnp.concatenate(
         [proj_ref[m, 0, :, n * 1024 : (n + 1) * 1024] for m in range(2) for n in range(2)], axis=0
     )
-    rows = dot_nt(shuffle, stacked).astype(BF)
+    halves = [
+        dot_nt(shuffle, stacked[:, n * 512 : (n + 1) * 512]).reshape(W, 8, 256) for n in range(2)
+    ]
+    rows = jnp.concatenate(halves, axis=1).reshape(1024, 256).astype(BF)
     for j in range(INNER):
         rest_ref[j // 2, j % 2, 0:128, :] = rows[j * 128 : (j + 1) * 128, 0:128]
         rest_ref[j // 2, j % 2, 256:384, :] = rows[j * 128 : (j + 1) * 128, 128:256]
@@ -123,9 +132,9 @@
 def kron_matrix(pick, corner):
     picked = dot(pick, corner).astype(BF)
     lane = iota((W, 512), 1)
-    spread = one_hot((lane // 128) * 16 + lane % 16 == iota((W, 512), 0))
+    spread = one_hot((lane // 64) * 8 + lane % 8 == iota((W, 512), 0))
     wide_lane = iota((512, 512), 1)
-    same = (wide_lane // 16) % 8 == iota((512, 512), 0) % 8
+    same = (wide_lane // 8) % 8 == iota((512, 512), 0) % 8
     return jnp.where(same, dot(picked, spread), 0.0).astype(BF)
 
 

time: 83.7 us -> 83.2 us (level)
  no operation moved by 1% of the time
where the time goes in v6:
time: 83.2 us; the launch traced here: 82.7 us
  starting transfers between devices  31.4 us (38%)
  blocking collectives  27 us (32%)
  waiting for transfers between devices  14.6 us (18%)
  Pallas kernels  8.34 us (10%)
  between operations  1.36 us (2%)
    all_to_all x2, blocking collectives, swap(): return lax.all_to_all(x, axis, split_axis=0, concat_axis=0, tiled=True)  27 us
    all_to_all x3, starting transfers between devices, swap(): return lax.all_to_all(x, axis, split_axis=0, concat_axis=0, tiled=True)  20.9 us
    all_to_all x3, waiting for transfers between devices, swap(): return lax.all_to_all(x, axis, split_axis=0, concat_axis=0, tiled=True)  14.5 us
    pallas_call x7, Pallas kernels, call(): pl.pallas_call(kernel, out_shape=outs, in_specs=specs or [vmem()] * len(a...  8.34 us
    ppermute x6, starting transfers between devices, body(): steps[step] = lax.ppermute(steps[step], 'inner', pairs)  7.19 us
    ppermute x1, starting transfers between devices, body(): took = lax.ppermute(give, 'inner', [(i, i ^ 1) for i in range(INNER)])  3.33 us
  transfers between devices with their start and end apart: 10, of which 3 were waited for; matrix products, arithmetic and copies ran while one was open for 0% of the time, Pallas kernels for 2%

profile of v6, /device:TPU:1, one launch (start us, length us, event | category | flops | bytes accessed | tf_op | source)
XLA Modules:
  0.0 82.7 jit_solution(12942975553174565466)
XLA Ops:
  0.6 3.0 %prep.1 = (bf16[8,192,128]{2,1,0:T(8,128)(2,1)}, bf16[4,384,128]{2,1,0:T(8,128)(2,1)}, bf16[4,384,128]{2,1,0:T(8,128)(2,1)}) custom-call(bf16[2,1,32,4096]{3,2,1,0:T(8,128)(2,1)} %edge_hbm.1, bf16[1,32,256]{2,1,0:T(8,128)(2,1)} %bitcast.1, bf16[2,1,64,2048]{3,2,1,0:T(8,128)(2,1)} %proj_hbm.1), custom_call_target="tpu_custom_call" | custom-call | tf_op jit(solution)/shard_map/prep/pallas_call | solution.py:278
  3.7 3.3 %collective-permute-start = (bf16[4,384,128]{2,1,0:T(8,128)(2,1)}, bf16[4,384,128]{2,1,0:T(8,128)(2,1)S(1)}, u32[]{:S(2)}, u32[]{:S(2)}) collective-permute-start(bf16[4,384,128]{2,1,0:T(8,128)(2,1)} %get-tuple-element.21), channel_id=1, source_target_pairs={{0,1},{1,0},{2,3},{3,2},{4,5},{5,4},{6,7},{7,6},{8,9},{9,8},{10,11... | collective-permute-start | bytes 1179656 | tf_op jit(solution)/shard_map/ppermute | solution.py:327
  7.0 3.5 %all-to-all-start = ((bf16[8,192,128]{2,1,0:T(8,128)(2,1)}), bf16[8,192,128]{2,1,0:T(8,128)(2,1)S(1)}, u32[]{:S(2)}, u32[]{:S(2)}) async-start(bf16[8,192,128]{2,1,0:T(8,128)(2,1)} %get-tuple-element.19), calls=%async_computation | async-start | bytes 786432 | tf_op jit(solution)/shard_map/all_to_all | solution.py:294
  11.2 0.0 copy-done.1
  11.2 0.0 copy-done.2
  11.2 0.6 tables.1
  11.9 6.8 %all-to-all-done.first_ref = bf16[8,192,128]{2,1,0:T(8,128)(2,1)S(1)} async-done(((bf16[8,192,128]{2,1,0:T(8,128)(2,1)}), bf16[8,192,128]{2,1,0:T(8,128)(2,1)S(1)}, u32[]{:S(2)}, u32[]{:S(2)}) %all-to-all-start) | async-done | bytes 393248 | tf_op jit(solution)/shard_map/all_to_all | solution.py:294
  18.6 0.0 collective-permute-done.took_ref
  18.6 0.0 copy-done
  18.6 1.2 %first_rows.1 = (bf16[32,16,256]{2,1,0:T(8,128)(2,1)}, bf16[2,128,128]{2,1,0:T(8,128)(2,1)S(1)}, bf16[2,128,128]{2,1,0:T(8,128)(2,1)S(1)}, bf16[2,128,128]{2,1,0...) custom-call(bf16[512,512]{1,0:T(8,128)(2,1)S(1)} %get-tuple-element., ...), custom_call_target="tpu_custom_call" | custom-call | tf_op jit(solution)/shard_map/first_rows/pallas_call | solution.py:278
  19.9 10.4 %all-to-all-start.1 = ((bf16[32,16,256]{2,1,0:T(8,128)(2,1)}), bf16[32,16,256]{2,1,0:T(8,128)(2,1)S(1)}, u32[]{:S(2)}, u32[]{:S(2)}) async-start(bf16[32,16,256]{2,1,0:T(8,128)(2,1)} %get-tuple-element.22), calls=%async_computation.1 | async-start | bytes 524288 | tf_op jit(solution)/shard_map/all_to_all | solution.py:294
  30.3 0.4 collective-permute-start.1
  30.7 1.8 %collective-permute-start.2 = (bf16[2,128,128]{2,1,0:T(8,128)(2,1)S(1)}, bf16[2,128,128]{2,1,0:T(8,128)(2,1)S(1)}, u32[]{:S(2)}, u32[]{:S(2)}) collective-permute-start(bf16[2,128,128]{2,1,0:T(8,128)(2,1)S(1)} %get-tuple-element.26), channel_id=1, source_target_pairs={{0,4},{1,5},{2,6},{3,7},{4,0},{5,1},{6,2},{7,3},{8,12},{9,13},{10,... | collective-permute-start | bytes 196616 | tf_op jit(solution)/shard_map/ppermute | solution.py:342
  32.5 0.7 collective-permute-start.3
  33.2 0.8 collective-permute-start.4
  33.9 1.5 %collective-permute-start.5 = (bf16[2,256,128]{2,1,0:T(8,128)(2,1)S(1)}, bf16[2,256,128]{2,1,0:T(8,128)(2,1)S(1)}, u32[]{:S(2)}, u32[]{:S(2)}) collective-permute-start(bf16[2,256,128]{2,1,0:T(8,128)(2,1)S(1)} %get-tuple-element.30), channel_id=1, source_target_pairs={{0,4},{1,5},{2,6},{3,7},{4,0},{5,1},{6,2},{7,3},{8,12},{9,13},{10,... | collective-permute-start | bytes 393224 | tf_op jit(solution)/shard_map/ppermute | solution.py:342
  35.4 0.0 collective-permute-done.1.refs_1_
  35.4 2.1 %collective-permute-start.6 = (bf16[2,256,128]{2,1,0:T(8,128)(2,1)S(1)}, bf16[2,256,128]{2,1,0:T(8,128)(2,1)S(1)}, u32[]{:S(2)}, u32[]{:S(2)}) collective-permute-start(bf16[2,256,128]{2,1,0:T(8,128)(2,1)S(1)} %get-tuple-element.31), channel_id=1, source_target_pairs={{0,6},{1,7},{2,0},{3,1},{4,2},{5,3},{6,4},{7,5},{8,14},{9,15},{10,... | collective-permute-start | bytes 393224 | tf_op jit(solution)/shard_map/ppermute | solution.py:342
  37.5 0.0 collective-permute-done.2.refs_2_
  37.5 0.0 collective-permute-done.3.refs_3_
  37.5 2.5 %all-to-all-done.1.incoming_ref = bf16[32,16,256]{2,1,0:T(8,128)(2,1)S(1)} async-done(((bf16[32,16,256]{2,1,0:T(8,128)(2,1)}), bf16[32,16,256]{2,1,0:T(8,128)(2,1)S(1)}, u32[]{:S(2)}, u32[]{:S(2)}) %all-to-all-start.1) | async-done | bytes 262176 | tf_op jit(solution)/shard_map/all_to_all | solution.py:294
  40.0 1.3 %project_first.1 = f32[8,32,128]{2,1,0:T(8,128)} custom-call(bf16[32,16,256]{2,1,0:T(8,128)(2,1)S(1)} %all-to-all-done.1.incoming_ref, s32[8,512]{1,0:T(8,128)S(1)} %get-tuple-element.23.info_ref, bf16[2,128,128]{2,1,0:T(8,128)(2,1)S(1)} %get-tuple-element.24.refs_0_, bf16[2,128,128]{2,1,0:T(8,128)(2,1)S(1)} %collective-permute-done.1.refs_1_, ...), custom_call_target="tpu_custom_call" | custom-call | tf_op jit(solution)/shard_map/project_first/pallas_call | solution.py:278
  41.3 6.9 %all-to-all-start.2 = ((f32[8,32,128]{2,1,0:T(8,128)}), f32[8,32,128]{2,1,0:T(8,128)S(1)}, u32[]{:S(2)}, u32[]{:S(2)}) async-start(f32[8,32,128]{2,1,0:T(8,128)} %project_first.1), calls=%async_computation.2 | async-start | bytes 262144 | tf_op jit(solution)/shard_map/all_to_all | solution.py:294
  48.2 0.0 collective-permute-done.4.refs_1_
  48.2 0.0 collective-permute-done.5.refs_2_
  48.2 0.0 collective-permute-done.6.refs_3_
  48.2 5.3 %all-to-all-done.2.terms_ref = f32[8,32,128]{2,1,0:T(8,128)S(1)} async-done(((f32[8,32,128]{2,1,0:T(8,128)}), f32[8,32,128]{2,1,0:T(8,128)S(1)}, u32[]{:S(2)}, u32[]{:S(2)}) %all-to-all-start.2) | async-done | bytes 131104 | tf_op jit(solution)/shard_map/all_to_all | solution.py:294
  53.5 0.8 %second_rows.1 = (bf16[1,64,64]{2,1,0:T(8,128)(2,1)}, bf16[32,16,256]{2,1,0:T(8,128)(2,1)S(1)}) custom-call(f32[8,32,128]{2,1,0:T(8,128)S(1)} %all-to-all-done.2.terms_ref, s32[8,512]{1,0:T(8,128)S(1)} %get-tuple-element.23.info_ref, bf16[8,192,128]{2,1,0:T(8,128)(2,1)S(1)} %all-to-all-done.first_ref, bf16[2,256,128]{2,1,0:T(8,128)(2,1)S(1)} %get-tuple-element.28.refs_0_, ...), custom_call_target="tpu_custom_call" | custom-call | tf_op jit(solution)/shard_map/second_rows/pallas_call | solution.py:278
  54.3 15.7 %all_to_all.25.incoming_ref = bf16[32,16,256]{2,1,0:T(8,128)(2,1)S(1)} all-to-all(bf16[32,16,256]{2,1,0:T(8,128)(2,1)S(1)} %get-tuple-element.33), channel_id=1, replica_groups=mesh['sector'=32,'inner'=8] {'sector'}, dimensions={0} | all-to-all | bytes 524288 | tf_op jit(solution)/shard_map/all_to_all | solution.py:294
  70.1 0.6 project_second.1
  70.7 11.3 %all_to_all.26.terms_ref = f32[8,32,128]{2,1,0:T(8,128)S(1)} all-to-all(f32[8,32,128]{2,1,0:T(8,128)S(1)} %project_second.1), channel_id=1, replica_groups=mesh['sector'=32,'inner'=8] {'inner'}, dimensions={0} | all-to-all | bytes 262144 | tf_op jit(solution)/shard_map/all_to_all | solution.py:294
  82.0 0.7 last.1
  (3 shorter events, 0.0 us)
Async XLA Ops:
  3.7 15.0 %collective-permute-start = (bf16[4,384,128]{2,1,0:T(8,128)(2,1)}, bf16[4,384,128]{2,1,0:T(8,128)(2,1)S(1)}, u32[]{:S(2)}, u32[]{:S(2)}) collective-permute-start(bf16[4,384,128]{2,1,0:T(8,128)(2,1)} %get-tuple-element.21), channel_id=1, source_target_pairs={{0,1},{1,0},{2,3},{3,2},{4,5},{5,4},{6,7},{7,6},{8,9},{9,8},{10,11... | collective-permute-start | bytes 1179656 | tf_op jit(solution)/shard_map/ppermute | solution.py:327
  7.0 4.2 %copy-start.1 = (bf16[1,64,64]{2,1,0:T(8,128)(2,1)S(1)}, bf16[1,64,64]{2,1,0:T(8,128)(2,1)}, u32[]{:S(2)}) copy-start(bf16[1,64,64]{2,1,0:T(8,128)(2,1)} %corner_ref.1) | copy-start | bytes 24580
  7.0 4.2 %copy-start.2 = (s32[2,2048]{1,0:T(2,128)S(1)}, s32[2,2048]{1,0:T(2,128)}, u32[]{:S(2)}) copy-start(s32[2,2048]{1,0:T(2,128)} %joining_ref.1) | copy-start | bytes 49156
  7.0 11.6 %copy-start = (bf16[4,384,128]{2,1,0:T(8,128)(2,1)S(1)}, bf16[4,384,128]{2,1,0:T(8,128)(2,1)}, u32[]{:S(2)}) copy-start(bf16[4,384,128]{2,1,0:T(8,128)(2,1)} %get-tuple-element.20.keep_ref) | copy-start | bytes 1179652
  7.0 11.6 %all-to-all-start = ((bf16[8,192,128]{2,1,0:T(8,128)(2,1)}), bf16[8,192,128]{2,1,0:T(8,128)(2,1)S(1)}, u32[]{:S(2)}, u32[]{:S(2)}) async-start(bf16[8,192,128]{2,1,0:T(8,128)(2,1)} %get-tuple-element.19), calls=%async_computation | async-start | bytes 786432 | tf_op jit(solution)/shard_map/all_to_all | solution.py:294
  19.9 20.1 %all-to-all-start.1 = ((bf16[32,16,256]{2,1,0:T(8,128)(2,1)}), bf16[32,16,256]{2,1,0:T(8,128)(2,1)S(1)}, u32[]{:S(2)}, u32[]{:S(2)}) async-start(bf16[32,16,256]{2,1,0:T(8,128)(2,1)} %get-tuple-element.22), calls=%async_computation.1 | async-start | bytes 524288 | tf_op jit(solution)/shard_map/all_to_all | solution.py:294
  30.3 5.1 %collective-permute-start.1 = (bf16[2,128,128]{2,1,0:T(8,128)(2,1)S(1)}, bf16[2,128,128]{2,1,0:T(8,128)(2,1)S(1)}, u32[]{:S(2)}, u32[]{:S(2)}) collective-permute-start(bf16[2,128,128]{2,1,0:T(8,128)(2,1)S(1)} %get-tuple-element.25), channel_id=1, source_target_pairs={{0,2},{1,3},{2,4},{3,5},{4,6},{5,7},{6,0},{7,1},{8,10},{9,11},{10,... | collective-permute-start | bytes 196616 | tf_op jit(solution)/shard_map/ppermute | solution.py:342
  30.7 6.8 %collective-permute-start.2 = (bf16[2,128,128]{2,1,0:T(8,128)(2,1)S(1)}, bf16[2,128,128]{2,1,0:T(8,128)(2,1)S(1)}, u32[]{:S(2)}, u32[]{:S(2)}) collective-permute-start(bf16[2,128,128]{2,1,0:T(8,128)(2,1)S(1)} %get-tuple-element.26), channel_id=1, source_target_pairs={{0,4},{1,5},{2,6},{3,7},{4,0},{5,1},{6,2},{7,3},{8,12},{9,13},{10,... | collective-permute-start | bytes 196616 | tf_op jit(solution)/shard_map/ppermute | solution.py:342
  32.5 5.1 %collective-permute-start.3 = (bf16[2,128,128]{2,1,0:T(8,128)(2,1)S(1)}, bf16[2,128,128]{2,1,0:T(8,128)(2,1)S(1)}, u32[]{:S(2)}, u32[]{:S(2)}) collective-permute-start(bf16[2,128,128]{2,1,0:T(8,128)(2,1)S(1)} %get-tuple-element.27), channel_id=1, source_target_pairs={{0,6},{1,7},{2,0},{3,1},{4,2},{5,3},{6,4},{7,5},{8,14},{9,15},{10,... | collective-permute-start | bytes 196616 | tf_op jit(solution)/shard_map/ppermute | solution.py:342
  33.2 15.0 %collective-permute-start.4 = (bf16[2,256,128]{2,1,0:T(8,128)(2,1)S(1)}, bf16[2,256,128]{2,1,0:T(8,128)(2,1)S(1)}, u32[]{:S(2)}, u32[]{:S(2)}) collective-permute-start(bf16[2,256,128]{2,1,0:T(8,128)(2,1)S(1)} %get-tuple-element.29), channel_id=1, source_target_pairs={{0,2},{1,3},{2,4},{3,5},{4,6},{5,7},{6,0},{7,1},{8,10},{9,11},{10,... | collective-permute-start | bytes 393224 | tf_op jit(solution)/shard_map/ppermute | solution.py:342
  33.9 14.3 %collective-permute-start.5 = (bf16[2,256,128]{2,1,0:T(8,128)(2,1)S(1)}, bf16[2,256,128]{2,1,0:T(8,128)(2,1)S(1)}, u32[]{:S(2)}, u32[]{:S(2)}) collective-permute-start(bf16[2,256,128]{2,1,0:T(8,128)(2,1)S(1)} %get-tuple-element.30), channel_id=1, source_target_pairs={{0,4},{1,5},{2,6},{3,7},{4,0},{5,1},{6,2},{7,3},{8,12},{9,13},{10,... | collective-permute-start | bytes 393224 | tf_op jit(solution)/shard_map/ppermute | solution.py:342
  35.4 12.8 %collective-permute-start.6 = (bf16[2,256,128]{2,1,0:T(8,128)(2,1)S(1)}, bf16[2,256,128]{2,1,0:T(8,128)(2,1)S(1)}, u32[]{:S(2)}, u32[]{:S(2)}) collective-permute-start(bf16[2,256,128]{2,1,0:T(8,128)(2,1)S(1)} %get-tuple-element.31), channel_id=1, source_target_pairs={{0,6},{1,7},{2,0},{3,1},{4,2},{5,3},{6,4},{7,5},{8,14},{9,15},{10,... | collective-permute-start | bytes 393224 | tf_op jit(solution)/shard_map/ppermute | solution.py:342
  41.3 12.2 %all-to-all-start.2 = ((f32[8,32,128]{2,1,0:T(8,128)}), f32[8,32,128]{2,1,0:T(8,128)S(1)}, u32[]{:S(2)}, u32[]{:S(2)}) async-start(f32[8,32,128]{2,1,0:T(8,128)} %project_first.1), calls=%async_computation.2 | async-start | bytes 262144 | tf_op jit(solution)/shard_map/all_to_all | solution.py:294

commit v7 on v6

--- a/solution.py
+++ b/solution.py
@@ -37,54 +37,44 @@
     return one_hot(iota((512, 512), 1) == want)
 
 
-def prep(
-    edge_hbm,
-    site_hbm,
-    proj_hbm,
-    first_hbm,
-    keep_hbm,
-    give_hbm,
-    edge_ref,
-    site_ref,
-    proj_ref,
-    first_ref,
-    rest_ref,
-    sems,
-):
+def lane_tiles(blocks, j):
+    lanes = slice(j * W, (j + 1) * W)
+    tiles = []
+    for n in range(4):
+        low = blocks[n * 64 : n * 64 + 32, lanes]
+        high = blocks[n * 64 + 32 : n * 64 + 64, lanes]
+        tiles.append(jnp.concatenate([low, high], axis=1))
+    return jnp.concatenate(tiles, axis=0).astype(BF)
+
+
+def prep_first(edge_hbm, site_hbm, first_hbm, edge_ref, site_ref, first_ref, sems):
     copies = [
-        pltpu.make_async_copy(edge_hbm, edge_ref, sems.at[0]),
-        pltpu.make_async_copy(proj_hbm, proj_ref, sems.at[1]),
-        pltpu.make_async_copy(site_hbm, site_ref, sems.at[2]),
+        pltpu.make_async_copy(edge_hbm.at[0, 0], edge_ref, sems.at[0]),
+        pltpu.make_async_copy(site_hbm.at[0], site_ref, sems.at[1]),
     ]
     for copy in copies:
         copy.start()
     shuffle = shuffle_matrix()
-    copies[0].wait()
-    copies[2].wait()
+    for copy in copies:
+        copy.wait()
+    stacked = jnp.concatenate([edge_ref[:, n * 512 : (n + 1) * 512] for n in range(8)], axis=0)
+    blocks = dot_nt(stacked, shuffle)
+    for j in range(INNER):
+        first_ref[j, 0:128, :] = lane_tiles(blocks, j)
+        first_ref[j, 128:160, :] = site_ref[:, 0:128]
+        first_ref[j, 160:192, :] = site_ref[:, 128:256]
+    copy = pltpu.make_async_copy(first_ref, first_hbm, sems.at[2])
+    copy.start()
+    copy.wait()
+
+
+def prep_rest(edge_ref, proj_ref, keep_ref, give_ref, give_rest_ref):
+    core = lax.axis_index("inner") % 2
+    shuffle = shuffle_matrix()
     stacked = jnp.concatenate(
-        [edge_ref[m, 0, :, n * 512 : (n + 1) * 512] for m in range(2) for n in range(8)], axis=0
+        [edge_ref[1, 0, :, n * 512 : (n + 1) * 512] for n in range(8)], axis=0
     )
     blocks = dot_nt(stacked, shuffle)
-    site_t = site_ref[0]
-    for j in range(INNER):
-        lanes = slice(j * W, (j + 1) * W)
-        tiles = []
-        for n in range(8):
-            low = blocks[n * 64 : n * 64 + 32, lanes]
-            high = blocks[n * 64 + 32 : n * 64 + 64, lanes]
-            tiles.append(jnp.concatenate([low, high], axis=1))
-        first_ref[j, 0:128, :] = jnp.concatenate(tiles[:4], axis=0).astype(BF)
-        rest_ref[j // 2, j % 2, 128:256, :] = jnp.concatenate(tiles[4:], axis=0).astype(BF)
-        first_ref[j, 128:160, :] = site_t[:, 0:128]
-        first_ref[j, 160:192, :] = site_t[:, 128:256]
-    outs = [
-        pltpu.make_async_copy(first_ref, first_hbm, sems.at[3]),
-    ]
-    core = lax.axis_index("inner") % 2
-    outs.append(pltpu.make_async_copy(rest_ref.at[:, core], keep_hbm, sems.at[4]))
-    outs.append(pltpu.make_async_copy(rest_ref.at[:, 1 - core], give_hbm, sems.at[5]))
-    outs[0].start()
-    copies[1].wait()
     stacked = jnp.concatenate(
         [proj_ref[m, 0, :, n * 1024 : (n + 1) * 1024] for m in range(2) for n in range(2)], axis=0
     )
@@ -92,13 +82,17 @@
         dot_nt(shuffle, stacked[:, n * 512 : (n + 1) * 512]).reshape(W, 8, 256) for n in range(2)
     ]
     rows = jnp.concatenate(halves, axis=1).reshape(1024, 256).astype(BF)
-    for j in range(INNER):
-        rest_ref[j // 2, j % 2, 0:128, :] = rows[j * 128 : (j + 1) * 128, 0:128]
-        rest_ref[j // 2, j % 2, 256:384, :] = rows[j * 128 : (j + 1) * 128, 128:256]
-    for copy in outs[1:]:
-        copy.start()
-    for copy in outs:
-        copy.wait()
+    for chip in range(4):
+        both = []
+        for j in (chip * 2, chip * 2 + 1):
+            part = rows[j * 128 : (j + 1) * 128]
+            both.append(
+                jnp.concatenate([part[:, 0:128], lane_tiles(blocks, j), part[:, 128:256]], axis=0)
+            )
+        keep_ref[chip] = jnp.where(core == 0, both[0], both[1])
+        give = jnp.where(core == 0, both[1], both[0])
+        give_ref[chip] = give[0:192]
+        give_rest_ref[chip] = give[192:384]
 
 
 def tables(corner_ref, joining_ref, lengths_ref, kron_ref, info_ref):
@@ -166,7 +160,7 @@
     return jnp.concatenate(halves, axis=1)
 
 
-def first_rows(kron_ref, first_ref, keep_ref, took_ref, out_ref, *step_refs):
+def first_rows(kron_ref, first_ref, keep_ref, took_ref, took_rest_ref, out_ref, *step_refs):
     edges = gather_edges(lambda i, a, n: first_ref[i, a : a + n, :])
     rows = expand(kron_ref[...], edges, gather_site(first_ref))
     for t in range(SECTORS):
@@ -174,9 +168,11 @@
     chip = lax.axis_index("inner") // 2
     for step in range(4):
         to = (chip + step) % 4
-        for plane, ref in enumerate((keep_ref, took_ref)):
-            step_refs[step][plane] = ref[to, 0:128, :]
-            step_refs[4 + step][plane] = ref[to, 128:384, :]
+        step_refs[step][0] = keep_ref[to, 0:128, :]
+        step_refs[4 + step][0] = keep_ref[to, 128:384, :]
+        both = [took_ref[to], took_rest_ref[to]]
+        step_refs[step][1] = both[0][0:128, :]
+        step_refs[4 + step][1] = jnp.concatenate([both[0][128:], both[1]], axis=0)
 
 
 def arrival_rows(joining_ref, move, sector):
@@ -295,26 +291,30 @@
 
 
 def body(corner, edge_tensor, site_tensor, projector, lengths, joining):
-    first, keep, give = call(
-        prep,
-        (shape((INNER, 192, 128), BF),) + (shape((4, 384, 128), BF),) * 2,
+    first = call(
+        prep_first,
+        shape((INNER, 192, 128), BF),
         edge_tensor,
         jnp.swapaxes(site_tensor, 1, 2),
-        projector,
-        specs=[hbm(), hbm(), hbm()],
-        out_specs=(hbm(),) * 3,
+        specs=[hbm(), hbm()],
+        out_specs=hbm(),
         scratch=[
-            pltpu.VMEM((2, 1, 32, 4096), BF),
-            pltpu.VMEM((1, 32, KQ), BF),
-            pltpu.VMEM((2, 1, W, 2048), BF),
+            pltpu.VMEM((32, 4096), BF),
+            pltpu.VMEM((32, KQ), BF),
             pltpu.VMEM((INNER, 192, 128), BF),
-            pltpu.VMEM((4, 2, 384, 128), BF),
-            pltpu.SemaphoreType.DMA((6,)),
+            pltpu.SemaphoreType.DMA((3,)),
         ],
         room=60,
-        name="prep",
+        name="prep_first",
     )
     first = swap(first, "inner")
+    keep, *give = call(
+        prep_rest,
+        (shape((4, 384, 128), BF),) + (shape((4, 192, 128), BF),) * 2,
+        edge_tensor,
+        projector,
+        name="prep_rest",
+    )
     kron, info = call(
         tables,
         (shape((512, 512), BF), shape((8, 512), jnp.int32)),
@@ -324,7 +324,7 @@
         specs=[vmem(), vmem(), smem()],
         name="tables",
     )
-    took = lax.ppermute(give, "inner", [(i, i ^ 1) for i in range(INNER)])
+    took = [lax.ppermute(x, "inner", [(i, i ^ 1) for i in range(INNER)]) for x in give]
     rows_shape = shape((SECTORS, 16, KQ), BF)
     corner_shape = shape((1, W, W), BF)
     rows, *steps = call(
@@ -333,7 +333,7 @@
         kron,
         first,
         keep,
-        took,
+        *took,
         name="first_rows",
     )
     rows = swap(rows, "sector")

time: 83.2 us -> 82.1 us (0.987)
  waiting for transfers between devices: 14.6 us -> 13.2 us
    all_to_all x3, starting transfers between devices: 20.9 us -> 24 us  [swap(): return lax.all_to_all(x, axis, split_axis=0, concat_axis=0, tiled=True)]
    ppermute x1 -> x2, starting transfers between devices: 3.33 us -> 0.6 us  [body(): lax.ppermute(x, 'inner', [(i, i ^ 1) for i in range(INNER)])]
    all_to_all x3, waiting for transfers between devices: 14.5 us -> 13.2 us  [swap(): return lax.all_to_all(x, axis, split_axis=0, concat_axis=0, tiled=True)]
    pallas_call x7 -> x8, Pallas kernels: 8.34 us -> 8.19 us  [call(): pl.pallas_call(kernel, out_shape=outs, in_specs=specs or [vmem()] * len(a...]
  transfers between devices with their start and end apart: 10 -> 11, of which waited for: 3 -> 3; matrix products, arithmetic and copies ran while one was open for 0% -> 0% of each run, Pallas kernels for 2% -> 3%
where the time goes in v7:
time: 82.1 us; the launch traced here: 81.7 us
  starting transfers between devices  31.8 us (39%)
  blocking collectives  27 us (33%)
  waiting for transfers between devices  13.2 us (16%)
  Pallas kernels  8.19 us (10%)
  between operations  1.41 us (2%)
    all_to_all x2, blocking collectives, swap(): return lax.all_to_all(x, axis, split_axis=0, concat_axis=0, tiled=True)  27 us
    all_to_all x3, starting transfers between devices, swap(): return lax.all_to_all(x, axis, split_axis=0, concat_axis=0, tiled=True)  24 us
    all_to_all x3, waiting for transfers between devices, swap(): return lax.all_to_all(x, axis, split_axis=0, concat_axis=0, tiled=True)  13.2 us
    pallas_call x8, Pallas kernels, call(): pl.pallas_call(kernel, out_shape=outs, in_specs=specs or [vmem()] * len(a...  8.19 us
    ppermute x6, starting transfers between devices, body(): steps[step] = lax.ppermute(steps[step], 'inner', pairs)  7.19 us
  transfers between devices with their start and end apart: 11, of which 3 were waited for; matrix products, arithmetic and copies ran while one was open for 0% of the time, Pallas kernels for 3%

profile of v7, /device:TPU:1, one launch (start us, length us, event | category | flops | bytes accessed | tf_op | source)
XLA Modules:
  0.0 81.7 jit_solution(4020201680395614297)
XLA Ops:
  0.6 2.2 %prep_first.1 = bf16[8,192,128]{2,1,0:T(8,128)(2,1)} custom-call(bf16[2,1,32,4096]{3,2,1,0:T(8,128)(2,1)} %edge_ref.1, bf16[1,32,256]{2,1,0:T(8,128)(2,1)} %bitcast.1), custom_call_target="tpu_custom_call" | custom-call | tf_op jit(solution)/shard_map/prep_first/pallas_call | solution.py:274
  2.9 0.0 copy-start
  2.9 6.7 %all-to-all-start = ((bf16[8,192,128]{2,1,0:T(8,128)(2,1)}), bf16[8,192,128]{2,1,0:T(8,128)(2,1)S(1)}, u32[]{:S(2)}, u32[]{:S(2)}) async-start(bf16[8,192,128]{2,1,0:T(8,128)(2,1)} %prep_first.1), calls=%async_computation | async-start | bytes 786432 | tf_op jit(solution)/shard_map/all_to_all | solution.py:290
  9.6 0.0 copy-start.2
  9.6 0.0 copy-start.3
  9.6 0.7 prep_rest.1
  10.3 0.2 collective-permute-start
  10.5 0.4 collective-permute-start.1
  11.6 0.6 tables.1
  12.2 0.0 collective-permute-done.took_ref
  12.2 0.0 collective-permute-done.1.took_rest_ref
  12.3 5.4 %all-to-all-done.first_ref = bf16[8,192,128]{2,1,0:T(8,128)(2,1)S(1)} async-done(((bf16[8,192,128]{2,1,0:T(8,128)(2,1)}), bf16[8,192,128]{2,1,0:T(8,128)(2,1)S(1)}, u32[]{:S(2)}, u32[]{:S(2)}) %all-to-all-start) | async-done | bytes 393248 | tf_op jit(solution)/shard_map/all_to_all | solution.py:290
  17.7 1.2 %first_rows.1 = (bf16[32,16,256]{2,1,0:T(8,128)(2,1)}, bf16[2,128,128]{2,1,0:T(8,128)(2,1)S(1)}, bf16[2,128,128]{2,1,0:T(8,128)(2,1)S(1)}, bf16[2,128,128]{2,1,0...) custom-call(bf16[512,512]{1,0:T(8,128)(2,1)S(1)} %get-tuple-element., ...), custom_call_target="tpu_custom_call" | custom-call | tf_op jit(solution)/shard_map/first_rows/pallas_call | solution.py:274
  18.9 10.4 %all-to-all-start.1 = ((bf16[32,16,256]{2,1,0:T(8,128)(2,1)}), bf16[32,16,256]{2,1,0:T(8,128)(2,1)S(1)}, u32[]{:S(2)}, u32[]{:S(2)}) async-start(bf16[32,16,256]{2,1,0:T(8,128)(2,1)} %get-tuple-element.22), calls=%async_computation.1 | async-start | bytes 524288 | tf_op jit(solution)/shard_map/all_to_all | solution.py:290
  29.3 0.4 collective-permute-start.2
  29.7 1.8 %collective-permute-start.3 = (bf16[2,128,128]{2,1,0:T(8,128)(2,1)S(1)}, bf16[2,128,128]{2,1,0:T(8,128)(2,1)S(1)}, u32[]{:S(2)}, u32[]{:S(2)}) collective-permute-start(bf16[2,128,128]{2,1,0:T(8,128)(2,1)S(1)} %get-tuple-element.26), channel_id=1, source_target_pairs={{0,4},{1,5},{2,6},{3,7},{4,0},{5,1},{6,2},{7,3},{8,12},{9,13},{10,... | collective-permute-start | bytes 196616 | tf_op jit(solution)/shard_map/ppermute | solution.py:342
  31.5 0.7 collective-permute-start.4
  32.2 0.8 collective-permute-start.5
  32.9 1.5 %collective-permute-start.6 = (bf16[2,256,128]{2,1,0:T(8,128)(2,1)S(1)}, bf16[2,256,128]{2,1,0:T(8,128)(2,1)S(1)}, u32[]{:S(2)}, u32[]{:S(2)}) collective-permute-start(bf16[2,256,128]{2,1,0:T(8,128)(2,1)S(1)} %get-tuple-element.30), channel_id=1, source_target_pairs={{0,4},{1,5},{2,6},{3,7},{4,0},{5,1},{6,2},{7,3},{8,12},{9,13},{10,... | collective-permute-start | bytes 393224 | tf_op jit(solution)/shard_map/ppermute | solution.py:342
  34.4 0.0 collective-permute-done.2.refs_1_
  34.4 2.1 %collective-permute-start.7 = (bf16[2,256,128]{2,1,0:T(8,128)(2,1)S(1)}, bf16[2,256,128]{2,1,0:T(8,128)(2,1)S(1)}, u32[]{:S(2)}, u32[]{:S(2)}) collective-permute-start(bf16[2,256,128]{2,1,0:T(8,128)(2,1)S(1)} %get-tuple-element.31), channel_id=1, source_target_pairs={{0,6},{1,7},{2,0},{3,1},{4,2},{5,3},{6,4},{7,5},{8,14},{9,15},{10,... | collective-permute-start | bytes 393224 | tf_op jit(solution)/shard_map/ppermute | solution.py:342
  36.5 0.0 collective-permute-done.3.refs_2_
  36.5 2.5 %all-to-all-done.1.incoming_ref = bf16[32,16,256]{2,1,0:T(8,128)(2,1)S(1)} async-done(((bf16[32,16,256]{2,1,0:T(8,128)(2,1)}), bf16[32,16,256]{2,1,0:T(8,128)(2,1)S(1)}, u32[]{:S(2)}, u32[]{:S(2)}) %all-to-all-start.1) | async-done | bytes 262176 | tf_op jit(solution)/shard_map/all_to_all | solution.py:290
  39.0 1.3 %project_first.1 = f32[8,32,128]{2,1,0:T(8,128)} custom-call(bf16[32,16,256]{2,1,0:T(8,128)(2,1)S(1)} %all-to-all-done.1.incoming_ref, s32[8,512]{1,0:T(8,128)S(1)} %get-tuple-element.23.info_ref, bf16[2,128,128]{2,1,0:T(8,128)(2,1)S(1)} %get-tuple-element.24.refs_0_, bf16[2,128,128]{2,1,0:T(8,128)(2,1)S(1)} %collective-permute-done.2.refs_1_, ...), custom_call_target="tpu_custom_call" | custom-call | tf_op jit(solution)/shard_map/project_first/pallas_call | solution.py:274
  40.3 6.9 %all-to-all-start.2 = ((f32[8,32,128]{2,1,0:T(8,128)}), f32[8,32,128]{2,1,0:T(8,128)S(1)}, u32[]{:S(2)}, u32[]{:S(2)}) async-start(f32[8,32,128]{2,1,0:T(8,128)} %project_first.1), calls=%async_computation.2 | async-start | bytes 262144 | tf_op jit(solution)/shard_map/all_to_all | solution.py:290
  47.2 0.0 collective-permute-done.6.refs_2_
  47.2 5.3 %all-to-all-done.2.terms_ref = f32[8,32,128]{2,1,0:T(8,128)S(1)} async-done(((f32[8,32,128]{2,1,0:T(8,128)}), f32[8,32,128]{2,1,0:T(8,128)S(1)}, u32[]{:S(2)}, u32[]{:S(2)}) %all-to-all-start.2) | async-done | bytes 131104 | tf_op jit(solution)/shard_map/all_to_all | solution.py:290
  52.5 0.8 %second_rows.1 = (bf16[1,64,64]{2,1,0:T(8,128)(2,1)}, bf16[32,16,256]{2,1,0:T(8,128)(2,1)S(1)}) custom-call(f32[8,32,128]{2,1,0:T(8,128)S(1)} %all-to-all-done.2.terms_ref, s32[8,512]{1,0:T(8,128)S(1)} %get-tuple-element.23.info_ref, bf16[8,192,128]{2,1,0:T(8,128)(2,1)S(1)} %all-to-all-done.first_ref, bf16[2,256,128]{2,1,0:T(8,128)(2,1)S(1)} %get-tuple-element.28.refs_0_, ...), custom_call_target="tpu_custom_call" | custom-call | tf_op jit(solution)/shard_map/second_rows/pallas_call | solution.py:274
  53.3 15.7 %all_to_all.25.incoming_ref = bf16[32,16,256]{2,1,0:T(8,128)(2,1)S(1)} all-to-all(bf16[32,16,256]{2,1,0:T(8,128)(2,1)S(1)} %get-tuple-element.33), channel_id=1, replica_groups=mesh['sector'=32,'inner'=8] {'sector'}, dimensions={0} | all-to-all | bytes 524288 | tf_op jit(solution)/shard_map/all_to_all | solution.py:290
  69.1 0.6 project_second.1
  69.7 11.3 %all_to_all.26.terms_ref = f32[8,32,128]{2,1,0:T(8,128)S(1)} all-to-all(f32[8,32,128]{2,1,0:T(8,128)S(1)} %project_second.1), channel_id=1, replica_groups=mesh['sector'=32,'inner'=8] {'inner'}, dimensions={0} | all-to-all | bytes 262144 | tf_op jit(solution)/shard_map/all_to_all | solution.py:290
  81.0 0.7 last.1
  (8 shorter events, 0.0 us)
Async XLA Ops:
  0.6 9.0 %copy-start.1 = (bf16[2,1,64,2048]{3,2,1,0:T(8,128)(2,1)S(1)}, bf16[2,1,64,2048]{3,2,1,0:T(8,128)(2,1)}, u32[]{:S(2)}) copy-start(bf16[2,1,64,2048]{3,2,1,0:T(8,128)(2,1)} %proj_ref.1) | copy-start | bytes 1572868
  2.9 6.8 %copy-start = (bf16[2,1,32,4096]{3,2,1,0:T(8,128)(2,1)S(1)}, bf16[2,1,32,4096]{3,2,1,0:T(8,128)(2,1)}, u32[]{:S(2)}) copy-start(bf16[2,1,32,4096]{3,2,1,0:T(8,128)(2,1)} %edge_ref.1) | copy-start | bytes 1572868
  2.9 14.8 %all-to-all-start = ((bf16[8,192,128]{2,1,0:T(8,128)(2,1)}), bf16[8,192,128]{2,1,0:T(8,128)(2,1)S(1)}, u32[]{:S(2)}, u32[]{:S(2)}) async-start(bf16[8,192,128]{2,1,0:T(8,128)(2,1)} %prep_first.1), calls=%async_computation | async-start | bytes 786432 | tf_op jit(solution)/shard_map/all_to_all | solution.py:290
  9.6 2.0 %copy-start.2 = (bf16[1,64,64]{2,1,0:T(8,128)(2,1)S(1)}, bf16[1,64,64]{2,1,0:T(8,128)(2,1)}, u32[]{:S(2)}) copy-start(bf16[1,64,64]{2,1,0:T(8,128)(2,1)} %corner_ref.1) | copy-start | bytes 24580
  9.6 2.0 %copy-start.3 = (s32[2,2048]{1,0:T(2,128)S(1)}, s32[2,2048]{1,0:T(2,128)}, u32[]{:S(2)}) copy-start(s32[2,2048]{1,0:T(2,128)} %joining_ref.1) | copy-start | bytes 49156
  10.3 1.9 %collective-permute-start = (bf16[4,192,128]{2,1,0:T(8,128)(2,1)S(1)}, bf16[4,192,128]{2,1,0:T(8,128)(2,1)S(1)}, u32[]{:S(2)}, u32[]{:S(2)}) collective-permute-start(bf16[4,192,128]{2,1,0:T(8,128)(2,1)S(1)} %get-tuple-element.20), channel_id=1, source_target_pairs={{0,1},{1,0},{2,3},{3,2},{4,5},{5,4},{6,7},{7,6},{8,9},{9,8},{10,11... | collective-permute-start | bytes 589832 | tf_op jit(solution)/shard_map/ppermute | solution.py:327
  10.5 1.7 %collective-permute-start.1 = (bf16[4,192,128]{2,1,0:T(8,128)(2,1)S(1)}, bf16[4,192,128]{2,1,0:T(8,128)(2,1)S(1)}, u32[]{:S(2)}, u32[]{:S(2)}) collective-permute-start(bf16[4,192,128]{2,1,0:T(8,128)(2,1)S(1)} %get-tuple-element.21), channel_id=1, source_target_pairs={{0,1},{1,0},{2,3},{3,2},{4,5},{5,4},{6,7},{7,6},{8,9},{9,8},{10,11... | collective-permute-start | bytes 589832 | tf_op jit(solution)/shard_map/ppermute | solution.py:327
  18.9 20.1 %all-to-all-start.1 = ((bf16[32,16,256]{2,1,0:T(8,128)(2,1)}), bf16[32,16,256]{2,1,0:T(8,128)(2,1)S(1)}, u32[]{:S(2)}, u32[]{:S(2)}) async-start(bf16[32,16,256]{2,1,0:T(8,128)(2,1)} %get-tuple-element.22), calls=%async_computation.1 | async-start | bytes 524288 | tf_op jit(solution)/shard_map/all_to_all | solution.py:290
  29.3 5.1 %collective-permute-start.2 = (bf16[2,128,128]{2,1,0:T(8,128)(2,1)S(1)}, bf16[2,128,128]{2,1,0:T(8,128)(2,1)S(1)}, u32[]{:S(2)}, u32[]{:S(2)}) collective-permute-start(bf16[2,128,128]{2,1,0:T(8,128)(2,1)S(1)} %get-tuple-element.25), channel_id=1, source_target_pairs={{0,2},{1,3},{2,4},{3,5},{4,6},{5,7},{6,0},{7,1},{8,10},{9,11},{10,... | collective-permute-start | bytes 196616 | tf_op jit(solution)/shard_map/ppermute | solution.py:342
  29.7 6.8 %collective-permute-start.3 = (bf16[2,128,128]{2,1,0:T(8,128)(2,1)S(1)}, bf16[2,128,128]{2,1,0:T(8,128)(2,1)S(1)}, u32[]{:S(2)}, u32[]{:S(2)}) collective-permute-start(bf16[2,128,128]{2,1,0:T(8,128)(2,1)S(1)} %get-tuple-element.26), channel_id=1, source_target_pairs={{0,4},{1,5},{2,6},{3,7},{4,0},{5,1},{6,2},{7,3},{8,12},{9,13},{10,... | collective-permute-start | bytes 196616 | tf_op jit(solution)/shard_map/ppermute | solution.py:342
  31.5 5.1 %collective-permute-start.4 = (bf16[2,128,128]{2,1,0:T(8,128)(2,1)S(1)}, bf16[2,128,128]{2,1,0:T(8,128)(2,1)S(1)}, u32[]{:S(2)}, u32[]{:S(2)}) collective-permute-start(bf16[2,128,128]{2,1,0:T(8,128)(2,1)S(1)} %get-tuple-element.27), channel_id=1, source_target_pairs={{0,6},{1,7},{2,0},{3,1},{4,2},{5,3},{6,4},{7,5},{8,14},{9,15},{10,... | collective-permute-start | bytes 196616 | tf_op jit(solution)/shard_map/ppermute | solution.py:342
  32.2 15.0 %collective-permute-start.5 = (bf16[2,256,128]{2,1,0:T(8,128)(2,1)S(1)}, bf16[2,256,128]{2,1,0:T(8,128)(2,1)S(1)}, u32[]{:S(2)}, u32[]{:S(2)}) collective-permute-start(bf16[2,256,128]{2,1,0:T(8,128)(2,1)S(1)} %get-tuple-element.29), channel_id=1, source_target_pairs={{0,2},{1,3},{2,4},{3,5},{4,6},{5,7},{6,0},{7,1},{8,10},{9,11},{10,... | collective-permute-start | bytes 393224 | tf_op jit(solution)/shard_map/ppermute | solution.py:342
  32.9 14.3 %collective-permute-start.6 = (bf16[2,256,128]{2,1,0:T(8,128)(2,1)S(1)}, bf16[2,256,128]{2,1,0:T(8,128)(2,1)S(1)}, u32[]{:S(2)}, u32[]{:S(2)}) collective-permute-start(bf16[2,256,128]{2,1,0:T(8,128)(2,1)S(1)} %get-tuple-element.30), channel_id=1, source_target_pairs={{0,4},{1,5},{2,6},{3,7},{4,0},{5,1},{6,2},{7,3},{8,12},{9,13},{10,... | collective-permute-start | bytes 393224 | tf_op jit(solution)/shard_map/ppermute | solution.py:342
  34.4 12.8 %collective-permute-start.7 = (bf16[2,256,128]{2,1,0:T(8,128)(2,1)S(1)}, bf16[2,256,128]{2,1,0:T(8,128)(2,1)S(1)}, u32[]{:S(2)}, u32[]{:S(2)}) collective-permute-start(bf16[2,256,128]{2,1,0:T(8,128)(2,1)S(1)} %get-tuple-element.31), channel_id=1, source_target_pairs={{0,6},{1,7},{2,0},{3,1},{4,2},{5,3},{6,4},{7,5},{8,14},{9,15},{10,... | collective-permute-start | bytes 393224 | tf_op jit(solution)/shard_map/ppermute | solution.py:342
  40.3 12.2 %all-to-all-start.2 = ((f32[8,32,128]{2,1,0:T(8,128)}), f32[8,32,128]{2,1,0:T(8,128)S(1)}, u32[]{:S(2)}, u32[]{:S(2)}) async-start(f32[8,32,128]{2,1,0:T(8,128)} %project_first.1), calls=%async_computation.2 | async-start | bytes 262144 | tf_op jit(solution)/shard_map/all_to_all | solution.py:290

commit v8 on v7

--- a/solution.py
+++ b/solution.py
@@ -230,7 +230,7 @@
     term = both[:W, :W] + both[W:, W:]
     packed = jnp.concatenate([term[:32], term[32:]], axis=1)
     for j in range(INNER):
-        out_ref[j] = packed
+        out_ref[j] = packed.astype(out_ref.dtype)
 
 
 def finished(terms, info_ref):
@@ -255,7 +255,7 @@
 
 
 def last(terms_ref, info_ref, corner_ref):
-    corner_ref[0] = finished([terms_ref[j] for j in range(INNER)], info_ref)
+    corner_ref[0] = finished([terms_ref[j].astype(F32) for j in range(INNER)], info_ref)
 
 
 def vmem():
@@ -365,7 +365,7 @@
     rows = swap(rows, "sector")
     terms = call(
         functools.partial(project, 1),
-        terms_shape,
+        shape((INNER, 32, 128), BF),
         rows,
         info,
         *steps[4:],

time: 82.1 us -> 81.7 us (level)
  no operation moved by 1% of the time
where the time goes in v8:
time: 81.7 us; the launch traced here: 81.2 us
  starting transfers between devices  31.8 us (39%)
  blocking collectives  26.6 us (33%)
  waiting for transfers between devices  13.2 us (16%)
  Pallas kernels  8.2 us (10%)
  between operations  1.41 us (2%)
    all_to_all x2, blocking collectives, swap(): return lax.all_to_all(x, axis, split_axis=0, concat_axis=0, tiled=True)  26.6 us
    all_to_all x3, starting transfers between devices, swap(): return lax.all_to_all(x, axis, split_axis=0, concat_axis=0, tiled=True)  24 us
    all_to_all x3, waiting for transfers between devices, swap(): return lax.all_to_all(x, axis, split_axis=0, concat_axis=0, tiled=True)  13.2 us
    pallas_call x8, Pallas kernels, call(): pl.pallas_call(kernel, out_shape=outs, in_specs=specs or [vmem()] * len(a...  8.2 us
    ppermute x6, starting transfers between devices, body(): steps[step] = lax.ppermute(steps[step], 'inner', pairs)  7.19 us
  transfers between devices with their start and end apart: 11, of which 3 were waited for; matrix products, arithmetic and copies ran while one was open for 0% of the time, Pallas kernels for 3%

profile of v8, /device:TPU:1, one launch (start us, length us, event | category | flops | bytes accessed | tf_op | source)
XLA Modules:
  0.0 81.2 jit_solution(4527828688478580806)
XLA Ops:
  0.6 2.2 %prep_first.1 = bf16[8,192,128]{2,1,0:T(8,128)(2,1)} custom-call(bf16[2,1,32,4096]{3,2,1,0:T(8,128)(2,1)} %edge_ref.1, bf16[1,32,256]{2,1,0:T(8,128)(2,1)} %bitcast.1), custom_call_target="tpu_custom_call" | custom-call | tf_op jit(solution)/shard_map/prep_first/pallas_call | solution.py:274
  2.9 0.0 copy-start
  2.9 6.7 %all-to-all-start = ((bf16[8,192,128]{2,1,0:T(8,128)(2,1)}), bf16[8,192,128]{2,1,0:T(8,128)(2,1)S(1)}, u32[]{:S(2)}, u32[]{:S(2)}) async-start(bf16[8,192,128]{2,1,0:T(8,128)(2,1)} %prep_first.1), calls=%async_computation | async-start | bytes 786432 | tf_op jit(solution)/shard_map/all_to_all | solution.py:290
  9.6 0.0 copy-start.2
  9.6 0.0 copy-start.3
  9.6 0.7 prep_rest.1
  10.3 0.2 collective-permute-start
  10.5 0.4 collective-permute-start.1
  11.6 0.6 tables.1
  12.2 0.0 collective-permute-done.1.took_rest_ref
  12.3 5.4 %all-to-all-done.first_ref = bf16[8,192,128]{2,1,0:T(8,128)(2,1)S(1)} async-done(((bf16[8,192,128]{2,1,0:T(8,128)(2,1)}), bf16[8,192,128]{2,1,0:T(8,128)(2,1)S(1)}, u32[]{:S(2)}, u32[]{:S(2)}) %all-to-all-start) | async-done | bytes 393248 | tf_op jit(solution)/shard_map/all_to_all | solution.py:290
  17.7 1.2 %first_rows.1 = (bf16[32,16,256]{2,1,0:T(8,128)(2,1)}, bf16[2,128,128]{2,1,0:T(8,128)(2,1)S(1)}, bf16[2,128,128]{2,1,0:T(8,128)(2,1)S(1)}, bf16[2,128,128]{2,1,0...) custom-call(bf16[512,512]{1,0:T(8,128)(2,1)S(1)} %get-tuple-element., ...), custom_call_target="tpu_custom_call" | custom-call | tf_op jit(solution)/shard_map/first_rows/pallas_call | solution.py:274
  18.9 10.4 %all-to-all-start.1 = ((bf16[32,16,256]{2,1,0:T(8,128)(2,1)}), bf16[32,16,256]{2,1,0:T(8,128)(2,1)S(1)}, u32[]{:S(2)}, u32[]{:S(2)}) async-start(bf16[32,16,256]{2,1,0:T(8,128)(2,1)} %get-tuple-element.22), calls=%async_computation.1 | async-start | bytes 524288 | tf_op jit(solution)/shard_map/all_to_all | solution.py:290
  29.3 0.4 collective-permute-start.2
  29.7 1.8 %collective-permute-start.3 = (bf16[2,128,128]{2,1,0:T(8,128)(2,1)S(1)}, bf16[2,128,128]{2,1,0:T(8,128)(2,1)S(1)}, u32[]{:S(2)}, u32[]{:S(2)}) collective-permute-start(bf16[2,128,128]{2,1,0:T(8,128)(2,1)S(1)} %get-tuple-element.26), channel_id=1, source_target_pairs={{0,4},{1,5},{2,6},{3,7},{4,0},{5,1},{6,2},{7,3},{8,12},{9,13},{10,... | collective-permute-start | bytes 196616 | tf_op jit(solution)/shard_map/ppermute | solution.py:342
  31.5 0.7 collective-permute-start.4
  32.2 0.8 collective-permute-start.5
  32.9 1.5 %collective-permute-start.6 = (bf16[2,256,128]{2,1,0:T(8,128)(2,1)S(1)}, bf16[2,256,128]{2,1,0:T(8,128)(2,1)S(1)}, u32[]{:S(2)}, u32[]{:S(2)}) collective-permute-start(bf16[2,256,128]{2,1,0:T(8,128)(2,1)S(1)} %get-tuple-element.30), channel_id=1, source_target_pairs={{0,4},{1,5},{2,6},{3,7},{4,0},{5,1},{6,2},{7,3},{8,12},{9,13},{10,... | collective-permute-start | bytes 393224 | tf_op jit(solution)/shard_map/ppermute | solution.py:342
  34.4 0.0 collective-permute-done.2.refs_1_
  34.4 2.1 %collective-permute-start.7 = (bf16[2,256,128]{2,1,0:T(8,128)(2,1)S(1)}, bf16[2,256,128]{2,1,0:T(8,128)(2,1)S(1)}, u32[]{:S(2)}, u32[]{:S(2)}) collective-permute-start(bf16[2,256,128]{2,1,0:T(8,128)(2,1)S(1)} %get-tuple-element.31), channel_id=1, source_target_pairs={{0,6},{1,7},{2,0},{3,1},{4,2},{5,3},{6,4},{7,5},{8,14},{9,15},{10,... | collective-permute-start | bytes 393224 | tf_op jit(solution)/shard_map/ppermute | solution.py:342
  36.5 0.0 collective-permute-done.3.refs_2_
  36.5 0.0 collective-permute-done.4.refs_3_
  36.5 2.5 %all-to-all-done.1.incoming_ref = bf16[32,16,256]{2,1,0:T(8,128)(2,1)S(1)} async-done(((bf16[32,16,256]{2,1,0:T(8,128)(2,1)}), bf16[32,16,256]{2,1,0:T(8,128)(2,1)S(1)}, u32[]{:S(2)}, u32[]{:S(2)}) %all-to-all-start.1) | async-done | bytes 262176 | tf_op jit(solution)/shard_map/all_to_all | solution.py:290
  39.0 1.3 %project_first.1 = f32[8,32,128]{2,1,0:T(8,128)} custom-call(bf16[32,16,256]{2,1,0:T(8,128)(2,1)S(1)} %all-to-all-done.1.incoming_ref, s32[8,512]{1,0:T(8,128)S(1)} %get-tuple-element.23.info_ref, bf16[2,128,128]{2,1,0:T(8,128)(2,1)S(1)} %get-tuple-element.24.refs_0_, bf16[2,128,128]{2,1,0:T(8,128)(2,1)S(1)} %collective-permute-done.2.refs_1_, ...), custom_call_target="tpu_custom_call" | custom-call | tf_op jit(solution)/shard_map/project_first/pallas_call | solution.py:274
  40.3 6.9 %all-to-all-start.2 = ((f32[8,32,128]{2,1,0:T(8,128)}), f32[8,32,128]{2,1,0:T(8,128)S(1)}, u32[]{:S(2)}, u32[]{:S(2)}) async-start(f32[8,32,128]{2,1,0:T(8,128)} %project_first.1), calls=%async_computation.2 | async-start | bytes 262144 | tf_op jit(solution)/shard_map/all_to_all | solution.py:290
  47.2 0.0 collective-permute-done.7.refs_3_
  47.2 5.3 %all-to-all-done.2.terms_ref = f32[8,32,128]{2,1,0:T(8,128)S(1)} async-done(((f32[8,32,128]{2,1,0:T(8,128)}), f32[8,32,128]{2,1,0:T(8,128)S(1)}, u32[]{:S(2)}, u32[]{:S(2)}) %all-to-all-start.2) | async-done | bytes 131104 | tf_op jit(solution)/shard_map/all_to_all | solution.py:290
  52.5 0.8 %second_rows.1 = (bf16[1,64,64]{2,1,0:T(8,128)(2,1)}, bf16[32,16,256]{2,1,0:T(8,128)(2,1)S(1)}) custom-call(f32[8,32,128]{2,1,0:T(8,128)S(1)} %all-to-all-done.2.terms_ref, s32[8,512]{1,0:T(8,128)S(1)} %get-tuple-element.23.info_ref, bf16[8,192,128]{2,1,0:T(8,128)(2,1)S(1)} %all-to-all-done.first_ref, bf16[2,256,128]{2,1,0:T(8,128)(2,1)S(1)} %get-tuple-element.28.refs_0_, ...), custom_call_target="tpu_custom_call" | custom-call | tf_op jit(solution)/shard_map/second_rows/pallas_call | solution.py:274
  53.3 15.7 %all_to_all.25.incoming_ref = bf16[32,16,256]{2,1,0:T(8,128)(2,1)S(1)} all-to-all(bf16[32,16,256]{2,1,0:T(8,128)(2,1)S(1)} %get-tuple-element.33), channel_id=1, replica_groups=mesh['sector'=32,'inner'=8] {'sector'}, dimensions={0} | all-to-all | bytes 524288 | tf_op jit(solution)/shard_map/all_to_all | solution.py:290
  69.1 0.6 project_second.1
  69.7 10.8 %all_to_all.26.terms_ref = bf16[8,32,128]{2,1,0:T(8,128)(2,1)S(1)} all-to-all(bf16[8,32,128]{2,1,0:T(8,128)(2,1)S(1)} %project_second.1), channel_id=1, replica_groups=mesh['sector'=32,'inner'=8] {'inner'}, dimensions={0} | all-to-all | bytes 131072 | tf_op jit(solution)/shard_map/all_to_all | solution.py:290
  80.5 0.7 last.1
  (8 shorter events, 0.0 us)
Async XLA Ops:
  0.6 9.0 %copy-start.1 = (bf16[2,1,64,2048]{3,2,1,0:T(8,128)(2,1)S(1)}, bf16[2,1,64,2048]{3,2,1,0:T(8,128)(2,1)}, u32[]{:S(2)}) copy-start(bf16[2,1,64,2048]{3,2,1,0:T(8,128)(2,1)} %proj_ref.1) | copy-start | bytes 1572868
  2.9 6.8 %copy-start = (bf16[2,1,32,4096]{3,2,1,0:T(8,128)(2,1)S(1)}, bf16[2,1,32,4096]{3,2,1,0:T(8,128)(2,1)}, u32[]{:S(2)}) copy-start(bf16[2,1,32,4096]{3,2,1,0:T(8,128)(2,1)} %edge_ref.1) | copy-start | bytes 1572868
  2.9 14.8 %all-to-all-start = ((bf16[8,192,128]{2,1,0:T(8,128)(2,1)}), bf16[8,192,128]{2,1,0:T(8,128)(2,1)S(1)}, u32[]{:S(2)}, u32[]{:S(2)}) async-start(bf16[8,192,128]{2,1,0:T(8,128)(2,1)} %prep_first.1), calls=%async_computation | async-start | bytes 786432 | tf_op jit(solution)/shard_map/all_to_all | solution.py:290
  9.6 2.0 %copy-start.2 = (bf16[1,64,64]{2,1,0:T(8,128)(2,1)S(1)}, bf16[1,64,64]{2,1,0:T(8,128)(2,1)}, u32[]{:S(2)}) copy-start(bf16[1,64,64]{2,1,0:T(8,128)(2,1)} %corner_ref.1) | copy-start | bytes 24580
  9.6 2.0 %copy-start.3 = (s32[2,2048]{1,0:T(2,128)S(1)}, s32[2,2048]{1,0:T(2,128)}, u32[]{:S(2)}) copy-start(s32[2,2048]{1,0:T(2,128)} %joining_ref.1) | copy-start | bytes 49156
  10.3 1.9 %collective-permute-start = (bf16[4,192,128]{2,1,0:T(8,128)(2,1)S(1)}, bf16[4,192,128]{2,1,0:T(8,128)(2,1)S(1)}, u32[]{:S(2)}, u32[]{:S(2)}) collective-permute-start(bf16[4,192,128]{2,1,0:T(8,128)(2,1)S(1)} %get-tuple-element.20), channel_id=1, source_target_pairs={{0,1},{1,0},{2,3},{3,2},{4,5},{5,4},{6,7},{7,6},{8,9},{9,8},{10,11... | collective-permute-start | bytes 589832 | tf_op jit(solution)/shard_map/ppermute | solution.py:327
  10.5 1.7 %collective-permute-start.1 = (bf16[4,192,128]{2,1,0:T(8,128)(2,1)S(1)}, bf16[4,192,128]{2,1,0:T(8,128)(2,1)S(1)}, u32[]{:S(2)}, u32[]{:S(2)}) collective-permute-start(bf16[4,192,128]{2,1,0:T(8,128)(2,1)S(1)} %get-tuple-element.21), channel_id=1, source_target_pairs={{0,1},{1,0},{2,3},{3,2},{4,5},{5,4},{6,7},{7,6},{8,9},{9,8},{10,11... | collective-permute-start | bytes 589832 | tf_op jit(solution)/shard_map/ppermute | solution.py:327
  18.9 20.1 %all-to-all-start.1 = ((bf16[32,16,256]{2,1,0:T(8,128)(2,1)}), bf16[32,16,256]{2,1,0:T(8,128)(2,1)S(1)}, u32[]{:S(2)}, u32[]{:S(2)}) async-start(bf16[32,16,256]{2,1,0:T(8,128)(2,1)} %get-tuple-element.22), calls=%async_computation.1 | async-start | bytes 524288 | tf_op jit(solution)/shard_map/all_to_all | solution.py:290
  29.3 5.1 %collective-permute-start.2 = (bf16[2,128,128]{2,1,0:T(8,128)(2,1)S(1)}, bf16[2,128,128]{2,1,0:T(8,128)(2,1)S(1)}, u32[]{:S(2)}, u32[]{:S(2)}) collective-permute-start(bf16[2,128,128]{2,1,0:T(8,128)(2,1)S(1)} %get-tuple-element.25), channel_id=1, source_target_pairs={{0,2},{1,3},{2,4},{3,5},{4,6},{5,7},{6,0},{7,1},{8,10},{9,11},{10,... | collective-permute-start | bytes 196616 | tf_op jit(solution)/shard_map/ppermute | solution.py:342
  29.7 6.8 %collective-permute-start.3 = (bf16[2,128,128]{2,1,0:T(8,128)(2,1)S(1)}, bf16[2,128,128]{2,1,0:T(8,128)(2,1)S(1)}, u32[]{:S(2)}, u32[]{:S(2)}) collective-permute-start(bf16[2,128,128]{2,1,0:T(8,128)(2,1)S(1)} %get-tuple-element.26), channel_id=1, source_target_pairs={{0,4},{1,5},{2,6},{3,7},{4,0},{5,1},{6,2},{7,3},{8,12},{9,13},{10,... | collective-permute-start | bytes 196616 | tf_op jit(solution)/shard_map/ppermute | solution.py:342
  31.5 5.1 %collective-permute-start.4 = (bf16[2,128,128]{2,1,0:T(8,128)(2,1)S(1)}, bf16[2,128,128]{2,1,0:T(8,128)(2,1)S(1)}, u32[]{:S(2)}, u32[]{:S(2)}) collective-permute-start(bf16[2,128,128]{2,1,0:T(8,128)(2,1)S(1)} %get-tuple-element.27), channel_id=1, source_target_pairs={{0,6},{1,7},{2,0},{3,1},{4,2},{5,3},{6,4},{7,5},{8,14},{9,15},{10,... | collective-permute-start | bytes 196616 | tf_op jit(solution)/shard_map/ppermute | solution.py:342
  32.2 15.0 %collective-permute-start.5 = (bf16[2,256,128]{2,1,0:T(8,128)(2,1)S(1)}, bf16[2,256,128]{2,1,0:T(8,128)(2,1)S(1)}, u32[]{:S(2)}, u32[]{:S(2)}) collective-permute-start(bf16[2,256,128]{2,1,0:T(8,128)(2,1)S(1)} %get-tuple-element.29), channel_id=1, source_target_pairs={{0,2},{1,3},{2,4},{3,5},{4,6},{5,7},{6,0},{7,1},{8,10},{9,11},{10,... | collective-permute-start | bytes 393224 | tf_op jit(solution)/shard_map/ppermute | solution.py:342
  32.9 14.3 %collective-permute-start.6 = (bf16[2,256,128]{2,1,0:T(8,128)(2,1)S(1)}, bf16[2,256,128]{2,1,0:T(8,128)(2,1)S(1)}, u32[]{:S(2)}, u32[]{:S(2)}) collective-permute-start(bf16[2,256,128]{2,1,0:T(8,128)(2,1)S(1)} %get-tuple-element.30), channel_id=1, source_target_pairs={{0,4},{1,5},{2,6},{3,7},{4,0},{5,1},{6,2},{7,3},{8,12},{9,13},{10,... | collective-permute-start | bytes 393224 | tf_op jit(solution)/shard_map/ppermute | solution.py:342
  34.4 12.8 %collective-permute-start.7 = (bf16[2,256,128]{2,1,0:T(8,128)(2,1)S(1)}, bf16[2,256,128]{2,1,0:T(8,128)(2,1)S(1)}, u32[]{:S(2)}, u32[]{:S(2)}) collective-permute-start(bf16[2,256,128]{2,1,0:T(8,128)(2,1)S(1)} %get-tuple-element.31), channel_id=1, source_target_pairs={{0,6},{1,7},{2,0},{3,1},{4,2},{5,3},{6,4},{7,5},{8,14},{9,15},{10,... | collective-permute-start | bytes 393224 | tf_op jit(solution)/shard_map/ppermute | solution.py:342
  40.3 12.2 %all-to-all-start.2 = ((f32[8,32,128]{2,1,0:T(8,128)}), f32[8,32,128]{2,1,0:T(8,128)S(1)}, u32[]{:S(2)}, u32[]{:S(2)}) async-start(f32[8,32,128]{2,1,0:T(8,128)} %project_first.1), calls=%async_computation.2 | async-start | bytes 262144 | tf_op jit(solution)/shard_map/all_to_all | solution.py:290
